TPU v7x, 256 devices: a whole 4x4x8 slice. The times are simulated.
256 devices in a mesh: seq: 32 (over y, z), grp: 8 (over x, core).
Axes of the slice: x: 4, y: 4, z: 8, core: 2. Of those that a mesh axis runs over, the one named last changes fastest.
Arguments:
- queries: bfloat16 [8, 128, 8192], P('grp', None, 'seq'), may hold values from -64 to 64
- kv_cache: bfloat16 [8, 32768, 1024], P('grp', 'seq'), may hold values from -40 to 40
- kv_scale: float32 [8, 256, 8], P('grp', 'seq'), may hold values from 0.5 to 2
- block_mask: int32 [8, 1, 256], P('grp'), may hold values from 0 to 1, as said below
- resid: bfloat16 [8, 128, 4096], P('grp', 'seq'), may hold values from -4 to 4
- w_out: bfloat16 [8192, 4096], P('seq'), may hold values from -0.0625 to 0.0625
- norm_gain: float32 [4096], replicated, may hold values from 0.5 to 1.5
- expert_ids: int32 [8, 128, 8], P('grp'), may hold values from 0 to 31, all different within a row; in each aligned block of 128 rows (0 to 127, 128 to 255, ..., all dimensions but the last counted through in order) at most 64 rows name the same one
- gate_weights: float32 [8, 128, 8], P('grp'), may hold values from 0.05 to 1
- w_gate: bfloat16 [8, 6144, 4096], P('grp', 'seq'), may hold values from -0.09375 to 0.09375
- w_up: bfloat16 [8, 6144, 4096], P('grp', 'seq'), may hold values from -0.09375 to 0.09375
- w_down: bfloat16 [8, 6144, 4096], P('grp', 'seq'), may hold values from -0.15625 to 0.15625
Outputs:
- out: bfloat16 [8, 128, 4096], P('grp', 'seq')
Inputs may be any that keep to these rules, and one draw needn't show every extreme that they name: `block_mask`: every block of window rows may read the first key block and its own. `expert_ids`: each token names 8 different experts; in every trajectory no expert is named by more than 64 tokens, a bound that some block reaches.
All inputs are finite; a program needn't handle non-finite values.
Results may differ from a plain program's by a relative error of at most 0.038.
Values may be sent and summed in bfloat16 or wider, within the bound.
No kernel may reach another device: no remote copies, remote signals or barrier semaphores. Data moves between devices by JAX's collectives and lax.ppermute only.
A program may use at most 128 MiB of HBM per device.

v0:
```python
import math

import jax
import jax.numpy as jnp
from jax import lax
from jax.sharding import PartitionSpec as P

HEADS = 64
KV_HEADS = 4
HEAD_DIM = 128
BLOCK = 128
E_SUB = 4
CAP = 64


masked_score = -1e30


def rms_norm(stream, gain):
    rows_wide = stream.astype(jnp.float32)
    factor = lax.rsqrt(jnp.mean(rows_wide * rows_wide, axis=-1, keepdims=True) + 1e-06)
    return (rows_wide * factor * gain).astype(jnp.bfloat16)


def per_device(
    queries,
    kv_cache,
    kv_scale,
    block_mask,
    resid,
    w_out,
    norm_gain,
    expert_ids,
    gate_weights,
    w_gate,
    w_up,
    w_down,
):
    seq_count = lax.axis_size("seq")
    seq_pos = lax.axis_index("seq")
    grp_count = lax.axis_size("grp")
    window = queries.shape[1]
    ctx_local = kv_cache.shape[1]
    total_ctx = ctx_local * seq_count
    head_dim = HEAD_DIM
    per_kv = HEADS // KV_HEADS
    heads_mine = queries.shape[2] // head_dim
    score_scale = 1.0 / math.sqrt(head_dim)
    spread = jnp.repeat(jnp.repeat(kv_scale[0], BLOCK, axis=0), head_dim, axis=1)
    keyvals = (kv_cache[0].astype(jnp.float32) * spread).astype(jnp.bfloat16)
    mask_cols = jnp.repeat(block_mask[0], BLOCK, axis=1) == 1
    query_pos = total_ctx - window + jnp.arange(window, dtype=jnp.int32)
    queries_all = lax.all_gather(queries[0], "seq", axis=1, tiled=True)
    local_cols = lax.dynamic_slice_in_dim(mask_cols, seq_pos * ctx_local, ctx_local, 1)
    key_pos = seq_pos * ctx_local + jnp.arange(ctx_local, dtype=jnp.int32)
    allowed = jnp.repeat(local_cols, BLOCK, axis=0) & (key_pos[None, :] <= query_pos[:, None])
    pieces = []
    maxima = []
    totals = []
    for kv_head in range(KV_HEADS):
        query_block = queries_all[
            :, kv_head * per_kv * head_dim : (kv_head + 1) * per_kv * head_dim
        ]
        query_block = query_block.reshape(window, per_kv, head_dim)
        key_block = keyvals[:, kv_head * head_dim : (kv_head + 1) * head_dim]
        value_block = keyvals[
            :, (KV_HEADS + kv_head) * head_dim : (KV_HEADS + kv_head + 1) * head_dim
        ]
        scores = (
            jnp.einsum("wgd,kd->gwk", query_block, key_block, preferred_element_type=jnp.float32)
            * score_scale
        )
        highest = jnp.max(jnp.where(allowed[None], scores, masked_score), axis=-1)
        weights = jnp.exp(jnp.where(allowed[None], scores - highest[:, :, None], -jnp.inf))
        summed = jnp.einsum(
            "gwk,kd->wgd",
            weights.astype(jnp.bfloat16),
            value_block,
            preferred_element_type=jnp.float32,
        )
        pieces.append(summed.reshape(window, per_kv * head_dim))
        maxima.append(jnp.transpose(highest))
        totals.append(jnp.transpose(jnp.sum(weights, axis=-1)))
    partial_value = jnp.concatenate(pieces, axis=1)
    peak_rows = jnp.concatenate(maxima, axis=1)
    total_rows = jnp.concatenate(totals, axis=1)
    got_parts, got_peaks, got_totals = (
        lax.all_to_all(
            partial_value[None].astype(jnp.bfloat16), "seq", split_axis=2, concat_axis=0, tiled=True
        ).astype(jnp.float32),
        lax.all_to_all(
            peak_rows[None].astype(jnp.bfloat16), "seq", split_axis=2, concat_axis=0, tiled=True
        ).astype(jnp.float32),
        lax.all_to_all(
            total_rows[None].astype(jnp.bfloat16), "seq", split_axis=2, concat_axis=0, tiled=True
        ).astype(jnp.float32),
    )
    highest_all = jnp.max(got_peaks, axis=0)
    factor = jnp.exp(got_peaks - highest_all[None])
    denominator = jnp.sum(got_totals * factor, axis=0)
    numerator = jnp.sum(
        got_parts.reshape(seq_count, window, heads_mine, head_dim) * factor[:, :, :, None], axis=0
    )
    attended = (
        (numerator / denominator[:, :, None])
        .reshape(window, heads_mine * head_dim)
        .astype(jnp.bfloat16)
    )
    projected = jnp.dot(attended, w_out, preferred_element_type=jnp.float32)
    rows_mine = resid.shape[1]
    first_row = seq_pos * rows_mine
    own_rows = lax.dynamic_slice_in_dim(projected, first_row, rows_mine, 0) + resid[0].astype(
        jnp.float32
    )
    projected = lax.dynamic_update_slice_in_dim(projected, own_rows, first_row, 0)
    stream = lax.psum_scatter(
        projected.astype(jnp.bfloat16), "seq", scatter_dimension=0, tiled=True
    )
    normed_mine = rms_norm(stream, norm_gain)
    normed_all = lax.all_gather(normed_mine, "seq", axis=0, tiled=True)
    slices = seq_count // E_SUB
    owners = jnp.arange(grp_count, dtype=jnp.int32) * E_SUB + seq_pos // slices
    matches = expert_ids[0][None, :, :] == owners[:, None, None]
    chosen = jnp.any(matches, axis=-1)
    weight = jnp.sum(jnp.where(matches, gate_weights[0][None, :, :], 0.0), axis=-1)
    slot_index = jnp.cumsum(chosen.astype(jnp.int32), axis=1) - 1
    slot_range = jnp.arange(CAP, dtype=jnp.int32)
    dispatch_table = (
        chosen[:, None, :] & (slot_index[:, None, :] == slot_range[None, :, None])
    ).astype(jnp.bfloat16)
    outgoing_rows = jnp.einsum(
        "gcw,wd->gcd", dispatch_table, normed_all, preferred_element_type=jnp.float32
    ).astype(jnp.bfloat16)
    arrivals = lax.all_to_all(outgoing_rows, "grp", split_axis=0, concat_axis=0, tiled=True)
    gate_part = jnp.einsum("scd,hd->sch", arrivals, w_gate[0], preferred_element_type=jnp.float32)
    up_part = jnp.einsum("scd,hd->sch", arrivals, w_up[0], preferred_element_type=jnp.float32)
    hidden = (jax.nn.silu(gate_part) * up_part).astype(jnp.bfloat16)
    computed = jnp.einsum(
        "sch,hd->scd", hidden, w_down[0], preferred_element_type=jnp.float32
    ).astype(jnp.bfloat16)
    returned = lax.all_to_all(computed, "grp", split_axis=0, concat_axis=0, tiled=True)
    picked = jnp.einsum(
        "gcw,gcd->gwd", dispatch_table, returned, preferred_element_type=jnp.float32
    )
    mixture = jnp.sum(picked * weight[:, :, None], axis=0)
    expert_rows = lax.psum_scatter(
        mixture.astype(jnp.bfloat16), "seq", scatter_dimension=0, tiled=True
    ).astype(jnp.float32)
    return (stream.astype(jnp.float32) + expert_rows).astype(jnp.bfloat16)[None]


def solution(mesh):
    in_specs = (
        P("grp", None, "seq"),
        P("grp", "seq", None),
        P("grp", "seq", None),
        P("grp", None, None),
        P("grp", "seq", None),
        P("seq", None),
        P(),
        P("grp", None, None),
        P("grp", None, None),
        P("grp", "seq", None),
        P("grp", "seq", None),
        P("grp", "seq", None),
    )
    out_specs = P("grp", "seq", None)
    return jax.shard_map(
        per_device, mesh=mesh, in_specs=in_specs, out_specs=out_specs, check_vma=False
    )
```

profile of v0, /device:TPU:2, one launch (start us, length us, event | category | flops | bytes accessed | tf_op | source)
XLA Modules:
  0.0 833.7 jit_solution(6360393241466895282)
XLA Ops:
  6.5 1.7 copy.78
  8.3 0.0 all-gather.5.cloned.1.call-update
  8.3 0.7 compare_reduce_fusion.1
  9.0 0.1 broadcast_bitcast_fusion
  9.1 0.1 copy.120
  9.3 1.0 compare_and_fusion
  10.3 0.7 broadcast_in_dim.96
  11.0 1.1 broadcast_in_dim.97
  12.2 2.5 fusion.20
  14.6 76.3 %all-gather.5.cloned.1.call-done = bf16[1,128,8192]{1,2,0:T(8,128)(2,1)} async-done(((bf16[1,128,256]{1,2,0:T(8,128)(2,1)}), bf16[1,128,8192]{1,2,0:T(8,128)(2,1)}) %all-gather.5.cloned.1.call-update) | async-done | bytes 2097168 | tf_op jit(solution)/shard_map/all_gather | solution.py:53
  90.9 2.6 fusion.95
  93.5 1.2 fusion.64
  94.7 1.2 fusion.65
  96.0 4.5 fusion.9
  100.5 10.3 %fusion.12 = (bf16[16,128]{1,0:T(8,128)(2,1)}, f32[16,128]{1,0:T(8,128)S(1)}, f32[16,128]{1,0:T(8,128)S(1)}, f32[16,128]{1,0:T(8,128)S(1)}, f32[1024,128,16]{1,0,2:T(8,128)}) fusion(f32[1024,128,16]{1,0,2:T(8,128)} %get-tuple-element.19, f32[16,128]{1,0:T(8,128)S(1)} %get-tuple-element.18, pred[128,1024]{0,1:T(8,128)(4,1)} %compare_and_fusion, ...), kind=kOutput, calls=%fused_computation.21 | convolution fusion | flops 564125696 | bytes 34508800 | tf_op jit(solution)/shard_map/wgd,kd->gwk/dot_general | solution.py:70
  110.8 9.9 %fusion.14 = (bf16[16,128]{1,0:T(8,128)(2,1)S(1)}, bf16[16,128]{1,0:T(8,128)(2,1)S(1)}, bf16[16,128]{1,0:T(8,128)(2,1)}) fusion(f32[1024,128,16]{1,0,2:T(8,128)} %get-tuple-element.20, f32[16,128]{1,0:T(8,128)S(1)} %get-tuple-element.6, pred[128,1024]{0,1:T(8,128)(4,1)} %compare_and_fusion, f32[16,128]{1,0:T(8,128)S(1)} %get-tuple-element.7, ...), kind=kLoop, calls=%fused_computation.23 | loop fusion | flops 25159680 | bytes 25333760 | tf_op jit(solution)/shard_map/reduce_sum | solution.py:83
  120.7 6.2 fusion.42
  127.0 2.9 fusion.45
  129.9 2.9 fusion.48
  132.9 2.9 fusion.39
  135.8 0.6 copy.124
  136.4 6.3 all-to-all-start.1
  142.7 0.6 copy.123
  143.3 1.8 copy.92
  145.1 2.6 copy.93
  147.7 2.6 copy.94
  150.3 8.9 %copy.91 = bf16[1,128,2048]{1,0,2:T(2,128)(2,1)} copy(bf16[1,128,2048]{1,2,0:T(8,128)(2,1)S(1)} %bitcast.249) | data formatting | bytes 1048576 | tf_op jit(solution)/shard_map/concatenate | solution.py:84
  159.2 10.1 %all-to-all-start.2 = ((bf16[32,2,128]{2,1,0:T(2,128)(2,1)}), bf16[32,2,128]{2,1,0:T(2,128)(2,1)S(1)}, u32[]{:S(2)}, u32[]{:S(2)}) async-start(bf16[32,2,128]{2,1,0:T(2,128)(2,1)} %bitcast.235), calls=%async_computation.2 | async-start | bytes 32768 | tf_op jit(solution)/shard_map/all_to_all | solution.py:94
  169.3 31.7 %fusion.96 = bf16[8192,1,128]{2,1,0:T(2,128)(2,1)} fusion(bf16[1,128,2048]{1,0,2:T(2,128)(2,1)} %copy.94, bf16[1,128,2048]{1,0,2:T(2,128)(2,1)} %copy.93, bf16[1,128,2048]{1,0,2:T(2,128)(2,1)S(1)} %copy.92, bf16[1,128,2048]{1,0,2:T(2,128)(2,1)} %copy.91), kind=kLoop, calls=%fused_computation.129 | loop fusion | flops 3145728 | bytes 4194304
  201.0 0.5 broadcast.153
  201.5 46.4 %reduce.7 = bf16[8192,128]{1,0:T(8,128)(2,1)} reduce(bf16[8192,1,128]{2,1,0:T(2,128)(2,1)} %fusion.96, bf16[]{:T(256)} %broadcast.153), dimensions={1}, to_apply=%fusion.96.reduce_sub_computation | reduce | bytes 4194306
  247.9 4.0 reshape.380
  251.9 10.0 %all-to-all-start = ((bf16[32,2,16384]{2,1,0:T(2,128)(2,1)}), bf16[32,2,16384]{2,1,0:T(2,128)(2,1)}, u32[]{:S(2)}, u32[]{:S(2)}) async-start(bf16[32,2,16384]{2,1,0:T(2,128)(2,1)} %reshape.380), calls=%async_computation | async-start | bytes 4194304 | tf_op jit(solution)/shard_map/all_to_all | solution.py:88
  261.9 0.0 all-reduce.5.cloned.1.call-start
  262.1 0.1 multiply_reduce_fusion.1
  262.2 45.1 %all-to-all-done = bf16[32,2,16384]{2,1,0:T(2,128)(2,1)} async-done(((bf16[32,2,16384]{2,1,0:T(2,128)(2,1)}), bf16[32,2,16384]{2,1,0:T(2,128)(2,1)}, u32[]{:S(2)}, u32[]{:S(2)}) %all-to-all-start) | async-done | bytes 2097184 | tf_op jit(solution)/shard_map/all_to_all | solution.py:88
  307.3 10.5 %reshape.381 = bf16[8192,1,128]{2,1,0:T(2,128)(2,1)} reshape(bf16[32,2,16384]{2,1,0:T(2,128)(2,1)} %all-to-all-done) | data formatting | bytes 4194304
  317.7 7.0 bitcast_convert_fusion
  324.8 0.5 fusion.21
  325.3 0.5 fusion.97
  325.9 1.1 convert_element_type.145
  327.0 0.0 all-reduce.5.cloned.1.call-update
  327.0 0.3 all-gather.7.cloned.1.call-start
  327.3 0.6 dynamic-slice
  328.5 145.1 %all-reduce.5.cloned.1.call-done = bf16[128,4096]{1,0:T(8,128)(2,1)} async-done(((bf16[128,4096]{1,0:T(8,128)(2,1)}), bf16[128,4096]{1,0:T(8,128)(2,1)}) %all-reduce.5.cloned.1.call-update) | async-done | bytes 1048592
  473.6 1.0 fusion.77
  474.6 1.5 fusion.84
  476.2 0.0 all-gather.7.cloned.1.call-update
  476.2 0.1 compare_reduce_fusion
  476.3 0.3 reduce_window_sum.11
  476.6 73.3 %all-gather.7.cloned.1.call-done = bf16[32,4,4096]{2,1,0:T(4,128)(2,1)} async-done(((bf16[1,4,4096]{2,1,0:T(4,128)(2,1)}), bf16[32,4,4096]{2,1,0:T(4,128)(2,1)}) %all-gather.7.cloned.1.call-update) | async-done | bytes 1048592 | tf_op jit(solution)/shard_map/all_gather | solution.py:120
  549.9 1.3 reshape.370
  551.2 1.2 convolution_convert_fusion.1
  552.5 53.6 %all_to_all.43 = bf16[8,64,4096]{2,1,0:T(8,128)(2,1)S(1)} all-to-all(bf16[8,64,4096]{2,1,0:T(8,128)(2,1)S(1)} %convolution_convert_fusion.1), channel_id=1, replica_groups=mesh['seq'=32,'grp'=8] {'grp'}, dimensions={0} | all-to-all | bytes 8388608 | tf_op jit(solution)/shard_map/all_to_all | solution.py:134
  606.1 1.9 copy-done.1
  608.0 1.3 fusion.37
  609.3 9.6 %convolution_convert_fusion = bf16[8,64,4096]{2,1,0:T(8,128)(2,1)} fusion(bf16[1,192,4096]{2,1,0:T(8,128)(2,1)} %param.23, bf16[8,64,4096]{2,1,0:T(8,128)(2,1)} %copy-done.1, bf16[1,192,4096]{2,1,0:T(8,128)(2,1)} %param.22, f32[8,64,192]{2,1,0:T(8,128)S(1)} %fusion.37), kind=kOutput, calls=%fused_computation.29 | convolution fusion | flops 1613299712 | bytes 11927552 | tf_op jit(solution)/shard_map/sch,hd->scd/dot_general | solution.py:138
  618.9 6.0 all-to-all-start.4
  624.9 0.1 fusion.82
  625.0 48.2 %all-to-all-done.4 = bf16[8,64,4096]{2,1,0:T(8,128)(2,1)} async-done(((bf16[8,64,4096]{2,1,0:T(8,128)(2,1)}), bf16[8,64,4096]{2,1,0:T(8,128)(2,1)}, u32[]{:S(2)}, u32[]{:S(2)}) %all-to-all-start.4) | async-done | bytes 4194336 | tf_op jit(solution)/shard_map/all_to_all | solution.py:141
  673.2 5.8 multiply_reduce_fusion
  679.1 0.0 all-reduce.7.cloned.1.call-update
  679.1 146.4 %all-reduce.7.cloned.1.call-done = bf16[128,4096]{1,0:T(8,128)(2,1)} async-done(((bf16[128,4096]{1,0:T(8,128)(2,1)}), bf16[128,4096]{1,0:T(8,128)(2,1)}) %all-reduce.7.cloned.1.call-update) | async-done | bytes 1048592
  825.4 1.5 fusion.83
  (59 shorter events, 0.4 us)
Async XLA Ops:
  6.5 318.8 %copy-start = (bf16[256,4096]{1,0:T(8,128)(2,1)S(1)}, bf16[256,4096]{1,0:T(8,128)(2,1)}, u32[]{:S(2)}) copy-start(bf16[256,4096]{1,0:T(8,128)(2,1)} %param.17) | copy-start | bytes 6291460
  6.5 84.3 %all-gather.5.cloned.1.call-start = ((), (), s32[]{:S(2)}) async-start(), calls=%async_computation.5 | async-start | bytes 2162688 | tf_op jit(solution)/shard_map/all_gather | solution.py:53
  9.2 2.9 copy-start.5
  90.9 2.6 copy-start.2
  94.7 1.3 copy-start.3
  110.8 9.9 %copy-start.4 = (pred[128,1024]{0,1:T(8,128)(4,1)S(1)}, pred[128,1024]{0,1:T(8,128)(4,1)}, u32[]{:S(2)}) copy-start(pred[128,1024]{0,1:T(8,128)(4,1)} %compare_and_fusion) | copy-start | bytes 393220
  127.0 5.9 slice-start
  129.9 2.9 slice-start.1
  132.8 9.8 %copy-start.10 = (bf16[16,128]{1,0:T(8,128)(2,1)S(1)}, bf16[16,128]{1,0:T(8,128)(2,1)}, u32[]{:S(2)}) copy-start(bf16[16,128]{1,0:T(8,128)(2,1)} %get-tuple-element.11) | copy-start | bytes 12292
  132.8 9.8 %copy-start.12 = (bf16[16,128]{1,0:T(8,128)(2,1)S(1)}, bf16[16,128]{1,0:T(8,128)(2,1)}, u32[]{:S(2)}) copy-start(bf16[16,128]{1,0:T(8,128)(2,1)} %get-tuple-element.5) | copy-start | bytes 12292
  136.4 22.9 %all-to-all-start.1 = ((bf16[32,2,128]{2,1,0:T(2,128)(2,1)}), bf16[32,2,128]{2,1,0:T(2,128)(2,1)S(1)}, u32[]{:S(2)}, u32[]{:S(2)}) async-start(bf16[32,2,128]{2,1,0:T(2,128)(2,1)} %bitcast.236), calls=%async_computation.1 | async-start | bytes 32768 | tf_op jit(solution)/shard_map/all_to_all | solution.py:91
  142.6 7.7 copy-start.6
  159.2 92.7 %all-to-all-start.2 = ((bf16[32,2,128]{2,1,0:T(2,128)(2,1)}), bf16[32,2,128]{2,1,0:T(2,128)(2,1)S(1)}, u32[]{:S(2)}, u32[]{:S(2)}) async-start(bf16[32,2,128]{2,1,0:T(2,128)(2,1)} %bitcast.235), calls=%async_computation.2 | async-start | bytes 32768 | tf_op jit(solution)/shard_map/all_to_all | solution.py:94
  251.9 55.4 %all-to-all-start = ((bf16[32,2,16384]{2,1,0:T(2,128)(2,1)}), bf16[32,2,16384]{2,1,0:T(2,128)(2,1)}, u32[]{:S(2)}, u32[]{:S(2)}) async-start(bf16[32,2,16384]{2,1,0:T(2,128)(2,1)} %reshape.380), calls=%async_computation | async-start | bytes 4194304 | tf_op jit(solution)/shard_map/all_to_all | solution.py:88
  261.9 211.7 %all-reduce.5.cloned.1.call-start = ((), (), s32[]{:S(2)}) async-start(), calls=%async_computation.7 | async-start | bytes 2097152
  324.7 1.1 copy-start.7
  325.3 2.0 copy-start.14
  325.3 149.3 %copy-start.9 = (f32[4096]{0:T(1024)S(1)}, f32[4096]{0:T(1024)}, u32[]{:S(2)}) copy-start(f32[4096]{0:T(1024)} %param.18) | copy-start | bytes 49156
  325.3 150.9 %copy-start.8 = (s32[1,128,8]{1,2,0:T(8,128)S(1)}, s32[1,128,8]{1,2,0:T(8,128)}, u32[]{:S(2)}) copy-start(s32[1,128,8]{1,2,0:T(8,128)} %param.19) | copy-start | bytes 12292
  327.0 222.8 %all-gather.7.cloned.1.call-start = ((), (), s32[]{:S(2)}) async-start(), calls=%async_computation.6 | async-start | bytes 1081344 | tf_op jit(solution)/shard_map/all_gather | solution.py:120
  552.5 55.6 %copy-start.13 = (bf16[1,192,4096]{2,1,0:T(8,128)(2,1)S(1)}, bf16[1,192,4096]{2,1,0:T(8,128)(2,1)}, u32[]{:S(2)}) copy-start(bf16[1,192,4096]{2,1,0:T(8,128)(2,1)} %param.21) | copy-start | bytes 4718596
  606.1 1.9 copy-start.1
  618.9 6.0 copy-start.11
  618.9 54.4 %all-to-all-start.4 = ((bf16[8,64,4096]{2,1,0:T(8,128)(2,1)}), bf16[8,64,4096]{2,1,0:T(8,128)(2,1)}, u32[]{:S(2)}, u32[]{:S(2)}) async-start(bf16[8,64,4096]{2,1,0:T(8,128)(2,1)} %convolution_convert_fusion), calls=%async_computation.4 | async-start | bytes 8388608 | tf_op jit(solution)/shard_map/all_to_all | solution.py:141
  624.9 200.6 %all-reduce.7.cloned.1.call-start = ((), (), s32[]{:S(2)}) async-start(), calls=%async_computation.8 | async-start | bytes 2097152
Sparse Core Ops, SparseCore 0:
  10.0 80.8 all-gather.4
  327.1 146.4 all-reduce.4
  476.3 73.5 all-gather.6
  679.2 146.1 all-reduce.6
where the time goes:
time: 840 us; the launch traced here: 834 us
  waiting for transfers between devices  534 us (64%)
  other arithmetic  106 us (13%)
  blocking collectives  53.6 us (6%)
  matrix products  50.7 us (6%)
  local copies, waits for them, and re-layouts  42.5 us (5%)
  starting transfers between devices  32.7 us (4%)
  between operations  14.4 us (2%)
    unnamed x6, waiting for transfers between devices  291 us
    unnamed x4, other arithmetic  79.7 us
    all_gather x1, waiting for transfers between devices, per_device(): queries_all = lax.all_gather(queries[0], 'seq', axis=1, tiled=True)  76.3 us
    all_gather x1, waiting for transfers between devices, per_device(): normed_all = lax.all_gather(normed_mine, 'seq', axis=0, tiled=True)  73.3 us
    all_to_all x1, blocking collectives, per_device(): lax.all_to_all(outgoing_rows, 'grp', split_axis=0, concat_axis=0, tiled=T...  53.6 us
    all_to_all x1, waiting for transfers between devices, per_device(): lax.all_to_all(computed, 'grp', split_axis=0, concat_axis=0, tiled=True)  48.2 us
    all_to_all x1, waiting for transfers between devices, per_device(): lax.all_to_all(partial_value[None].astype(jnp.bfloat16), 'seq', split_axi...  45.1 us
    unnamed x47, local copies, waits for them, and re-layouts  22 us
  transfers between devices with their start and end apart: 8, of which 6 were waited for; matrix products, arithmetic and copies ran while one was open for 13% of the time, Pallas kernels for 0%

commit v1 on v0

v1 whole, which is shorter than its diff:
```python
import math

import jax
import jax.numpy as jnp
from jax import lax
from jax.experimental import pallas as pl
from jax.experimental.pallas import tpu as pltpu
from jax.sharding import Mesh
from jax.sharding import PartitionSpec as P

HEADS = 64
KV_HEADS = 4
HEAD_DIM = 128
BLOCK = 128
E_SUB = 4
CAP = 64
N_Y, N_Z, N_X, N_C = 4, 8, 4, 2
N_GRP = N_X * N_C
WIN = 128
D = 4096
COLS = D // N_Z
CTX_LOCAL = 1024
HIDDEN = 192
STAT_ROWS = 16
MASKED = -1e30
SCALE2 = math.log2(math.e) / math.sqrt(HEAD_DIM)
VMEM = 56 * 1024 * 1024

f32 = jnp.float32
bf16 = jnp.bfloat16


def params():
    return pltpu.CompilerParams(vmem_limit_bytes=VMEM)


def attention_kernel(q_ref, kv_ref, bias_ref, causal_ref, out_ref, s_ref):
    q_pair = jnp.concatenate([q_ref[0, :, :HEAD_DIM], q_ref[0, :, HEAD_DIM:]], axis=0)
    peak = jnp.full((2 * WIN, BLOCK), -jnp.inf, f32)
    for src in range(N_Y):
        s = lax.dot_general(
            q_pair, kv_ref[src, 0], (((1,), (1,)), ((), ())), preferred_element_type=f32
        )
        s = s + bias_ref[src]
        if src == N_Y - 1:
            s = jnp.concatenate(
                [s[:, : CTX_LOCAL - BLOCK], s[:, CTX_LOCAL - BLOCK :] + causal_ref[...]], axis=1
            )
        s_ref[:, src * CTX_LOCAL : (src + 1) * CTX_LOCAL] = s
        for b in range(CTX_LOCAL // BLOCK):
            peak = jnp.maximum(peak, s[:, b * BLOCK : (b + 1) * BLOCK])
    m = jnp.max(peak, axis=1, keepdims=True)
    total = jnp.zeros((2 * WIN, BLOCK), f32)
    acc = jnp.zeros((2 * WIN, HEAD_DIM), f32)
    for src in range(N_Y):
        s = s_ref[:, src * CTX_LOCAL : (src + 1) * CTX_LOCAL]
        p = jnp.exp2((s - m) * SCALE2)
        for b in range(CTX_LOCAL // BLOCK):
            total = total + p[:, b * BLOCK : (b + 1) * BLOCK]
        acc = acc + jnp.dot(p.astype(bf16), kv_ref[src, 1], preferred_element_type=f32)
    l = jnp.sum(total, axis=1, keepdims=True)
    out_ref[0, : 2 * WIN, :] = acc.astype(bf16)
    lane = lax.broadcasted_iota(jnp.int32, (2 * WIN, 128), 1)
    stats = jnp.zeros((2 * WIN, 128), f32)
    for i, value in enumerate((m, l)):
        rest = value
        for j in range(3):
            term = rest.astype(bf16).astype(f32)
            rest = rest - term
            stats = jnp.where(lane == i + 2 * j, term, stats)
    rows = jnp.transpose(stats)
    out_ref[0, 2 * WIN :, :] = jnp.concatenate([rows[:8, :WIN], rows[:8, WIN:]], axis=0).astype(
        bf16
    )


def attention(queries, keyvals, bias, causal):
    return pl.pallas_call(
        attention_kernel,
        grid=(N_Z,),
        in_specs=[
            pl.BlockSpec((1, WIN, 2 * HEAD_DIM), lambda i: (i, 0, 0)),
            pl.BlockSpec((N_Y, 2, CTX_LOCAL, HEAD_DIM), lambda i: (0, 0, 0, 0)),
            pl.BlockSpec((N_Y, 1, CTX_LOCAL), lambda i: (0, 0, 0)),
            pl.BlockSpec((2 * WIN, BLOCK), lambda i: (0, 0)),
        ],
        out_specs=pl.BlockSpec((1, 2 * WIN + STAT_ROWS, HEAD_DIM), lambda i: (i, 0, 0)),
        out_shape=jax.ShapeDtypeStruct((N_Z, 2 * WIN + STAT_ROWS, HEAD_DIM), bf16),
        scratch_shapes=[pltpu.VMEM((2 * WIN, N_Y * CTX_LOCAL), f32)],
        compiler_params=params(),
        name="attention",
    )(queries, keyvals, bias, causal)


def combine_kernel(in_ref, out_ref):
    stats = in_ref[:, 2 * WIN :, :].astype(f32)
    for head in range(2):
        st = stats[:, 8 * head : 8 * head + 8]
        m = st[:, 0] + st[:, 2] + st[:, 4]
        l = st[:, 1] + st[:, 3] + st[:, 5]
        w = jnp.exp2((m - jnp.max(m, axis=0, keepdims=True)) * SCALE2)
        w = w / jnp.sum(w * l, axis=0, keepdims=True)
        wide = jnp.concatenate([w, jnp.zeros((WIN - N_Z, WIN), f32)], axis=0)
        cols = jnp.transpose(wide)
        total = jnp.zeros((WIN, HEAD_DIM), f32)
        for z in range(N_Z):
            part = in_ref[z, head * WIN : (head + 1) * WIN, :].astype(f32)
            total = total + part * cols[:, z : z + 1]
        done = total.astype(bf16)
        for z in range(N_Z):
            out_ref[z, :, head * HEAD_DIM : (head + 1) * HEAD_DIM] = done


def combine(parts):
    return pl.pallas_call(
        combine_kernel,
        out_shape=jax.ShapeDtypeStruct((N_Z, WIN, 2 * HEAD_DIM), bf16),
        compiler_params=params(),
        name="combine",
    )(parts)


def project_kernel(a_ref, w_ref, resid_ref, out_ref):
    acc = resid_ref[...].astype(f32)
    for z in range(N_Z):
        acc = acc + jnp.dot(a_ref[z], w_ref[z], preferred_element_type=f32)
    done = acc.astype(bf16)
    for y in range(N_Y):
        out_ref[y] = done


def project(attended, w_cols, resid_rows):
    return pl.pallas_call(
        project_kernel,
        out_shape=jax.ShapeDtypeStruct((N_Y, WIN, COLS), bf16),
        compiler_params=params(),
        name="project",
    )(attended, w_cols, resid_rows)


def dispatch_kernel(parts_ref, table_ref, stream_ref, out_ref):
    total = parts_ref[0].astype(f32)
    for y in range(1, N_Y):
        total = total + parts_ref[y].astype(f32)
    stream = total.astype(bf16)
    stream_ref[...] = stream
    out_ref[...] = jnp.dot(table_ref[...], stream, preferred_element_type=f32).astype(bf16)


def dispatch(parts, table):
    return pl.pallas_call(
        dispatch_kernel,
        out_shape=(
            jax.ShapeDtypeStruct((WIN, COLS), bf16),
            jax.ShapeDtypeStruct((N_GRP * CAP, COLS), bf16),
        ),
        compiler_params=params(),
        name="dispatch",
    )(parts, table)


def experts_kernel(x_ref, gain_ref, wg_ref, wu_ref, wd_ref, out_ref):
    tokens = x_ref.shape[1]
    squares = jnp.zeros((tokens, COLS), f32)
    for z in range(N_Z):
        wide = x_ref[z].astype(f32)
        squares = squares + wide * wide
    factor = lax.rsqrt(jnp.sum(squares, axis=1, keepdims=True) * (1.0 / D) + 1e-06)
    gate = jnp.zeros((tokens, HIDDEN), f32)
    up = jnp.zeros((tokens, HIDDEN), f32)
    contract = (((1,), (1,)), ((), ()))
    for z in range(N_Z):
        cols = slice(z * COLS, (z + 1) * COLS)
        normed = (x_ref[z].astype(f32) * factor * gain_ref[:, cols]).astype(bf16)
        gate = gate + lax.dot_general(
            normed, wg_ref[:, cols], contract, preferred_element_type=f32
        )
        up = up + lax.dot_general(normed, wu_ref[:, cols], contract, preferred_element_type=f32)
    hidden = (gate / (1.0 + jnp.exp(-gate)) * up).astype(bf16)
    for z in range(N_Z):
        cols = slice(z * COLS, (z + 1) * COLS)
        out_ref[:, cols] = jnp.dot(
            hidden, wd_ref[:, cols], preferred_element_type=f32
        ).astype(bf16)


def experts(x, gain, w_gate, w_up, w_down, tile=128):
    tokens = x.shape[1]
    whole = pl.BlockSpec((HIDDEN, D), lambda i: (0, 0))
    return pl.pallas_call(
        experts_kernel,
        grid=(tokens // tile,),
        in_specs=[
            pl.BlockSpec((N_Z, tile, COLS), lambda i: (0, i, 0)),
            pl.BlockSpec((1, D), lambda i: (0, 0)),
            whole,
            whole,
            whole,
        ],
        out_specs=pl.BlockSpec((tile, D), lambda i: (i, 0)),
        out_shape=jax.ShapeDtypeStruct((tokens, D), bf16),
        compiler_params=params(),
        name="experts",
    )(x, gain, w_gate, w_up, w_down)


def mix_kernel(table_ref, parts_ref, out_ref):
    out_ref[...] = jnp.dot(
        table_ref[...], parts_ref[...], preferred_element_type=f32
    ).astype(bf16)


def mix(table, parts):
    tile = 1024
    return pl.pallas_call(
        mix_kernel,
        grid=(D // tile,),
        in_specs=[
            pl.BlockSpec(table.shape, lambda i: (0, 0)),
            pl.BlockSpec((parts.shape[0], tile), lambda i: (0, i)),
        ],
        out_specs=pl.BlockSpec((WIN, tile), lambda i: (0, i)),
        out_shape=jax.ShapeDtypeStruct((WIN, D), bf16),
        compiler_params=params(),
        name="mix",
    )(table, parts)


def per_device(
    queries,
    kv_cache,
    kv_scale,
    block_mask,
    resid,
    w_out,
    norm_gain,
    expert_ids,
    gate_weights,
    w_gate,
    w_up,
    w_down,
):
    y_pos = lax.axis_index("y")
    z_pos = lax.axis_index("z")

    blocks = CTX_LOCAL // BLOCK
    spread = kv_scale[0].reshape(blocks, 2, KV_HEADS).transpose(2, 1, 0)
    raw = kv_cache[0].reshape(blocks, BLOCK, 2, KV_HEADS, HEAD_DIM).transpose(3, 2, 0, 1, 4)
    keyvals = (raw.astype(f32) * spread[:, :, :, None, None]).astype(bf16)
    keyvals = keyvals.reshape(KV_HEADS, 2, CTX_LOCAL, HEAD_DIM)
    keyvals = lax.all_to_all(keyvals, "y", 0, 0, tiled=True)
    queries_mine = lax.all_to_all(
        jnp.broadcast_to(queries, (N_Z,) + queries.shape[1:]), "z", 0, 0, tiled=True
    )

    mask = block_mask[0, 0].reshape(N_Y, N_Z, blocks)
    mask = lax.dynamic_slice_in_dim(mask, z_pos, 1, 1)[:, 0]
    bias = jnp.where(mask == 1, 0.0, MASKED).astype(f32)
    bias = jnp.repeat(bias, BLOCK, axis=1)[:, None, :]
    place = jnp.arange(BLOCK, dtype=jnp.int32)
    later = (place[None, :] > place[:, None]) & (z_pos == N_Z - 1)
    causal = jnp.where(later, MASKED, 0.0).astype(f32)
    causal = jnp.concatenate([causal, causal], axis=0)

    w_cols = w_out.reshape(2 * HEAD_DIM, N_Z, COLS).transpose(1, 0, 2)
    w_cols = lax.all_to_all(w_cols, "z", 0, 0, tiled=True)
    resid_cols = resid[0].reshape(-1, N_Z, COLS).transpose(1, 0, 2)
    resid_cols = lax.all_to_all(resid_cols, "z", 0, 0, tiled=True).reshape(-1, COLS)
    rows = WIN // N_Y
    resid_rows = lax.dynamic_update_slice_in_dim(
        jnp.zeros((WIN, COLS), bf16), resid_cols, y_pos * rows, 0
    )

    owners = jnp.arange(N_GRP, dtype=jnp.int32) * E_SUB + y_pos
    matches = expert_ids[0][None, :, :] == owners[:, None, None]
    chosen = jnp.any(matches, axis=-1)
    weight = jnp.sum(jnp.where(matches, gate_weights[0][None, :, :], 0.0), axis=-1)
    slot = jnp.cumsum(chosen.astype(jnp.int32), axis=1) - 1
    in_slot = chosen[:, None, :] & (
        slot[:, None, :] == jnp.arange(CAP, dtype=jnp.int32)[None, :, None]
    )
    out_table = in_slot.astype(bf16).reshape(N_GRP * CAP, WIN)
    back_table = jnp.where(in_slot, weight[:, None, :], 0.0).astype(bf16)
    back_table = back_table.reshape(N_GRP * CAP, WIN).T

    parts = attention(queries_mine, keyvals, bias, causal)
    parts = lax.all_to_all(parts, "z", 0, 0, tiled=True)
    attended = lax.all_to_all(combine(parts), "z", 0, 0, tiled=True)
    projected = lax.all_to_all(project(attended, w_cols, resid_rows), "y", 0, 0, tiled=True)
    stream, outgoing = dispatch(projected, out_table)

    arrivals = lax.all_to_all(
        outgoing.reshape(N_GRP, CAP, COLS), ("x", "c"), 0, 0, tiled=True
    ).reshape(N_GRP * CAP, COLS)
    arrivals = lax.all_gather(arrivals, "z", axis=0, tiled=False)
    pieces = experts(arrivals, norm_gain[None], w_gate[0], w_up[0], w_down[0])
    returned = lax.all_to_all(
        pieces.reshape(N_GRP, CAP, D), ("x", "c"), 0, 0, tiled=True
    ).reshape(N_GRP * CAP, D)
    mixture = mix(back_table, returned).reshape(N_Y, rows, D)

    mixture = lax.all_to_all(mixture, "y", 0, 0, tiled=True)
    mixture = jnp.sum(mixture.astype(f32), axis=0).astype(bf16).reshape(N_Z, -1, D)
    mixture = lax.all_to_all(mixture, "z", 0, 0, tiled=True)
    mixture = jnp.sum(mixture.astype(f32), axis=0)
    stream_rows = lax.dynamic_slice_in_dim(stream, y_pos * rows, rows, 0)
    stream_rows = lax.all_to_all(
        stream_rows.reshape(N_Z, -1, COLS), "z", 0, 0, tiled=True
    )
    stream_rows = stream_rows.transpose(1, 0, 2).reshape(-1, D)
    return (stream_rows.astype(f32) + mixture).astype(bf16)[None]


def solution(mesh):
    fine = Mesh(mesh.devices.reshape(N_Y, N_Z, N_X, N_C), ("y", "z", "x", "c"))
    seq, grp = ("y", "z"), ("x", "c")
    in_specs = (
        P(grp, None, seq),
        P(grp, seq, None),
        P(grp, seq, None),
        P(grp, None, None),
        P(grp, seq, None),
        P(seq, None),
        P(),
        P(grp, None, None),
        P(grp, None, None),
        P(grp, seq, None),
        P(grp, seq, None),
        P(grp, seq, None),
    )
    return jax.shard_map(
        per_device, mesh=fine, in_specs=in_specs, out_specs=P(grp, seq, None), check_vma=False
    )
```

time: 840 us -> 392 us (0.47)
  waiting for transfers between devices: 534 us -> 177 us
  other arithmetic: 106 us -> 8.2 us
  matrix products: 50.7 us -> 0 us
  Pallas kernels: 0 us -> 42.1 us
  blocking collectives: 53.6 us -> 89.4 us
  local copies, waits for them, and re-layouts: 42.5 us -> 21.7 us
    unnamed x6 -> x1, waiting for transfers between devices: 291 us -> 0.02 us
    all_gather x2 -> x1, waiting for transfers between devices: 150 us -> 48.3 us  [per_device(): arrivals = lax.all_gather(arrivals, 'z', axis=0, tiled=False)]
    unnamed x4 -> x1, other arithmetic: 79.7 us -> 0.66 us
    dot_general x13 -> x0, matrix products: 50.7 us -> none  [the longest x4 17.3 us: per_device(): jnp.einsum('wgd,kd->gwk', query_block, key_block, preferred_element_type=...]
    pallas_call x0 -> x6, Pallas kernels: none -> 42.1 us  [the longest x1 19 us: attention(): pl.pallas_call(attention_kernel, grid=(N_Z,), in_specs=[pl.BlockSpec((1,...]
    all_to_all x1 -> x3, blocking collectives: 53.6 us -> 89.4 us  [the longest x1 53.9 us: per_device(): lax.all_to_all(pieces.reshape(N_GRP, CAP, D), ('x', 'c'), 0, 0, tiled=True)]
    all_to_all x4 -> x9, waiting for transfers between devices: 93.3 us -> 128 us  [the longest x1 45.3 us: per_device(): w_cols = lax.all_to_all(w_cols, 'z', 0, 0, tiled=True)]
    concatenate x6 -> x0, local copies, waits for them, and re-layouts: 15.9 us -> none  [the longest x4 15.9 us: per_device(): partial_value = jnp.concatenate(pieces, axis=1)]
  transfers between devices with their start and end apart: 8 -> 10, of which waited for: 6 -> 10; matrix products, arithmetic and copies ran while one was open for 13% -> 6% of each run, Pallas kernels for 0% -> 1%
where the time goes in v1:
time: 392 us; the launch traced here: 391 us
  waiting for transfers between devices  177 us (45%)
  blocking collectives  89.4 us (23%)
  Pallas kernels  42.1 us (11%)
  starting transfers between devices  38.9 us (10%)
  local copies, waits for them, and re-layouts  21.7 us (6%)
  between operations  13.6 us (3%)
  other arithmetic  8.2 us (2%)
    all_to_all x1, blocking collectives, per_device(): lax.all_to_all(pieces.reshape(N_GRP, CAP, D), ('x', 'c'), 0, 0, tiled=True)  53.9 us
    all_gather x1, waiting for transfers between devices, per_device(): arrivals = lax.all_gather(arrivals, 'z', axis=0, tiled=False)  48.3 us
    all_to_all x1, waiting for transfers between devices, per_device(): w_cols = lax.all_to_all(w_cols, 'z', 0, 0, tiled=True)  45.3 us
    all_to_all x1, waiting for transfers between devices, per_device(): keyvals = lax.all_to_all(keyvals, 'y', 0, 0, tiled=True)  24.5 us
    all_to_all x1, blocking collectives, per_device(): parts = lax.all_to_all(parts, 'z', 0, 0, tiled=True)  21.7 us
    pallas_call x1, Pallas kernels, attention(): pl.pallas_call(attention_kernel, grid=(N_Z,), in_specs=[pl.BlockSpec((1,...  19 us
    all_to_all x1, blocking collectives, per_device(): lax.all_to_all(outgoing.reshape(N_GRP, CAP, COLS), ('x', 'c'), 0, 0, tile...  13.9 us
    all_to_all x1, waiting for transfers between devices, per_device(): mixture = lax.all_to_all(mixture, 'y', 0, 0, tiled=True)  13.3 us
  transfers between devices with their start and end apart: 10, of which 10 were waited for; matrix products, arithmetic and copies ran while one was open for 6% of the time, Pallas kernels for 1%

profile of v1, /device:TPU:2, one launch (start us, length us, event | category | flops | bytes accessed | tf_op | source)
XLA Modules:
  0.0 390.8 jit_solution(12568553405951397223)
XLA Ops:
  6.5 1.7 broadcast_in_dim.70
  8.2 8.5 %all-to-all-start = ((bf16[8,128,256]{2,1,0:T(8,128)(2,1)}), bf16[8,128,256]{2,1,0:T(8,128)(2,1)S(1)}, u32[]{:S(2)}, u32[]{:S(2)}) async-start(bf16[8,128,256]{2,1,0:T(8,128)(2,1)} %broadcast_in_dim.70), calls=%async_computation | async-start | bytes 1048576 | tf_op jit(solution)/shard_map/all_to_all | solution.py:252
  16.7 5.0 %reshape.93 = f32[8,128,2,4,128]{4,3,2,1,0:T(4,128)} reshape(bf16[1,1024,1024]{2,1,0:T(8,128)(2,1)} %param.13) | data formatting | bytes 6291456 | tf_op jit(solution)/shard_map/convert_element_type | solution.py:249
  21.7 0.1 copy.85
  21.8 4.4 %fusion = bf16[4,2,8,128,128]{4,3,2,1,0:T(8,128)(2,1)} fusion(f32[8,128,2,4,128]{4,3,2,1,0:T(4,128)} %reshape.93, f32[4,2,8]{2,1,0:T(2,128)S(1)} %copy.86), kind=kLoop, calls=%fused_computation.1 | loop fusion | flops 2097152 | bytes 6291712 | tf_op jit(solution)/shard_map/convert_element_type | solution.py:249
  26.2 8.0 %all-to-all-done.q_ref = bf16[8,128,256]{2,1,0:T(8,128)(2,1)S(1)} async-done(((bf16[8,128,256]{2,1,0:T(8,128)(2,1)}), bf16[8,128,256]{2,1,0:T(8,128)(2,1)S(1)}, u32[]{:S(2)}, u32[]{:S(2)}) %all-to-all-start) | async-done | bytes 524320 | tf_op jit(solution)/shard_map/all_to_all | solution.py:252
  34.2 0.8 copy-done.3
  35.0 4.5 %all-to-all-start.1 = ((bf16[4,2,1024,128]{3,2,1,0:T(8,128)(2,1)}), bf16[4,2,1024,128]{3,2,1,0:T(8,128)(2,1)S(1)}, u32[]{:S(2)}, u32[]{:S(2)}) async-start(bf16[4,2,1024,128]{3,2,1,0:T(8,128)(2,1)} %bitcast.44), calls=%async_computation.1 | async-start | bytes 4194304 | tf_op jit(solution)/shard_map/all_to_all | solution.py:251
  39.4 0.5 broadcast.44
  40.0 0.7 reduce.4
  40.6 0.1 reshape_squeeze.11
  40.7 0.7 pad_maximum_fusion.causal_ref
  41.4 24.5 %all-to-all-done.1.kv_ref = bf16[4,2,1024,128]{3,2,1,0:T(8,128)(2,1)S(1)} async-done(((bf16[4,2,1024,128]{3,2,1,0:T(8,128)(2,1)}), bf16[4,2,1024,128]{3,2,1,0:T(8,128)(2,1)S(1)}, u32[]{:S(2)}, u32[]{:S(2)}) %all-to-all-start.1) | async-done | bytes 2097184 | tf_op jit(solution)/shard_map/all_to_all | solution.py:251
  66.0 0.8 broadcast_in_dim.73
  66.7 0.6 copy-done.1
  67.3 19.0 %attention.1 = bf16[8,272,128]{2,1,0:T(8,128)(2,1)} custom-call(bf16[8,128,256]{2,1,0:T(8,128)(2,1)} %copy-done.3, bf16[4,2,1024,128]{3,2,1,0:T(8,128)(2,1)} %copy-done.1, f32[4,1,1024]{2,1,0:T(1,128)} %bitcast.55, f32[256,128]{1,0:T(8,128)} %pad_maximum_fusion.causal_ref), custom_call_target="tpu_custom_call" | custom-call | tf_op jit(solution)/shard_map/attention/pallas_call | solution.py:78
  86.3 21.7 %all_to_all.60.in_ref = bf16[8,272,128]{2,1,0:T(8,128)(2,1)} all-to-all(bf16[8,272,128]{2,1,0:T(8,128)(2,1)} %attention.1), channel_id=1, replica_groups=mesh['y'=4,'z'=8,'x'=4,'c'=2] {'z'}, dimensions={0} | all-to-all | bytes 1114112 | tf_op jit(solution)/shard_map/all_to_all | solution.py:287
  107.9 3.3 all-to-all-start.5
  111.3 2.4 combine.1
  113.7 5.6 %all-to-all-done.5 = bf16[8,4,512]{2,1,0:T(4,128)(2,1)S(1)} async-done(((bf16[8,4,512]{2,1,0:T(4,128)(2,1)}), bf16[8,4,512]{2,1,0:T(4,128)(2,1)S(1)}, u32[]{:S(2)}, u32[]{:S(2)}) %all-to-all-start.5) | async-done | bytes 32800 | tf_op jit(solution)/shard_map/all_to_all | solution.py:268
  119.2 3.5 all-to-all-start.3
  122.7 3.3 copy.88
  126.0 2.4 copy.89
  128.5 8.2 %all-to-all-done.3.a_ref = bf16[8,128,256]{2,1,0:T(8,128)(2,1)S(1)} async-done(((bf16[8,128,256]{2,1,0:T(8,128)(2,1)}), bf16[8,128,256]{2,1,0:T(8,128)(2,1)S(1)}, u32[]{:S(2)}, u32[]{:S(2)}) %all-to-all-start.3) | async-done | bytes 524320 | tf_op jit(solution)/shard_map/all_to_all | solution.py:288
  136.7 0.8 copy-done.2
  137.5 3.6 all-to-all-start.4
  141.1 0.0 copy-done.6
  141.1 0.0 copy-done.8
  141.1 0.1 fusion.5
  141.2 0.1 copy.94
  141.4 0.1 compare_reduce_fusion
  141.5 0.2 copy.92
  141.6 0.3 reduce_window_sum.11
  142.0 0.0 copy-start.5
  142.0 45.3 %all-to-all-done.4.w_ref = bf16[8,256,512]{2,1,0:T(8,128)(2,1)S(1)} async-done(((bf16[8,256,512]{2,1,0:T(8,128)(2,1)}), bf16[8,256,512]{2,1,0:T(8,128)(2,1)S(1)}, u32[]{:S(2)}, u32[]{:S(2)}) %all-to-all-start.4) | async-done | bytes 2097184 | tf_op jit(solution)/shard_map/all_to_all | solution.py:266
  187.3 1.3 copy-done
  188.6 2.9 project.1
  191.6 3.5 all-to-all-start.6
  195.0 0.0 all-gather.2.cloned.1.call-start
  195.1 0.1 copy.91
  195.3 0.1 eq.56
  195.3 0.7 fusion.1
  196.1 0.8 copy.93.table_ref
  196.8 6.2 %all-to-all-done.6.parts_ref = bf16[4,128,512]{2,1,0:T(8,128)(2,1)S(1)} async-done(((bf16[4,128,512]{2,1,0:T(8,128)(2,1)}), bf16[4,128,512]{2,1,0:T(8,128)(2,1)S(1)}, u32[]{:S(2)}, u32[]{:S(2)}) %all-to-all-start.6) | async-done | bytes 524320 | tf_op jit(solution)/shard_map/all_to_all | solution.py:289
  203.1 0.8 copy-done.4
  203.9 2.2 dispatch.1
  206.1 13.9 %all_to_all.61 = bf16[8,64,512]{2,1,0:T(8,128)(2,1)} all-to-all(bf16[8,64,512]{2,1,0:T(8,128)(2,1)} %bitcast.51), channel_id=1, replica_groups=mesh['y'=4,'z'=8,'x'=4,'c'=2] {'x','c'}, dimensions={0} | all-to-all | bytes 1048576 | tf_op jit(solution)/shard_map/all_to_all | solution.py:292
  219.9 0.0 all-gather.2.cloned.1.call-update
  220.0 48.3 %all-gather.2.cloned.1.call-done.x_ref = bf16[8,512,512]{2,1,0:T(8,128)(2,1)} async-done(((bf16[1,512,512]{2,1,0:T(8,128)(2,1)}), bf16[8,512,512]{2,1,0:T(8,128)(2,1)}) %all-gather.2.cloned.1.call-update) | async-done | bytes 4194320 | tf_op jit(solution)/shard_map/all_gather | solution.py:295
  268.3 11.0 %experts.1 = bf16[512,4096]{1,0:T(8,128)(2,1)} custom-call(bf16[8,512,512]{2,1,0:T(8,128)(2,1)} %all-gather.2.cloned.1.call-done.x_ref, f32[1,4096]{1,0:T(1,128)} %bitcast.57, bf16[192,4096]{1,0:T(8,128)(2,1)} %bitcast.47, bf16[192,4096]{1,0:T(8,128)(2,1)} %bitcast.48, bf16[192,4096]{1,0:T(8,128)(2,1)} %bitcast.49), custom_call_target="tpu_custom_call" | custom-call | tf_op jit(solution)/shard_map/experts/pallas_call | solution.py:190
  279.3 53.9 %all_to_all.62 = bf16[8,64,4096]{2,1,0:T(8,128)(2,1)} all-to-all(bf16[8,64,4096]{2,1,0:T(8,128)(2,1)} %bitcast.42), channel_id=1, replica_groups=mesh['y'=4,'z'=8,'x'=4,'c'=2] {'x','c'}, dimensions={0} | all-to-all | bytes 8388608 | tf_op jit(solution)/shard_map/all_to_all | solution.py:297
  333.2 4.6 %mix.1 = bf16[128,4096]{1,0:T(8,128)(2,1)} custom-call(bf16[128,512]{1,0:T(8,128)(2,1)} %get-tuple-element.9.table_ref, bf16[512,4096]{1,0:T(8,128)(2,1)} %bitcast.41), custom_call_target="tpu_custom_call" | custom-call | tf_op jit(solution)/shard_map/mix/pallas_call | solution.py:215
  337.8 4.3 %all-to-all-start.10 = ((bf16[4,32,4096]{2,1,0:T(8,128)(2,1)}), bf16[4,32,4096]{2,1,0:T(8,128)(2,1)S(1)}, u32[]{:S(2)}, u32[]{:S(2)}) async-start(bf16[4,32,4096]{2,1,0:T(8,128)(2,1)} %bitcast.45), calls=%async_computation.10 | async-start | bytes 2097152 | tf_op jit(solution)/shard_map/all_to_all | solution.py:302
  342.1 0.8 constant_dynamic-slice_fusion
  342.9 0.6 reshape.86
  343.5 13.3 %all-to-all-done.10 = bf16[4,32,4096]{2,1,0:T(8,128)(2,1)S(1)} async-done(((bf16[4,32,4096]{2,1,0:T(8,128)(2,1)}), bf16[4,32,4096]{2,1,0:T(8,128)(2,1)S(1)}, u32[]{:S(2)}, u32[]{:S(2)}) %all-to-all-start.10) | async-done | bytes 1048608 | tf_op jit(solution)/shard_map/all_to_all | solution.py:302
  356.8 4.3 %all-to-all-start.7 = ((bf16[8,4,512]{2,1,0:T(4,128)(2,1)}), bf16[8,4,512]{2,1,0:T(4,128)(2,1)S(1)}, u32[]{:S(2)}, u32[]{:S(2)}) async-start(bf16[8,4,512]{2,1,0:T(4,128)(2,1)} %reshape.86), calls=%async_computation.7 | async-start | bytes 65536 | tf_op jit(solution)/shard_map/all_to_all | solution.py:307
  361.1 0.2 reduce_sum.33
  361.4 0.8 reshape.91
  362.2 7.0 %all-to-all-done.7 = bf16[8,4,512]{2,1,0:T(4,128)(2,1)S(1)} async-done(((bf16[8,4,512]{2,1,0:T(4,128)(2,1)}), bf16[8,4,512]{2,1,0:T(4,128)(2,1)S(1)}, u32[]{:S(2)}, u32[]{:S(2)}) %all-to-all-start.7) | async-done | bytes 32800 | tf_op jit(solution)/shard_map/all_to_all | solution.py:307
  369.2 3.4 all-to-all-start.11
  372.6 10.4 %all-to-all-done.11 = bf16[8,4,4096]{2,1,0:T(4,128)(2,1)S(1)} async-done(((bf16[8,4,4096]{2,1,0:T(4,128)(2,1)}), bf16[8,4,4096]{2,1,0:T(4,128)(2,1)S(1)}, u32[]{:S(2)}, u32[]{:S(2)}) %all-to-all-start.11) | async-done | bytes 262176 | tf_op jit(solution)/shard_map/all_to_all | solution.py:304
  383.0 0.3 convert_reduce_fusion
  383.3 0.6 fusion.2
  (28 shorter events, 0.2 us)
Async XLA Ops:
  8.2 26.0 %all-to-all-start = ((bf16[8,128,256]{2,1,0:T(8,128)(2,1)}), bf16[8,128,256]{2,1,0:T(8,128)(2,1)S(1)}, u32[]{:S(2)}, u32[]{:S(2)}) async-start(bf16[8,128,256]{2,1,0:T(8,128)(2,1)} %broadcast_in_dim.70), calls=%async_computation | async-start | bytes 1048576 | tf_op jit(solution)/shard_map/all_to_all | solution.py:252
  16.7 5.0 %copy-start.7 = (f32[1,8,8]{2,1,0:T(8,128)S(1)}, f32[1,8,8]{2,1,0:T(8,128)}, u32[]{:S(2)}) copy-start(f32[1,8,8]{2,1,0:T(8,128)} %param.14) | copy-start | bytes 772
  34.2 0.8 copy-start.3
  34.2 5.8 %copy-start.9 = (s32[1,1,256]{2,1,0:T(1,128)S(1)}, s32[1,1,256]{2,1,0:T(1,128)}, u32[]{:S(2)}) copy-start(s32[1,1,256]{2,1,0:T(1,128)} %param.15) | copy-start | bytes 3076
  35.0 31.0 %all-to-all-start.1 = ((bf16[4,2,1024,128]{3,2,1,0:T(8,128)(2,1)}), bf16[4,2,1024,128]{3,2,1,0:T(8,128)(2,1)S(1)}, u32[]{:S(2)}, u32[]{:S(2)}) async-start(bf16[4,2,1024,128]{3,2,1,0:T(8,128)(2,1)} %bitcast.44), calls=%async_computation.1 | async-start | bytes 4194304 | tf_op jit(solution)/shard_map/all_to_all | solution.py:251
  66.0 1.3 copy-start.1
  107.9 11.3 %all-to-all-start.5 = ((bf16[8,4,512]{2,1,0:T(4,128)(2,1)}), bf16[8,4,512]{2,1,0:T(4,128)(2,1)S(1)}, u32[]{:S(2)}, u32[]{:S(2)}) async-start(bf16[8,4,512]{2,1,0:T(4,128)(2,1)} %bitcast.10), calls=%async_computation.5 | async-start | bytes 65536 | tf_op jit(solution)/shard_map/all_to_all | solution.py:268
  119.2 17.4 %all-to-all-start.3 = ((bf16[8,128,256]{2,1,0:T(8,128)(2,1)}), bf16[8,128,256]{2,1,0:T(8,128)(2,1)S(1)}, u32[]{:S(2)}, u32[]{:S(2)}) async-start(bf16[8,128,256]{2,1,0:T(8,128)(2,1)} %combine.1), calls=%async_computation.3 | async-start | bytes 1048576 | tf_op jit(solution)/shard_map/all_to_all | solution.py:288
  136.6 0.8 copy-start.2
  136.6 4.4 %copy-start.6 = (s32[1,128,8]{1,2,0:T(8,128)S(1)}, s32[1,128,8]{1,2,0:T(8,128)}, u32[]{:S(2)}) copy-start(s32[1,128,8]{1,2,0:T(8,128)} %param.19) | copy-start | bytes 12292
  136.7 4.4 %copy-start.8 = (f32[1,128,8]{1,2,0:T(8,128)S(1)}, f32[1,128,8]{1,2,0:T(8,128)}, u32[]{:S(2)}) copy-start(f32[1,128,8]{1,2,0:T(8,128)} %param.20) | copy-start | bytes 12292
  137.5 49.8 %all-to-all-start.4 = ((bf16[8,256,512]{2,1,0:T(8,128)(2,1)}), bf16[8,256,512]{2,1,0:T(8,128)(2,1)S(1)}, u32[]{:S(2)}, u32[]{:S(2)}) async-start(bf16[8,256,512]{2,1,0:T(8,128)(2,1)} %bitcast.8), calls=%async_computation.4 | async-start | bytes 4194304 | tf_op jit(solution)/shard_map/all_to_all | solution.py:266
  142.0 45.3 %copy-start.5 = (bf16[128,512]{1,0:T(8,128)(2,1)}, bf16[128,512]{1,0:T(8,128)(2,1)S(1)}, u32[]{:S(2)}) copy-start(bf16[128,512]{1,0:T(8,128)(2,1)S(1)} %constant_dynamic-update-slice_fusion.resid_ref) | copy-start | bytes 393220
  187.3 1.3 copy-start
  191.6 11.5 %all-to-all-start.6 = ((bf16[4,128,512]{2,1,0:T(8,128)(2,1)}), bf16[4,128,512]{2,1,0:T(8,128)(2,1)S(1)}, u32[]{:S(2)}, u32[]{:S(2)}) async-start(bf16[4,128,512]{2,1,0:T(8,128)(2,1)} %project.1), calls=%async_computation.6 | async-start | bytes 1048576 | tf_op jit(solution)/shard_map/all_to_all | solution.py:289
  195.0 73.3 %all-gather.2.cloned.1.call-start = ((), (), s32[]{:S(2)}) async-start(), calls=%async_computation.12 | async-start | bytes 4718592 | tf_op jit(solution)/shard_map/all_gather | solution.py:295
  203.1 0.8 copy-start.4
  337.8 19.0 %all-to-all-start.10 = ((bf16[4,32,4096]{2,1,0:T(8,128)(2,1)}), bf16[4,32,4096]{2,1,0:T(8,128)(2,1)S(1)}, u32[]{:S(2)}, u32[]{:S(2)}) async-start(bf16[4,32,4096]{2,1,0:T(8,128)(2,1)} %bitcast.45), calls=%async_computation.10 | async-start | bytes 2097152 | tf_op jit(solution)/shard_map/all_to_all | solution.py:302
  356.8 12.3 %all-to-all-start.7 = ((bf16[8,4,512]{2,1,0:T(4,128)(2,1)}), bf16[8,4,512]{2,1,0:T(4,128)(2,1)S(1)}, u32[]{:S(2)}, u32[]{:S(2)}) async-start(bf16[8,4,512]{2,1,0:T(4,128)(2,1)} %reshape.86), calls=%async_computation.7 | async-start | bytes 65536 | tf_op jit(solution)/shard_map/all_to_all | solution.py:307
  369.2 13.8 %all-to-all-start.11 = ((bf16[8,4,4096]{2,1,0:T(4,128)(2,1)}), bf16[8,4,4096]{2,1,0:T(4,128)(2,1)S(1)}, u32[]{:S(2)}, u32[]{:S(2)}) async-start(bf16[8,4,4096]{2,1,0:T(4,128)(2,1)} %reshape.91), calls=%async_computation.11 | async-start | bytes 524288 | tf_op jit(solution)/shard_map/all_to_all | solution.py:304
Sparse Core Ops, SparseCore 0:
  220.1 48.1 all-gather.1

commit v2 on v1

--- a/solution.py
+++ b/solution.py
@@ -34,32 +34,87 @@
     return pltpu.CompilerParams(vmem_limit_bytes=VMEM)
 
 
-def attention_kernel(q_ref, kv_ref, bias_ref, causal_ref, out_ref, s_ref):
+def dequantize_kernel(y_ref, scale_ref, cache_ref, *out_refs):
+    step = pl.program_id(0)
+    for d, out_ref in enumerate(out_refs):
+        head = lax.rem(y_ref[0] + d, N_Y)
+        for part in range(2):
+            column = part * KV_HEADS + head
+            lanes = pl.ds(pl.multiple_of(column * HEAD_DIM, HEAD_DIM), HEAD_DIM)
+            for b in range(2):
+                rows = slice(b * BLOCK, (b + 1) * BLOCK)
+                raw = cache_ref[rows, lanes].astype(f32)
+                out_ref[part, rows, :] = (raw * scale_ref[2 * step + b, column]).astype(bf16)
+
+
+def dequantize(y_pos, scale, cache):
+    shape = jax.ShapeDtypeStruct((2, CTX_LOCAL, HEAD_DIM), bf16)
+    return pl.pallas_call(
+        dequantize_kernel,
+        grid_spec=pltpu.PrefetchScalarGridSpec(
+            num_scalar_prefetch=2,
+            grid=(CTX_LOCAL // (2 * BLOCK),),
+            in_specs=[pl.BlockSpec((2 * BLOCK, 2 * KV_HEADS * HEAD_DIM), lambda i, *_: (i, 0))],
+            out_specs=[pl.BlockSpec((2, 2 * BLOCK, HEAD_DIM), lambda i, *_: (0, i, 0))] * N_Y,
+        ),
+        out_shape=[shape] * N_Y,
+        compiler_params=params(),
+        cost_estimate=pl.CostEstimate(flops=1 << 20, bytes_accessed=4 << 20, transcendentals=0),
+        name="dequantize",
+    )(y_pos, scale, cache)
+
+
+def attend_chunks(q_ref, kv_refs, bias_ref, last_ref, s_ref, order):
     q_pair = jnp.concatenate([q_ref[0, :, :HEAD_DIM], q_ref[0, :, HEAD_DIM:]], axis=0)
     peak = jnp.full((2 * WIN, BLOCK), -jnp.inf, f32)
-    for src in range(N_Y):
+    row = lax.broadcasted_iota(jnp.int32, (2 * WIN, BLOCK), 0)
+    row = jnp.where(row >= WIN, row - WIN, row)
+    later = lax.broadcasted_iota(jnp.int32, (2 * WIN, BLOCK), 1) > row
+    for i, (kv_ref, d) in enumerate(zip(kv_refs, order)):
         s = lax.dot_general(
-            q_pair, kv_ref[src, 0], (((1,), (1,)), ((), ())), preferred_element_type=f32
+            q_pair, kv_ref[0], (((1,), (1,)), ((), ())), preferred_element_type=f32
         )
-        s = s + bias_ref[src]
-        if src == N_Y - 1:
-            s = jnp.concatenate(
-                [s[:, : CTX_LOCAL - BLOCK], s[:, CTX_LOCAL - BLOCK :] + causal_ref[...]], axis=1
-            )
-        s_ref[:, src * CTX_LOCAL : (src + 1) * CTX_LOCAL] = s
-        for b in range(CTX_LOCAL // BLOCK):
+        s = s + bias_ref[d]
+        cut = jnp.where(later & (last_ref[d] == 1), MASKED, 0.0)
+        end = CTX_LOCAL - BLOCK
+        s_ref[:, i * CTX_LOCAL : i * CTX_LOCAL + end] = s[:, :end]
+        tail = s[:, end:] + cut
+        s_ref[:, i * CTX_LOCAL + end : (i + 1) * CTX_LOCAL] = tail
+        for b in range(CTX_LOCAL // BLOCK - 1):
             peak = jnp.maximum(peak, s[:, b * BLOCK : (b + 1) * BLOCK])
-    m = jnp.max(peak, axis=1, keepdims=True)
+        peak = jnp.maximum(peak, tail)
+    return jnp.max(peak, axis=1, keepdims=True)
+
+
+def weigh_chunks(kv_refs, s_ref, m):
     total = jnp.zeros((2 * WIN, BLOCK), f32)
     acc = jnp.zeros((2 * WIN, HEAD_DIM), f32)
-    for src in range(N_Y):
-        s = s_ref[:, src * CTX_LOCAL : (src + 1) * CTX_LOCAL]
+    for i, kv_ref in enumerate(kv_refs):
+        s = s_ref[:, i * CTX_LOCAL : (i + 1) * CTX_LOCAL]
         p = jnp.exp2((s - m) * SCALE2)
         for b in range(CTX_LOCAL // BLOCK):
             total = total + p[:, b * BLOCK : (b + 1) * BLOCK]
-        acc = acc + jnp.dot(p.astype(bf16), kv_ref[src, 1], preferred_element_type=f32)
-    l = jnp.sum(total, axis=1, keepdims=True)
-    out_ref[0, : 2 * WIN, :] = acc.astype(bf16)
+        acc = acc + jnp.dot(p.astype(bf16), kv_ref[1], preferred_element_type=f32)
+    return jnp.sum(total, axis=1, keepdims=True), acc
+
+
+def near_kernel(last_ref, q_ref, bias_ref, kv0, kv1, kv3, acc_ref, stat_ref, s_ref):
+    kv_refs = (kv0, kv1, kv3)
+    m = attend_chunks(q_ref, kv_refs, bias_ref, last_ref, s_ref, (0, 1, 3))
+    l, acc = weigh_chunks(kv_refs, s_ref, m)
+    acc_ref[0] = acc
+    lane = lax.broadcasted_iota(jnp.int32, (2 * WIN, 128), 1)
+    stat_ref[0] = jnp.where(lane == 0, m, l)
+
+
+def far_kernel(last_ref, q_ref, bias_ref, kv2, acc_ref, stat_ref, out_ref, s_ref):
+    m = attend_chunks(q_ref, (kv2,), bias_ref, last_ref, s_ref, (2,))
+    before = stat_ref[0, :, :1]
+    m = jnp.maximum(m, before)
+    l, acc = weigh_chunks((kv2,), s_ref, m)
+    keep = jnp.exp2((before - m) * SCALE2)
+    l = l + stat_ref[0, :, 1:2] * keep
+    out_ref[0, : 2 * WIN, :] = (acc + acc_ref[0] * keep).astype(bf16)
     lane = lax.broadcasted_iota(jnp.int32, (2 * WIN, 128), 1)
     stats = jnp.zeros((2 * WIN, 128), f32)
     for i, value in enumerate((m, l)):
@@ -74,22 +129,49 @@
     )
 
 
-def attention(queries, keyvals, bias, causal):
-    return pl.pallas_call(
-        attention_kernel,
+def attention_specs(extra, outs, chunks):
+    whole = pl.BlockSpec((2, CTX_LOCAL, HEAD_DIM), lambda i, *_: (0, 0, 0))
+    return pltpu.PrefetchScalarGridSpec(
+        num_scalar_prefetch=1,
         grid=(N_Z,),
         in_specs=[
-            pl.BlockSpec((1, WIN, 2 * HEAD_DIM), lambda i: (i, 0, 0)),
-            pl.BlockSpec((N_Y, 2, CTX_LOCAL, HEAD_DIM), lambda i: (0, 0, 0, 0)),
-            pl.BlockSpec((N_Y, 1, CTX_LOCAL), lambda i: (0, 0, 0)),
-            pl.BlockSpec((2 * WIN, BLOCK), lambda i: (0, 0)),
-        ],
-        out_specs=pl.BlockSpec((1, 2 * WIN + STAT_ROWS, HEAD_DIM), lambda i: (i, 0, 0)),
-        out_shape=jax.ShapeDtypeStruct((N_Z, 2 * WIN + STAT_ROWS, HEAD_DIM), bf16),
-        scratch_shapes=[pltpu.VMEM((2 * WIN, N_Y * CTX_LOCAL), f32)],
-        compiler_params=params(),
-        name="attention",
-    )(queries, keyvals, bias, causal)
+            pl.BlockSpec((1, WIN, 2 * HEAD_DIM), lambda i, *_: (i, 0, 0)),
+            pl.BlockSpec((N_Y, 1, CTX_LOCAL), lambda i, *_: (0, 0, 0)),
+        ]
+        + [whole] * chunks
+        + [pl.BlockSpec((1,) + e, lambda i, *_: (i, 0, 0)) for e in extra],
+        out_specs=[pl.BlockSpec((1,) + o, lambda i, *_: (i, 0, 0)) for o in outs],
+        scratch_shapes=[pltpu.VMEM((2 * WIN, chunks * CTX_LOCAL), f32)],
+    )
+
+
+def near_attention(last, queries, bias, kv0, kv1, kv3):
+    square = (2 * WIN, HEAD_DIM)
+    return pl.pallas_call(
+        near_kernel,
+        grid_spec=attention_specs([], [square, square], 3),
+        out_shape=[jax.ShapeDtypeStruct((N_Z,) + square, f32)] * 2,
+        compiler_params=params(),
+        cost_estimate=pl.CostEstimate(
+            flops=8 << 30, bytes_accessed=8 << 20, transcendentals=6 << 20
+        ),
+        name="near_attention",
+    )(last, queries, bias, kv0, kv1, kv3)
+
+
+def far_attention(last, queries, bias, kv2, acc, stat):
+    square = (2 * WIN, HEAD_DIM)
+    message = (2 * WIN + STAT_ROWS, HEAD_DIM)
+    return pl.pallas_call(
+        far_kernel,
+        grid_spec=attention_specs([square, square], [message], 1),
+        out_shape=[jax.ShapeDtypeStruct((N_Z,) + message, bf16)],
+        compiler_params=params(),
+        cost_estimate=pl.CostEstimate(
+            flops=3 << 30, bytes_accessed=8 << 20, transcendentals=2 << 20
+        ),
+        name="far_attention",
+    )(last, queries, bias, kv2, acc, stat)[0]
 
 
 def combine_kernel(in_ref, out_ref):
@@ -123,7 +205,8 @@
 def project_kernel(a_ref, w_ref, resid_ref, out_ref):
     acc = resid_ref[...].astype(f32)
     for z in range(N_Z):
-        acc = acc + jnp.dot(a_ref[z], w_ref[z], preferred_element_type=f32)
+        w_rows = jnp.concatenate([w_ref[g, z] for g in range(N_GRP)], axis=0)
+        acc = acc + jnp.dot(a_ref[z], w_rows, preferred_element_type=f32)
     done = acc.astype(bf16)
     for y in range(N_Y):
         out_ref[y] = done
@@ -243,33 +326,34 @@
     y_pos = lax.axis_index("y")
     z_pos = lax.axis_index("z")
 
-    blocks = CTX_LOCAL // BLOCK
-    spread = kv_scale[0].reshape(blocks, 2, KV_HEADS).transpose(2, 1, 0)
-    raw = kv_cache[0].reshape(blocks, BLOCK, 2, KV_HEADS, HEAD_DIM).transpose(3, 2, 0, 1, 4)
-    keyvals = (raw.astype(f32) * spread[:, :, :, None, None]).astype(bf16)
-    keyvals = keyvals.reshape(KV_HEADS, 2, CTX_LOCAL, HEAD_DIM)
-    keyvals = lax.all_to_all(keyvals, "y", 0, 0, tiled=True)
     queries_mine = lax.all_to_all(
         jnp.broadcast_to(queries, (N_Z,) + queries.shape[1:]), "z", 0, 0, tiled=True
     )
-
+    chunks = dequantize(y_pos[None], kv_scale[0], kv_cache[0])
+    kv_own = chunks[0]
+    kv_from = {
+        d: lax.ppermute(chunks[d], "y", [(i, (i + d) % N_Y) for i in range(N_Y)])
+        for d in (1, 3, 2)
+    }
+
+    blocks = CTX_LOCAL // BLOCK
+    source = (y_pos - jnp.arange(N_Y, dtype=jnp.int32)) % N_Y
     mask = block_mask[0, 0].reshape(N_Y, N_Z, blocks)
     mask = lax.dynamic_slice_in_dim(mask, z_pos, 1, 1)[:, 0]
+    mask = jnp.take(mask, source, axis=0)
     bias = jnp.where(mask == 1, 0.0, MASKED).astype(f32)
     bias = jnp.repeat(bias, BLOCK, axis=1)[:, None, :]
-    place = jnp.arange(BLOCK, dtype=jnp.int32)
-    later = (place[None, :] > place[:, None]) & (z_pos == N_Z - 1)
-    causal = jnp.where(later, MASKED, 0.0).astype(f32)
-    causal = jnp.concatenate([causal, causal], axis=0)
-
-    w_cols = w_out.reshape(2 * HEAD_DIM, N_Z, COLS).transpose(1, 0, 2)
-    w_cols = lax.all_to_all(w_cols, "z", 0, 0, tiled=True)
-    resid_cols = resid[0].reshape(-1, N_Z, COLS).transpose(1, 0, 2)
-    resid_cols = lax.all_to_all(resid_cols, "z", 0, 0, tiled=True).reshape(-1, COLS)
+    last = ((source == N_Y - 1) & (z_pos == N_Z - 1)).astype(jnp.int32)
+
     rows = WIN // N_Y
-    resid_rows = lax.dynamic_update_slice_in_dim(
-        jnp.zeros((WIN, COLS), bf16), resid_cols, y_pos * rows, 0
-    )
+    part = 2 * HEAD_DIM // N_GRP
+    own_rows = resid.shape[1]
+    grp_pos = lax.axis_index("x") * N_C + lax.axis_index("c")
+    w_mine = lax.dynamic_slice_in_dim(w_out, grp_pos * part, part, 0)
+    early = jnp.concatenate([w_mine, resid[0]], axis=0)
+    early = early.reshape(part + own_rows, N_Z, COLS).transpose(1, 0, 2)
+    early, queries_mine = lax.optimization_barrier((early, queries_mine))
+    early = lax.all_to_all(early, "z", 0, 0, tiled=True)
 
     owners = jnp.arange(N_GRP, dtype=jnp.int32) * E_SUB + y_pos
     matches = expert_ids[0][None, :, :] == owners[:, None, None]
@@ -283,7 +367,13 @@
     back_table = jnp.where(in_slot, weight[:, None, :], 0.0).astype(bf16)
     back_table = back_table.reshape(N_GRP * CAP, WIN).T
 
-    parts = attention(queries_mine, keyvals, bias, causal)
+    acc, stat = near_attention(last, queries_mine, bias, kv_own, kv_from[1], kv_from[3])
+    parts = far_attention(last, queries_mine, bias, kv_from[2], acc, stat)
+    parts, early = lax.optimization_barrier((parts, early))
+    resid_rows = lax.dynamic_update_slice_in_dim(
+        jnp.zeros((WIN, COLS), bf16), early[:, part:].reshape(rows, COLS), y_pos * rows, 0
+    )
+    w_cols = lax.all_gather(early[:, :part], ("x", "c"), axis=0, tiled=False)
     parts = lax.all_to_all(parts, "z", 0, 0, tiled=True)
     attended = lax.all_to_all(combine(parts), "z", 0, 0, tiled=True)
     projected = lax.all_to_all(project(attended, w_cols, resid_rows), "y", 0, 0, tiled=True)
@@ -299,16 +389,14 @@
     ).reshape(N_GRP * CAP, D)
     mixture = mix(back_table, returned).reshape(N_Y, rows, D)
 
+    stream_rows = lax.dynamic_slice_in_dim(stream, y_pos * rows, rows, 0)
+    stream_rows = lax.dynamic_update_slice_in_dim(
+        jnp.zeros((rows, D), bf16), stream_rows, z_pos * COLS, 1
+    )
     mixture = lax.all_to_all(mixture, "y", 0, 0, tiled=True)
-    mixture = jnp.sum(mixture.astype(f32), axis=0).astype(bf16).reshape(N_Z, -1, D)
-    mixture = lax.all_to_all(mixture, "z", 0, 0, tiled=True)
-    mixture = jnp.sum(mixture.astype(f32), axis=0)
-    stream_rows = lax.dynamic_slice_in_dim(stream, y_pos * rows, rows, 0)
-    stream_rows = lax.all_to_all(
-        stream_rows.reshape(N_Z, -1, COLS), "z", 0, 0, tiled=True
-    )
-    stream_rows = stream_rows.transpose(1, 0, 2).reshape(-1, D)
-    return (stream_rows.astype(f32) + mixture).astype(bf16)[None]
+    mixture = jnp.sum(mixture.astype(f32), axis=0) + stream_rows.astype(f32)
+    mixture = lax.all_to_all(mixture.astype(bf16).reshape(N_Z, -1, D), "z", 0, 0, tiled=True)
+    return jnp.sum(mixture.astype(f32), axis=0).astype(bf16)[None]
 
 
 def solution(mesh):

time: 392 us -> 308 us (0.79)
  blocking collectives: 89.4 us -> 49.2 us
  waiting for transfers between devices: 177 us -> 143 us
  local copies, waits for them, and re-layouts: 21.7 us -> 9.34 us
  Pallas kernels: 42.1 us -> 53.3 us
  other arithmetic: 8.2 us -> 3.59 us
    all_to_all x5 -> x2, waiting for transfers between devices: 92.8 us -> 47.4 us  [the longest x1 47.4 us: per_device(): lax.all_to_all(pieces.reshape(N_GRP, CAP, D), ('x', 'c'), 0, 0, tiled=True)]
    all_to_all x1, blocking collectives: 53.9 us -> 14.6 us  [per_device(): lax.all_to_all(mixture.astype(bf16).reshape(N_Z, -1, D), 'z', 0, 0, tiled...]
    pallas_call x1 -> x3, Pallas kernels: 19 us -> 30.1 us  [the longest x1 15.4 us: near_attention(): pl.pallas_call(near_kernel, grid_spec=attention_specs([], [square, square...]
    all_to_all x5 -> x2, starting transfers between devices: 19.1 us -> 8.57 us  [the longest x1 5.14 us: per_device(): lax.all_to_all(pieces.reshape(N_GRP, CAP, D), ('x', 'c'), 0, 0, tiled=True)]
    ppermute x0 -> x3, waiting for transfers between devices: none -> 8.36 us  [per_device(): lax.ppermute(chunks[d], 'y', [(i, (i + d) % N_Y) for i in range(N_Y)])]
    unnamed x23 -> x21, local copies, waits for them, and re-layouts: 8.19 us -> 2.25 us
    ppermute x0 -> x3, starting transfers between devices: none -> 5.22 us  [per_device(): lax.ppermute(chunks[d], 'y', [(i, (i + d) % N_Y) for i in range(N_Y)])]
    convert_element_type x1 -> x0, local copies, waits for them, and re-layouts: 5.03 us -> none  [per_device(): keyvals = (raw.astype(f32) * spread[:, :, :, None, None]).astype(bf16)]
  transfers between devices with their start and end apart: 10 -> 11, of which waited for: 10 -> 7; matrix products, arithmetic and copies ran while one was open for 6% -> 3% of each run, Pallas kernels for 1% -> 11%
where the time goes in v2:
time: 308 us; the launch traced here: 307 us
  waiting for transfers between devices  143 us (46%)
  Pallas kernels  53.3 us (17%)
  blocking collectives  49.2 us (16%)
  starting transfers between devices  35.1 us (11%)
  between operations  13.6 us (4%)
  local copies, waits for them, and re-layouts  9.34 us (3%)
  other arithmetic  3.59 us (1%)
    all_gather x1, waiting for transfers between devices, per_device(): arrivals = lax.all_gather(arrivals, 'z', axis=0, tiled=False)  48.4 us
    all_to_all x1, waiting for transfers between devices, per_device(): lax.all_to_all(pieces.reshape(N_GRP, CAP, D), ('x', 'c'), 0, 0, tiled=True)  47.4 us
    all_to_all x1, blocking collectives, per_device(): parts = lax.all_to_all(parts, 'z', 0, 0, tiled=True)  20.7 us
    pallas_call x1, Pallas kernels, near_attention(): pl.pallas_call(near_kernel, grid_spec=attention_specs([], [square, square...  15.4 us
    all_to_all x1, blocking collectives, per_device(): lax.all_to_all(mixture.astype(bf16).reshape(N_Z, -1, D), 'z', 0, 0, tiled...  14.6 us
    all_to_all x1, waiting for transfers between devices, per_device(): mixture = lax.all_to_all(mixture, 'y', 0, 0, tiled=True)  14.1 us
    all_to_all x1, blocking collectives, per_device(): lax.all_to_all(outgoing.reshape(N_GRP, CAP, COLS), ('x', 'c'), 0, 0, tile...  13.9 us
    all_to_all x1, waiting for transfers between devices, per_device(): attended = lax.all_to_all(combine(parts), 'z', 0, 0, tiled=True)  12.7 us
  transfers between devices with their start and end apart: 11, of which 7 were waited for; matrix products, arithmetic and copies ran while one was open for 3% of the time, Pallas kernels for 11%

profile of v2, /device:TPU:2, one launch (start us, length us, event | category | flops | bytes accessed | tf_op | source)
XLA Modules:
  0.0 306.7 jit_solution(7922565869879945742)
XLA Ops:
  6.5 1.8 broadcast_in_dim.83
  8.4 8.6 %all-to-all-start = ((bf16[8,128,256]{2,1,0:T(8,128)(2,1)}), bf16[8,128,256]{2,1,0:T(8,128)(2,1)S(1)}, u32[]{:S(2)}, u32[]{:S(2)}) async-start(bf16[8,128,256]{2,1,0:T(8,128)(2,1)} %broadcast_in_dim.83), calls=%async_computation | async-start | bytes 1048576 | tf_op jit(solution)/shard_map/all_to_all | solution.py:329
  17.0 4.7 %dequantize.1 = (bf16[2,1024,128]{2,1,0:T(8,128)(2,1)}, bf16[2,1024,128]{2,1,0:T(8,128)(2,1)}, bf16[2,1024,128]{2,1,0:T(8,128)(2,1)}, bf16[2,1024,128]{2,1,0:T(8,128)(2,1)}) custom-call(s32[1]{0:T(128)} %bitcast.11.y_ref, f32[8,8]{1,0:T(8,128)} %bitcast.60, bf16[1024,1024]{1,0:T(8,128)(2,1)} %bitcast.39), custom_call_target="tpu_custom_call" | custom-call | flops 1048576 | bytes 4194304 | tf_op jit(solution)/shard_map/dequantize/pallas_call | solution.py:52
  21.7 1.6 collective-permute-start.1
  23.3 1.7 collective-permute-start.2
  24.9 2.0 collective-permute-start
  27.0 0.5 broadcast.144
  27.5 0.7 reduce.4
  28.1 0.1 reshape_squeeze.3
  28.2 0.1 copy.52
  28.3 0.0 copy-done.5
  28.4 0.6 gather_fusion
  29.0 0.6 and_convert_fusion.last_ref
  29.6 0.1 fusion.2
  29.7 4.8 %all-to-all-done.q_ref = bf16[8,128,256]{2,1,0:T(8,128)(2,1)S(1)} async-done(((bf16[8,128,256]{2,1,0:T(8,128)(2,1)}), bf16[8,128,256]{2,1,0:T(8,128)(2,1)S(1)}, u32[]{:S(2)}, u32[]{:S(2)}) %all-to-all-start) | async-done | bytes 524320 | tf_op jit(solution)/shard_map/all_to_all | solution.py:329
  34.5 1.0 copy.49
  35.4 3.4 %all-to-all-start.1 = ((bf16[8,36,512]{2,1,0:T(8,128)(2,1)}), bf16[8,36,512]{2,1,0:T(8,128)(2,1)S(1)}, u32[]{:S(2)}, u32[]{:S(2)}) async-start(bf16[8,36,512]{2,1,0:T(8,128)(2,1)} %copy.49), calls=%async_computation.1 | async-start | bytes 655360 | tf_op jit(solution)/shard_map/all_to_all | solution.py:356
  38.8 0.0 all-gather.6.cloned.1.call-start
  38.9 0.0 collective-permute-done.1.kv1
  38.9 8.4 %collective-permute-done.2.kv3 = bf16[2,1024,128]{2,1,0:T(8,128)(2,1)} collective-permute-done((bf16[2,1024,128]{2,1,0:T(8,128)(2,1)}, bf16[2,1024,128]{2,1,0:T(8,128)(2,1)}, u32[]{:S(2)}, u32[]{:S(2)}) %collective-permute-start.2) | collective-permute-done | bytes 524320 | tf_op jit(solution)/shard_map/ppermute | solution.py:335
  47.3 0.7 broadcast_in_dim.88
  47.9 15.4 %near_attention.1 = (f32[8,256,128]{2,1,0:T(8,128)}, f32[8,256,128]{2,1,0:T(8,128)}) custom-call(s32[4]{0:T(128)} %and_convert_fusion.last_ref, bf16[8,128,256]{2,1,0:T(8,128)(2,1)} %copy-done.4, f32[4,1,1024]{2,1,0:T(1,128)} %bitcast.56, bf16[2,1024,128]{2,1,0:T(8,128)(2,1)} %get-tuple-element.19.kv0, bf16[2,1024,128]{2,1,0:T(8,128)(2,1)} %collective-permute-done.1.kv1, ...), custom_call_target="tpu_custom_call" | custom-call | flops 8589934592 | bytes 8388608 | tf_op jit(solution)/shard_map/near_attention/pallas_call | solution.py:150
  63.3 0.0 collective-permute-done.kv2
  63.3 10.0 %far_attention.1 = bf16[8,272,128]{2,1,0:T(8,128)(2,1)} custom-call(s32[4]{0:T(128)} %and_convert_fusion.last_ref, bf16[8,128,256]{2,1,0:T(8,128)(2,1)} %copy-done.4, f32[4,1,1024]{2,1,0:T(1,128)} %bitcast.57, bf16[2,1024,128]{2,1,0:T(8,128)(2,1)} %collective-permute-done.kv2, f32[8,256,128]{2,1,0:T(8,128)} %get-tuple-element.22.acc_ref, ...), custom_call_target="tpu_custom_call" | custom-call | flops 3221225472 | bytes 8388608 | tf_op jit(solution)/shard_map/far_attention/pallas_call | solution.py:165
  73.3 0.0 all-to-all-done.1
  73.3 0.7 slice.6
  74.1 0.0 all-gather.6.cloned.1.call-update
  74.1 20.7 %all_to_all.45.in_ref = bf16[8,272,128]{2,1,0:T(8,128)(2,1)} all-to-all(bf16[8,272,128]{2,1,0:T(8,128)(2,1)} %far_attention.1), channel_id=1, replica_groups=mesh['y'=4,'z'=8,'x'=4,'c'=2] {'z'}, dimensions={0} | all-to-all | bytes 1114112 | tf_op jit(solution)/shard_map/all_to_all | solution.py:377
  94.8 2.4 combine.1
  97.2 3.5 %all-to-all-start.3 = ((bf16[8,128,256]{2,1,0:T(8,128)(2,1)}), bf16[8,128,256]{2,1,0:T(8,128)(2,1)S(1)}, u32[]{:S(2)}, u32[]{:S(2)}) async-start(bf16[8,128,256]{2,1,0:T(8,128)(2,1)} %combine.1), calls=%async_computation.3 | async-start | bytes 1048576 | tf_op jit(solution)/shard_map/all_to_all | solution.py:378
  100.7 0.0 copy-done.6
  100.7 0.1 compare_reduce_fusion
  100.8 0.3 reduce_window_sum.11
  101.1 0.0 copy-start.3
  101.2 12.7 %all-to-all-done.3.a_ref = bf16[8,128,256]{2,1,0:T(8,128)(2,1)S(1)} async-done(((bf16[8,128,256]{2,1,0:T(8,128)(2,1)}), bf16[8,128,256]{2,1,0:T(8,128)(2,1)S(1)}, u32[]{:S(2)}, u32[]{:S(2)}) %all-to-all-start.3) | async-done | bytes 524320 | tf_op jit(solution)/shard_map/all_to_all | solution.py:378
  113.9 0.8 copy-done.1
  114.7 3.0 project.1
  117.6 4.9 %all-to-all-start.4 = ((bf16[4,128,512]{2,1,0:T(8,128)(2,1)}), bf16[4,128,512]{2,1,0:T(8,128)(2,1)S(1)}, u32[]{:S(2)}, u32[]{:S(2)}) async-start(bf16[4,128,512]{2,1,0:T(8,128)(2,1)} %project.1), calls=%async_computation.4 | async-start | bytes 1048576 | tf_op jit(solution)/shard_map/all_to_all | solution.py:379
  122.6 0.0 all-gather.4.cloned.1.call-start
  122.6 0.1 copy.45
  122.8 0.2 copy.46
  122.9 0.1 eq.57
  123.0 0.1 fusion.6
  123.1 0.8 copy.50.table_ref
  123.8 6.8 %all-to-all-done.4.parts_ref = bf16[4,128,512]{2,1,0:T(8,128)(2,1)S(1)} async-done(((bf16[4,128,512]{2,1,0:T(8,128)(2,1)}), bf16[4,128,512]{2,1,0:T(8,128)(2,1)S(1)}, u32[]{:S(2)}, u32[]{:S(2)}) %all-to-all-start.4) | async-done | bytes 524320 | tf_op jit(solution)/shard_map/all_to_all | solution.py:379
  130.7 0.8 copy-done.2
  131.5 2.2 dispatch.1
  133.6 13.9 %all_to_all.46 = bf16[8,64,512]{2,1,0:T(8,128)(2,1)} all-to-all(bf16[8,64,512]{2,1,0:T(8,128)(2,1)} %bitcast.48), channel_id=1, replica_groups=mesh['y'=4,'z'=8,'x'=4,'c'=2] {'x','c'}, dimensions={0} | all-to-all | bytes 1048576 | tf_op jit(solution)/shard_map/all_to_all | solution.py:382
  147.5 0.0 all-gather.4.cloned.1.call-update
  147.6 48.4 %all-gather.4.cloned.1.call-done.x_ref = bf16[8,512,512]{2,1,0:T(8,128)(2,1)} async-done(((bf16[1,512,512]{2,1,0:T(8,128)(2,1)}), bf16[8,512,512]{2,1,0:T(8,128)(2,1)}) %all-gather.4.cloned.1.call-update) | async-done | bytes 4194320 | tf_op jit(solution)/shard_map/all_gather | solution.py:385
  195.9 11.0 %experts.1 = bf16[512,4096]{1,0:T(8,128)(2,1)} custom-call(bf16[8,512,512]{2,1,0:T(8,128)(2,1)} %all-gather.4.cloned.1.call-done.x_ref, f32[1,4096]{1,0:T(1,128)} %bitcast.55, bf16[192,4096]{1,0:T(8,128)(2,1)} %bitcast.42, bf16[192,4096]{1,0:T(8,128)(2,1)} %bitcast.43, bf16[192,4096]{1,0:T(8,128)(2,1)} %bitcast.44), custom_call_target="tpu_custom_call" | custom-call | tf_op jit(solution)/shard_map/experts/pallas_call | solution.py:273
  207.0 5.1 %all-to-all-start.6 = ((bf16[8,64,4096]{2,1,0:T(8,128)(2,1)}), bf16[8,64,4096]{2,1,0:T(8,128)(2,1)}, u32[]{:S(2)}, u32[]{:S(2)}) async-start(bf16[8,64,4096]{2,1,0:T(8,128)(2,1)} %bitcast.37), calls=%async_computation.6 | async-start | bytes 8388608 | tf_op jit(solution)/shard_map/all_to_all | solution.py:387
  212.1 0.1 fusion.1
  212.2 0.1 copy.47
  212.4 0.7 fusion.table_ref
  213.0 47.4 %all-to-all-done.6 = bf16[8,64,4096]{2,1,0:T(8,128)(2,1)} async-done(((bf16[8,64,4096]{2,1,0:T(8,128)(2,1)}), bf16[8,64,4096]{2,1,0:T(8,128)(2,1)}, u32[]{:S(2)}, u32[]{:S(2)}) %all-to-all-start.6) | async-done | bytes 4194336 | tf_op jit(solution)/shard_map/all_to_all | solution.py:387
  260.5 4.6 %mix.1 = bf16[128,4096]{1,0:T(8,128)(2,1)} custom-call(bf16[128,512]{1,0:T(8,128)(2,1)} %fusion.table_ref, bf16[512,4096]{1,0:T(8,128)(2,1)} %bitcast.22.parts_ref), custom_call_target="tpu_custom_call" | custom-call | tf_op jit(solution)/shard_map/mix/pallas_call | solution.py:298
  265.0 4.3 %all-to-all-start.7 = ((bf16[4,32,4096]{2,1,0:T(8,128)(2,1)}), bf16[4,32,4096]{2,1,0:T(8,128)(2,1)S(1)}, u32[]{:S(2)}, u32[]{:S(2)}) async-start(bf16[4,32,4096]{2,1,0:T(8,128)(2,1)} %bitcast.38), calls=%async_computation.7 | async-start | bytes 2097152 | tf_op jit(solution)/shard_map/all_to_all | solution.py:396
  269.3 0.8 dynamic-slice_dynamic-update-slice_fusion
  270.1 14.1 %all-to-all-done.7 = bf16[4,32,4096]{2,1,0:T(8,128)(2,1)S(1)} async-done(((bf16[4,32,4096]{2,1,0:T(8,128)(2,1)}), bf16[4,32,4096]{2,1,0:T(8,128)(2,1)S(1)}, u32[]{:S(2)}, u32[]{:S(2)}) %all-to-all-start.7) | async-done | bytes 1048608 | tf_op jit(solution)/shard_map/all_to_all | solution.py:396
  284.2 0.2 convert_reduce_fusion
  284.4 0.1 reshape.106
  284.5 14.6 %all_to_all.47 = bf16[8,4,4096]{2,1,0:T(4,128)(2,1)S(1)} all-to-all(bf16[8,4,4096]{2,1,0:T(4,128)(2,1)S(1)} %reshape.106), channel_id=1, replica_groups=mesh['y'=4,'z'=8,'x'=4,'c'=2] {'z'}, dimensions={0} | all-to-all | bytes 524288 | tf_op jit(solution)/shard_map/all_to_all | solution.py:398
  299.1 0.7 reduce_sum.32
  (34 shorter events, 0.3 us)
Async XLA Ops:
  6.5 20.4 %copy-start = (bf16[256,4096]{1,0:T(8,128)(2,1)S(1)}, bf16[256,4096]{1,0:T(8,128)(2,1)}, u32[]{:S(2)}) copy-start(bf16[256,4096]{1,0:T(8,128)(2,1)} %param.17) | copy-start | bytes 6291460
  6.5 20.9 %copy-start.8 = (s32[1,1,256]{2,1,0:T(1,128)S(1)}, s32[1,1,256]{2,1,0:T(1,128)}, u32[]{:S(2)}) copy-start(s32[1,1,256]{2,1,0:T(1,128)} %param.15) | copy-start | bytes 3076
  8.4 20.0 %copy-start.5 = (bf16[1,4,4096]{2,1,0:T(4,128)(2,1)S(1)}, bf16[1,4,4096]{2,1,0:T(4,128)(2,1)}, u32[]{:S(2)}) copy-start(bf16[1,4,4096]{2,1,0:T(4,128)(2,1)} %param.16) | copy-start | bytes 98308
  8.4 26.1 %all-to-all-start = ((bf16[8,128,256]{2,1,0:T(8,128)(2,1)}), bf16[8,128,256]{2,1,0:T(8,128)(2,1)S(1)}, u32[]{:S(2)}, u32[]{:S(2)}) async-start(bf16[8,128,256]{2,1,0:T(8,128)(2,1)} %broadcast_in_dim.83), calls=%async_computation | async-start | bytes 1048576 | tf_op jit(solution)/shard_map/all_to_all | solution.py:329
  21.7 17.2 %collective-permute-start.1 = (bf16[2,1024,128]{2,1,0:T(8,128)(2,1)}, bf16[2,1024,128]{2,1,0:T(8,128)(2,1)}, u32[]{:S(2)}, u32[]{:S(2)}) collective-permute-start(bf16[2,1024,128]{2,1,0:T(8,128)(2,1)} %get-tuple-element.20), channel_id=1, source_target_pairs={{0,64},{64,128},{128,192},{192,0},{1,65},{65,129},{129,193},{193,1... | collective-permute-start | bytes 1572872 | tf_op jit(solution)/shard_map/ppermute | solution.py:335
  23.3 24.0 %collective-permute-start.2 = (bf16[2,1024,128]{2,1,0:T(8,128)(2,1)}, bf16[2,1024,128]{2,1,0:T(8,128)(2,1)}, u32[]{:S(2)}, u32[]{:S(2)}) collective-permute-start(bf16[2,1024,128]{2,1,0:T(8,128)(2,1)} %get-tuple-element.21), channel_id=1, source_target_pairs={{0,192},{64,0},{128,64},{192,128},{1,193},{65,1},{129,65},{193,129... | collective-permute-start | bytes 1572872 | tf_op jit(solution)/shard_map/ppermute | solution.py:335
  24.9 38.4 %collective-permute-start = (bf16[2,1024,128]{2,1,0:T(8,128)(2,1)}, bf16[2,1024,128]{2,1,0:T(8,128)(2,1)}, u32[]{:S(2)}, u32[]{:S(2)}) collective-permute-start(bf16[2,1024,128]{2,1,0:T(8,128)(2,1)} %get-tuple-element.18), channel_id=1, source_target_pairs={{0,128},{64,192},{128,0},{192,64},{1,129},{65,193},{129,1},{193,65... | collective-permute-start | bytes 1572872 | tf_op jit(solution)/shard_map/ppermute | solution.py:335
  34.5 13.5 %copy-start.4 = (bf16[8,128,256]{2,1,0:T(8,128)(2,1)}, bf16[8,128,256]{2,1,0:T(8,128)(2,1)S(1)}, u32[]{:S(2)}) copy-start(bf16[8,128,256]{2,1,0:T(8,128)(2,1)S(1)} %all-to-all-done.q_ref) | copy-start | bytes 1572868
  35.4 37.9 %all-to-all-start.1 = ((bf16[8,36,512]{2,1,0:T(8,128)(2,1)}), bf16[8,36,512]{2,1,0:T(8,128)(2,1)S(1)}, u32[]{:S(2)}, u32[]{:S(2)}) async-start(bf16[8,36,512]{2,1,0:T(8,128)(2,1)} %copy.49), calls=%async_computation.1 | async-start | bytes 655360 | tf_op jit(solution)/shard_map/all_to_all | solution.py:356
  38.8 75.0 %all-gather.6.cloned.1.call-start = ((), (), s32[]{:S(2)}) async-start(), calls=%async_computation.10 | async-start | bytes 2359296 | tf_op jit(solution)/shard_map/all_gather | solution.py:376
  73.3 27.3 %copy-start.6 = (s32[1,128,8]{1,2,0:T(8,128)S(1)}, s32[1,128,8]{1,2,0:T(8,128)}, u32[]{:S(2)}) copy-start(s32[1,128,8]{1,2,0:T(8,128)} %param.19) | copy-start | bytes 12292
  97.2 16.7 %all-to-all-start.3 = ((bf16[8,128,256]{2,1,0:T(8,128)(2,1)}), bf16[8,128,256]{2,1,0:T(8,128)(2,1)S(1)}, u32[]{:S(2)}, u32[]{:S(2)}) async-start(bf16[8,128,256]{2,1,0:T(8,128)(2,1)} %combine.1), calls=%async_computation.3 | async-start | bytes 1048576 | tf_op jit(solution)/shard_map/all_to_all | solution.py:378
  101.1 12.7 %copy-start.3 = (bf16[128,512]{1,0:T(8,128)(2,1)}, bf16[128,512]{1,0:T(8,128)(2,1)S(1)}, u32[]{:S(2)}) copy-start(bf16[128,512]{1,0:T(8,128)(2,1)S(1)} %constant_dynamic-update-slice_fusion.resid_ref) | copy-start | bytes 393220
  113.9 0.8 copy-start.1
  117.6 13.0 %all-to-all-start.4 = ((bf16[4,128,512]{2,1,0:T(8,128)(2,1)}), bf16[4,128,512]{2,1,0:T(8,128)(2,1)S(1)}, u32[]{:S(2)}, u32[]{:S(2)}) async-start(bf16[4,128,512]{2,1,0:T(8,128)(2,1)} %project.1), calls=%async_computation.4 | async-start | bytes 1048576 | tf_op jit(solution)/shard_map/all_to_all | solution.py:379
  122.6 73.4 %all-gather.4.cloned.1.call-start = ((), (), s32[]{:S(2)}) async-start(), calls=%async_computation.9 | async-start | bytes 4718592 | tf_op jit(solution)/shard_map/all_gather | solution.py:385
  130.7 0.8 copy-start.2
  207.0 5.1 %copy-start.7 = (f32[1,128,8]{1,2,0:T(8,128)S(1)}, f32[1,128,8]{1,2,0:T(8,128)}, u32[]{:S(2)}) copy-start(f32[1,128,8]{1,2,0:T(8,128)} %param.20) | copy-start | bytes 12292
  207.0 53.5 %all-to-all-start.6 = ((bf16[8,64,4096]{2,1,0:T(8,128)(2,1)}), bf16[8,64,4096]{2,1,0:T(8,128)(2,1)}, u32[]{:S(2)}, u32[]{:S(2)}) async-start(bf16[8,64,4096]{2,1,0:T(8,128)(2,1)} %bitcast.37), calls=%async_computation.6 | async-start | bytes 8388608 | tf_op jit(solution)/shard_map/all_to_all | solution.py:387
  265.0 19.2 %all-to-all-start.7 = ((bf16[4,32,4096]{2,1,0:T(8,128)(2,1)}), bf16[4,32,4096]{2,1,0:T(8,128)(2,1)S(1)}, u32[]{:S(2)}, u32[]{:S(2)}) async-start(bf16[4,32,4096]{2,1,0:T(8,128)(2,1)} %bitcast.38), calls=%async_computation.7 | async-start | bytes 2097152 | tf_op jit(solution)/shard_map/all_to_all | solution.py:396
Sparse Core Ops, SparseCore 0:
  74.2 28.3 all-gather.5
  147.7 48.1 all-gather.3

commit v3 on v2

--- a/solution.py
+++ b/solution.py
@@ -19,6 +19,7 @@
 WIN = 128
 D = 4096
 COLS = D // N_Z
+HALF = COLS // 2
 CTX_LOCAL = 1024
 HIDDEN = 192
 STAT_ROWS = 16
@@ -242,7 +243,7 @@
     )(parts, table)
 
 
-def experts_kernel(x_ref, gain_ref, wg_ref, wu_ref, wd_ref, out_ref):
+def experts_kernel(x_ref, gain_ref, wg_ref, wu_ref, wd_ref, by_z_ref, by_x_ref):
     tokens = x_ref.shape[1]
     squares = jnp.zeros((tokens, COLS), f32)
     for z in range(N_Z):
@@ -262,9 +263,9 @@
     hidden = (gate / (1.0 + jnp.exp(-gate)) * up).astype(bf16)
     for z in range(N_Z):
         cols = slice(z * COLS, (z + 1) * COLS)
-        out_ref[:, cols] = jnp.dot(
-            hidden, wd_ref[:, cols], preferred_element_type=f32
-        ).astype(bf16)
+        done = jnp.dot(hidden, wd_ref[:, cols], preferred_element_type=f32).astype(bf16)
+        by_z_ref[z] = done[:, :HALF]
+        by_x_ref[:, z * HALF : (z + 1) * HALF] = done[:, HALF:]
 
 
 def experts(x, gain, w_gate, w_up, w_down, tile=128):
@@ -280,8 +281,14 @@
             whole,
             whole,
         ],
-        out_specs=pl.BlockSpec((tile, D), lambda i: (i, 0)),
-        out_shape=jax.ShapeDtypeStruct((tokens, D), bf16),
+        out_specs=[
+            pl.BlockSpec((N_Z, tile, HALF), lambda i: (0, i, 0)),
+            pl.BlockSpec((tile, D // 2), lambda i: (i, 0)),
+        ],
+        out_shape=[
+            jax.ShapeDtypeStruct((N_Z, tokens, HALF), bf16),
+            jax.ShapeDtypeStruct((tokens, D // 2), bf16),
+        ],
         compiler_params=params(),
         name="experts",
     )(x, gain, w_gate, w_up, w_down)
@@ -294,19 +301,57 @@
 
 
 def mix(table, parts):
-    tile = 1024
+    tile = 512
     return pl.pallas_call(
         mix_kernel,
-        grid=(D // tile,),
+        grid=(parts.shape[1] // tile,),
         in_specs=[
             pl.BlockSpec(table.shape, lambda i: (0, 0)),
             pl.BlockSpec((parts.shape[0], tile), lambda i: (0, i)),
         ],
         out_specs=pl.BlockSpec((WIN, tile), lambda i: (0, i)),
-        out_shape=jax.ShapeDtypeStruct((WIN, D), bf16),
-        compiler_params=params(),
+        out_shape=jax.ShapeDtypeStruct((WIN, parts.shape[1]), bf16),
+        compiler_params=params(),
+        cost_estimate=pl.CostEstimate(flops=1 << 28, bytes_accessed=4 << 20, transcendentals=0),
         name="mix",
     )(table, parts)
+
+
+def mix_rest_kernel(table_ref, parts_ref, mixed_ref, out_ref):
+    out_ref[:, : D // 2] = mixed_ref[...]
+    out_ref[:, D // 2 :] = jnp.dot(
+        table_ref[...], parts_ref[...], preferred_element_type=f32
+    ).astype(bf16)
+
+
+def mix_rest(table, parts, mixed):
+    return pl.pallas_call(
+        mix_rest_kernel,
+        out_shape=jax.ShapeDtypeStruct((WIN, D // 2 + HALF), bf16),
+        compiler_params=params(),
+        name="mix_rest",
+    )(table, parts, mixed)
+
+
+def finish_kernel(in_ref, out_ref):
+    summed = in_ref[0, :, : D // 2].astype(f32)
+    for z in range(1, N_Z):
+        summed = summed + in_ref[z, :, : D // 2].astype(f32)
+    for z in range(N_Z):
+        mine = in_ref[z, :, D // 2 :].astype(f32)
+        first = mine[:, HALF : 2 * HALF] + mine[:, :HALF]
+        second = mine[:, 2 * HALF :] + summed[:, z * HALF : (z + 1) * HALF]
+        out_ref[:, z * COLS : z * COLS + HALF] = first.astype(bf16)
+        out_ref[:, z * COLS + HALF : (z + 1) * COLS] = second.astype(bf16)
+
+
+def finish(parts):
+    return pl.pallas_call(
+        finish_kernel,
+        out_shape=jax.ShapeDtypeStruct((parts.shape[1], D), bf16),
+        compiler_params=params(),
+        name="finish",
+    )(parts)
 
 
 def per_device(
@@ -326,11 +371,11 @@
     y_pos = lax.axis_index("y")
     z_pos = lax.axis_index("z")
 
+    chunks = dequantize(y_pos[None], kv_scale[0], kv_cache[0])
+    kv_own, queries = lax.optimization_barrier((chunks[0], queries))
     queries_mine = lax.all_to_all(
         jnp.broadcast_to(queries, (N_Z,) + queries.shape[1:]), "z", 0, 0, tiled=True
     )
-    chunks = dequantize(y_pos[None], kv_scale[0], kv_cache[0])
-    kv_own = chunks[0]
     kv_from = {
         d: lax.ppermute(chunks[d], "y", [(i, (i + d) % N_Y) for i in range(N_Y)])
         for d in (1, 3, 2)
@@ -383,20 +428,25 @@
         outgoing.reshape(N_GRP, CAP, COLS), ("x", "c"), 0, 0, tiled=True
     ).reshape(N_GRP * CAP, COLS)
     arrivals = lax.all_gather(arrivals, "z", axis=0, tiled=False)
-    pieces = experts(arrivals, norm_gain[None], w_gate[0], w_up[0], w_down[0])
-    returned = lax.all_to_all(
-        pieces.reshape(N_GRP, CAP, D), ("x", "c"), 0, 0, tiled=True
-    ).reshape(N_GRP * CAP, D)
-    mixture = mix(back_table, returned).reshape(N_Y, rows, D)
+    by_z, by_x = experts(arrivals, norm_gain[None], w_gate[0], w_up[0], w_down[0])
+    by_z = lax.psum_scatter(
+        by_z.reshape(N_Z * N_GRP * CAP, HALF), "z", scatter_dimension=0, tiled=True
+    )
+    by_x = lax.all_to_all(
+        by_x.reshape(N_GRP, CAP, D // 2), ("x", "c"), 0, 0, tiled=True
+    ).reshape(N_GRP * CAP, D // 2)
+    mixed = mix(back_table, by_x)
+    by_z, by_x = lax.optimization_barrier((by_z, by_x))
+    by_z = lax.all_to_all(
+        by_z.reshape(N_GRP, CAP, HALF), ("x", "c"), 0, 0, tiled=True
+    ).reshape(N_GRP * CAP, HALF)
+    mixture = mix_rest(back_table, by_z, mixed).reshape(N_Y, rows, -1)
 
     stream_rows = lax.dynamic_slice_in_dim(stream, y_pos * rows, rows, 0)
-    stream_rows = lax.dynamic_update_slice_in_dim(
-        jnp.zeros((rows, D), bf16), stream_rows, z_pos * COLS, 1
-    )
     mixture = lax.all_to_all(mixture, "y", 0, 0, tiled=True)
-    mixture = jnp.sum(mixture.astype(f32), axis=0) + stream_rows.astype(f32)
-    mixture = lax.all_to_all(mixture.astype(bf16).reshape(N_Z, -1, D), "z", 0, 0, tiled=True)
-    return jnp.sum(mixture.astype(f32), axis=0).astype(bf16)[None]
+    mixture = jnp.sum(mixture.astype(f32), axis=0).astype(bf16)
+    tail = jnp.concatenate([mixture, stream_rows], axis=1).reshape(N_Z, own_rows, -1)
+    return finish(lax.all_to_all(tail, "z", 0, 0, tiled=True))[None]
 
 
 def solution(mesh):

time: 308 us -> 307 us (level)
  waiting for transfers between devices: 143 us -> 104 us
  blocking collectives: 49.2 us -> 84.2 us
  Pallas kernels: 53.3 us -> 56.5 us
    all_to_all x1, waiting for transfers between devices: 47.4 us -> 2.13 us  [per_device(): lax.all_to_all(by_z.reshape(N_GRP, CAP, HALF), ('x', 'c'), 0, 0, tiled=True)]
    all_to_all x1 -> x2, blocking collectives: 14.6 us -> 45.2 us  [the longest x1 31 us: per_device(): lax.all_to_all(by_x.reshape(N_GRP, CAP, D // 2), ('x', 'c'), 0, 0, tiled=...]
    reduce_scatter x0 -> x1, waiting for transfers between devices: none -> 9.68 us  [per_device(): lax.psum_scatter(by_z.reshape(N_Z * N_GRP * CAP, HALF), 'z', scatter_dime...]
    all_to_all x1, waiting for transfers between devices: 14.1 us -> 9.05 us  [per_device(): mixture = lax.all_to_all(mixture, 'y', 0, 0, tiled=True)]
    all_to_all x1, blocking collectives: 20.7 us -> 25 us  [per_device(): parts = lax.all_to_all(parts, 'z', 0, 0, tiled=True)]
    all_to_all x1, waiting for transfers between devices: 4.77 us -> 8.38 us  [per_device(): lax.all_to_all(jnp.broadcast_to(queries, (N_Z,) + queries.shape[1:]), 'z'...]
    ppermute x3, waiting for transfers between devices: 8.36 us -> 4.93 us  [per_device(): lax.ppermute(chunks[d], 'y', [(i, (i + d) % N_Y) for i in range(N_Y)])]
    pallas_call x1 -> x3, Pallas kernels: 4.57 us -> 7.71 us  [the longest x1 3.95 us: mix(): pl.pallas_call(mix_kernel, grid=(parts.shape[1] // tile,), in_specs=[pl.B...]
  transfers between devices with their start and end apart: 11 -> 12, of which waited for: 7 -> 9; matrix products, arithmetic and copies ran while one was open for 3% -> 2% of each run, Pallas kernels for 11% -> 10%
where the time goes in v3:
time: 307 us; the launch traced here: 305 us
  waiting for transfers between devices  104 us (34%)
  blocking collectives  84.2 us (27%)
  Pallas kernels  56.5 us (18%)
  starting transfers between devices  36.2 us (12%)
  between operations  13.3 us (4%)
  local copies, waits for them, and re-layouts  8.9 us (3%)
    all_gather x1, waiting for transfers between devices, per_device(): arrivals = lax.all_gather(arrivals, 'z', axis=0, tiled=False)  48.6 us
    all_to_all x1, blocking collectives, per_device(): lax.all_to_all(by_x.reshape(N_GRP, CAP, D // 2), ('x', 'c'), 0, 0, tiled=...  31 us
    all_to_all x1, blocking collectives, per_device(): parts = lax.all_to_all(parts, 'z', 0, 0, tiled=True)  25 us
    pallas_call x1, Pallas kernels, near_attention(): pl.pallas_call(near_kernel, grid_spec=attention_specs([], [square, square...  15.4 us
    all_to_all x1, waiting for transfers between devices, per_device(): attended = lax.all_to_all(combine(parts), 'z', 0, 0, tiled=True)  14.5 us
    all_to_all x1, blocking collectives, per_device(): return finish(lax.all_to_all(tail, 'z', 0, 0, tiled=True))[None]  14.2 us
    all_to_all x1, blocking collectives, per_device(): lax.all_to_all(outgoing.reshape(N_GRP, CAP, COLS), ('x', 'c'), 0, 0, tile...  13.9 us
    pallas_call x1, Pallas kernels, experts(): pl.pallas_call(experts_kernel, grid=(tokens // tile,), in_specs=[pl.Block...  11.1 us
  transfers between devices with their start and end apart: 12, of which 9 were waited for; matrix products, arithmetic and copies ran while one was open for 2% of the time, Pallas kernels for 10%

profile of v3, /device:TPU:2, one launch (start us, length us, event | category | flops | bytes accessed | tf_op | source)
XLA Modules:
  0.0 305.4 jit_solution(13038373758459839189)
XLA Ops:
  6.5 4.9 %dequantize.1 = (bf16[2,1024,128]{2,1,0:T(8,128)(2,1)}, bf16[2,1024,128]{2,1,0:T(8,128)(2,1)}, bf16[2,1024,128]{2,1,0:T(8,128)(2,1)}, bf16[2,1024,128]{2,1,0:T(8,128)(2,1)}) custom-call(s32[1]{0:T(128)} %bitcast.7.y_ref, f32[8,8]{1,0:T(8,128)} %bitcast.67, bf16[1024,1024]{1,0:T(8,128)(2,1)} %bitcast.42), custom_call_target="tpu_custom_call" | custom-call | flops 1048576 | bytes 4194304 | tf_op jit(solution)/shard_map/dequantize/pallas_call | solution.py:53
  11.4 0.8 broadcast_in_dim.81
  12.2 8.5 %all-to-all-start = ((bf16[8,128,256]{2,1,0:T(8,128)(2,1)}), bf16[8,128,256]{2,1,0:T(8,128)(2,1)S(1)}, u32[]{:S(2)}, u32[]{:S(2)}) async-start(bf16[8,128,256]{2,1,0:T(8,128)(2,1)} %broadcast_in_dim.81), calls=%async_computation | async-start | bytes 1048576 | tf_op jit(solution)/shard_map/all_to_all | solution.py:376
  20.7 3.2 %collective-permute-start = (bf16[2,1024,128]{2,1,0:T(8,128)(2,1)}, bf16[2,1024,128]{2,1,0:T(8,128)(2,1)}, u32[]{:S(2)}, u32[]{:S(2)}) collective-permute-start(bf16[2,1024,128]{2,1,0:T(8,128)(2,1)} %get-tuple-element.25), channel_id=1, source_target_pairs={{0,128},{64,192},{128,0},{192,64},{1,129},{65,193},{129,1},{193,65... | collective-permute-start | bytes 1572872 | tf_op jit(solution)/shard_map/ppermute | solution.py:380
  23.9 0.7 collective-permute-start.1
  24.6 2.6 collective-permute-start.2
  27.2 0.1 copy.52
  27.3 0.5 broadcast.144
  27.8 0.7 reduce.4
  28.5 0.1 reshape_squeeze.3
  28.6 0.6 gather_fusion
  29.2 0.5 and_convert_fusion.last_ref
  29.7 0.1 fusion.2
  29.8 8.4 %all-to-all-done.q_ref = bf16[8,128,256]{2,1,0:T(8,128)(2,1)S(1)} async-done(((bf16[8,128,256]{2,1,0:T(8,128)(2,1)}), bf16[8,128,256]{2,1,0:T(8,128)(2,1)S(1)}, u32[]{:S(2)}, u32[]{:S(2)}) %all-to-all-start) | async-done | bytes 524320 | tf_op jit(solution)/shard_map/all_to_all | solution.py:376
  38.2 0.9 copy.49
  39.1 3.4 %all-to-all-start.1 = ((bf16[8,36,512]{2,1,0:T(8,128)(2,1)}), bf16[8,36,512]{2,1,0:T(8,128)(2,1)S(1)}, u32[]{:S(2)}, u32[]{:S(2)}) async-start(bf16[8,36,512]{2,1,0:T(8,128)(2,1)} %copy.49), calls=%async_computation.1 | async-start | bytes 655360 | tf_op jit(solution)/shard_map/all_to_all | solution.py:401
  42.6 0.0 all-gather.6.cloned.1.call-start
  42.6 4.5 %collective-permute-done.1.kv1 = bf16[2,1024,128]{2,1,0:T(8,128)(2,1)} collective-permute-done((bf16[2,1024,128]{2,1,0:T(8,128)(2,1)}, bf16[2,1024,128]{2,1,0:T(8,128)(2,1)}, u32[]{:S(2)}, u32[]{:S(2)}) %collective-permute-start.1) | collective-permute-done | bytes 524320 | tf_op jit(solution)/shard_map/ppermute | solution.py:380
  47.1 0.4 collective-permute-done.2.kv3
  47.5 0.7 broadcast_in_dim.86
  48.2 15.4 %near_attention.1 = (f32[8,256,128]{2,1,0:T(8,128)}, f32[8,256,128]{2,1,0:T(8,128)}) custom-call(s32[4]{0:T(128)} %and_convert_fusion.last_ref, bf16[8,128,256]{2,1,0:T(8,128)(2,1)} %copy-done.5, f32[4,1,1024]{2,1,0:T(1,128)} %bitcast.63, bf16[2,1024,128]{2,1,0:T(8,128)(2,1)} %get-tuple-element.26.kv0, bf16[2,1024,128]{2,1,0:T(8,128)(2,1)} %collective-permute-done.1.kv1, ...), custom_call_target="tpu_custom_call" | custom-call | flops 8589934592 | bytes 8388608 | tf_op jit(solution)/shard_map/near_attention/pallas_call | solution.py:151
  63.6 0.0 collective-permute-done.kv2
  63.6 10.0 %far_attention.1 = bf16[8,272,128]{2,1,0:T(8,128)(2,1)} custom-call(s32[4]{0:T(128)} %and_convert_fusion.last_ref, bf16[8,128,256]{2,1,0:T(8,128)(2,1)} %copy-done.5, f32[4,1,1024]{2,1,0:T(1,128)} %bitcast.64, bf16[2,1024,128]{2,1,0:T(8,128)(2,1)} %collective-permute-done.kv2, f32[8,256,128]{2,1,0:T(8,128)} %get-tuple-element.29.acc_ref, ...), custom_call_target="tpu_custom_call" | custom-call | flops 3221225472 | bytes 8388608 | tf_op jit(solution)/shard_map/far_attention/pallas_call | solution.py:166
  73.6 0.0 all-to-all-done.1
  73.6 0.7 slice.6
  74.3 0.0 all-gather.6.cloned.1.call-update
  74.4 25.0 %all_to_all.50.in_ref = bf16[8,272,128]{2,1,0:T(8,128)(2,1)} all-to-all(bf16[8,272,128]{2,1,0:T(8,128)(2,1)} %far_attention.1), channel_id=1, replica_groups=mesh['y'=4,'z'=8,'x'=4,'c'=2] {'z'}, dimensions={0} | all-to-all | bytes 1114112 | tf_op jit(solution)/shard_map/all_to_all | solution.py:422
  99.4 2.4 combine.1
  101.8 3.5 %all-to-all-start.3 = ((bf16[8,128,256]{2,1,0:T(8,128)(2,1)}), bf16[8,128,256]{2,1,0:T(8,128)(2,1)S(1)}, u32[]{:S(2)}, u32[]{:S(2)}) async-start(bf16[8,128,256]{2,1,0:T(8,128)(2,1)} %combine.1), calls=%async_computation.3 | async-start | bytes 1048576 | tf_op jit(solution)/shard_map/all_to_all | solution.py:423
  105.3 0.1 fusion.1
  105.4 0.1 copy.47
  105.5 0.1 compare_reduce_fusion
  105.7 0.2 copy.46
  105.8 0.3 reduce_window_sum.11
  106.2 14.5 %all-to-all-done.3.a_ref = bf16[8,128,256]{2,1,0:T(8,128)(2,1)S(1)} async-done(((bf16[8,128,256]{2,1,0:T(8,128)(2,1)}), bf16[8,128,256]{2,1,0:T(8,128)(2,1)S(1)}, u32[]{:S(2)}, u32[]{:S(2)}) %all-to-all-start.3) | async-done | bytes 524320 | tf_op jit(solution)/shard_map/all_to_all | solution.py:423
  120.7 0.8 copy-done.1
  121.5 2.9 project.1
  124.4 5.2 %all-to-all-start.4 = ((bf16[4,128,512]{2,1,0:T(8,128)(2,1)}), bf16[4,128,512]{2,1,0:T(8,128)(2,1)S(1)}, u32[]{:S(2)}, u32[]{:S(2)}) async-start(bf16[4,128,512]{2,1,0:T(8,128)(2,1)} %project.1), calls=%async_computation.4 | async-start | bytes 1048576 | tf_op jit(solution)/shard_map/all_to_all | solution.py:424
  129.6 0.1 copy.45
  129.8 0.1 eq.57
  129.8 0.7 fusion
  130.6 0.8 copy.50.table_ref
  131.4 6.3 %all-to-all-done.4.parts_ref = bf16[4,128,512]{2,1,0:T(8,128)(2,1)S(1)} async-done(((bf16[4,128,512]{2,1,0:T(8,128)(2,1)}), bf16[4,128,512]{2,1,0:T(8,128)(2,1)S(1)}, u32[]{:S(2)}, u32[]{:S(2)}) %all-to-all-start.4) | async-done | bytes 524320 | tf_op jit(solution)/shard_map/all_to_all | solution.py:424
  137.7 0.8 copy-done.2
  138.5 2.2 dispatch.1
  140.7 13.9 %all_to_all.51 = bf16[8,64,512]{2,1,0:T(8,128)(2,1)} all-to-all(bf16[8,64,512]{2,1,0:T(8,128)(2,1)} %bitcast.54), channel_id=1, replica_groups=mesh['y'=4,'z'=8,'x'=4,'c'=2] {'x','c'}, dimensions={0} | all-to-all | bytes 1048576 | tf_op jit(solution)/shard_map/all_to_all | solution.py:427
  154.6 0.0 all-gather.4.cloned.1.call-update
  154.6 0.0 reduce-scatter.2.cloned.1.call-start
  154.7 48.6 %all-gather.4.cloned.1.call-done.x_ref = bf16[8,512,512]{2,1,0:T(8,128)(2,1)} async-done(((bf16[1,512,512]{2,1,0:T(8,128)(2,1)}), bf16[8,512,512]{2,1,0:T(8,128)(2,1)}) %all-gather.4.cloned.1.call-update) | async-done | bytes 4194320 | tf_op jit(solution)/shard_map/all_gather | solution.py:430
  203.3 11.1 %experts.1 = (bf16[8,512,256]{2,1,0:T(8,128)(2,1)}, bf16[512,2048]{1,0:T(8,128)(2,1)}) custom-call(bf16[8,512,512]{2,1,0:T(8,128)(2,1)} %all-gather.4.cloned.1.call-done.x_ref, f32[1,4096]{1,0:T(1,128)} %bitcast.62, bf16[192,4096]{1,0:T(8,128)(2,1)} %bitcast.47, bf16[192,4096]{1,0:T(8,128)(2,1)} %bitcast.48, bf16[192,4096]{1,0:T(8,128)(2,1)} %bitcast.49), custom_call_target="tpu_custom_call" | custom-call | tf_op jit(solution)/shard_map/experts/pallas_call | solution.py:274
  214.3 0.0 reduce-scatter.2.cloned.1.call-update
  214.4 31.0 %all_to_all.52 = bf16[8,64,2048]{2,1,0:T(8,128)(2,1)} all-to-all(bf16[8,64,2048]{2,1,0:T(8,128)(2,1)} %bitcast.44), channel_id=1, replica_groups=mesh['y'=4,'z'=8,'x'=4,'c'=2] {'x','c'}, dimensions={0} | all-to-all | bytes 4194304 | tf_op jit(solution)/shard_map/all_to_all | solution.py:435
  245.3 9.7 %reduce-scatter.2.cloned.1.call-done = bf16[512,256]{1,0:T(8,128)(2,1)} async-done(((bf16[4096,256]{1,0:T(8,128)(2,1)}), bf16[512,256]{1,0:T(8,128)(2,1)}) %reduce-scatter.2.cloned.1.call-update) | async-done | bytes 262160 | tf_op jit(solution)/shard_map/reduce_scatter | solution.py:432
  255.0 4.8 %all-to-all-start.7 = ((bf16[8,64,256]{2,1,0:T(8,128)(2,1)}), bf16[8,64,256]{2,1,0:T(8,128)(2,1)S(1)}, u32[]{:S(2)}, u32[]{:S(2)}) async-start(bf16[8,64,256]{2,1,0:T(8,128)(2,1)} %bitcast.56), calls=%async_computation.8 | async-start | bytes 524288 | tf_op jit(solution)/shard_map/all_to_all | solution.py:440
  259.8 4.0 %mix.1.mixed_ref = bf16[128,2048]{1,0:T(8,128)(2,1)} custom-call(bf16[128,512]{1,0:T(8,128)(2,1)} %get-tuple-element.39.table_ref, bf16[512,2048]{1,0:T(8,128)(2,1)} %bitcast.40), custom_call_target="tpu_custom_call" | custom-call | flops 268435456 | bytes 4194304 | tf_op jit(solution)/shard_map/mix/pallas_call | solution.py:305
  263.8 2.1 all-to-all-done.7
  265.9 0.7 copy-done.3
  266.6 2.2 mix_rest.1
  268.8 4.3 %all-to-all-start.8 = ((bf16[4,32,2304]{2,1,0:T(8,128)(2,1)}), bf16[4,32,2304]{2,1,0:T(8,128)(2,1)S(1)}, u32[]{:S(2)}, u32[]{:S(2)}) async-start(bf16[4,32,2304]{2,1,0:T(8,128)(2,1)} %bitcast.41), calls=%async_computation.9 | async-start | bytes 1179648 | tf_op jit(solution)/shard_map/all_to_all | solution.py:446
  273.1 0.8 constant_dynamic-slice_fusion
  273.9 9.1 %all-to-all-done.8 = bf16[4,32,2304]{2,1,0:T(8,128)(2,1)S(1)} async-done(((bf16[4,32,2304]{2,1,0:T(8,128)(2,1)}), bf16[4,32,2304]{2,1,0:T(8,128)(2,1)S(1)}, u32[]{:S(2)}, u32[]{:S(2)}) %all-to-all-start.8) | async-done | bytes 589856 | tf_op jit(solution)/shard_map/all_to_all | solution.py:446
  282.9 0.1 reduce_sum.22
  283.1 14.2 %all_to_all.53.in_ref = bf16[8,4,2816]{2,1,0:T(4,128)(2,1)} all-to-all(bf16[8,4,2816]{2,1,0:T(4,128)(2,1)S(1)} %reshape.118), channel_id=1, replica_groups=mesh['y'=4,'z'=8,'x'=4,'c'=2] {'z'}, dimensions={0} | all-to-all | bytes 360448 | tf_op jit(solution)/shard_map/all_to_all | solution.py:449
  297.3 1.6 finish.1
  (42 shorter events, 0.3 us)
Async XLA Ops:
  6.5 20.6 %copy-start = (bf16[256,4096]{1,0:T(8,128)(2,1)S(1)}, bf16[256,4096]{1,0:T(8,128)(2,1)}, u32[]{:S(2)}) copy-start(bf16[256,4096]{1,0:T(8,128)(2,1)} %param.17) | copy-start | bytes 6291460
  6.5 4.9 %copy-start.6 = (bf16[1,128,256]{2,1,0:T(8,128)(2,1)S(1)}, bf16[1,128,256]{2,1,0:T(8,128)(2,1)}, u32[]{:S(2)}) copy-start(bf16[1,128,256]{2,1,0:T(8,128)(2,1)} %param.12) | copy-start | bytes 196612
  6.5 20.6 %copy-start.7 = (bf16[1,4,4096]{2,1,0:T(4,128)(2,1)S(1)}, bf16[1,4,4096]{2,1,0:T(4,128)(2,1)}, u32[]{:S(2)}) copy-start(bf16[1,4,4096]{2,1,0:T(4,128)(2,1)} %param.16) | copy-start | bytes 98308
  6.5 21.3 %copy-start.10 = (s32[1,1,256]{2,1,0:T(1,128)S(1)}, s32[1,1,256]{2,1,0:T(1,128)}, u32[]{:S(2)}) copy-start(s32[1,1,256]{2,1,0:T(1,128)} %param.15) | copy-start | bytes 3076
  12.2 26.0 %all-to-all-start = ((bf16[8,128,256]{2,1,0:T(8,128)(2,1)}), bf16[8,128,256]{2,1,0:T(8,128)(2,1)S(1)}, u32[]{:S(2)}, u32[]{:S(2)}) async-start(bf16[8,128,256]{2,1,0:T(8,128)(2,1)} %broadcast_in_dim.81), calls=%async_computation | async-start | bytes 1048576 | tf_op jit(solution)/shard_map/all_to_all | solution.py:376
  20.7 42.9 %collective-permute-start = (bf16[2,1024,128]{2,1,0:T(8,128)(2,1)}, bf16[2,1024,128]{2,1,0:T(8,128)(2,1)}, u32[]{:S(2)}, u32[]{:S(2)}) collective-permute-start(bf16[2,1024,128]{2,1,0:T(8,128)(2,1)} %get-tuple-element.25), channel_id=1, source_target_pairs={{0,128},{64,192},{128,0},{192,64},{1,129},{65,193},{129,1},{193,65... | collective-permute-start | bytes 1572872 | tf_op jit(solution)/shard_map/ppermute | solution.py:380
  23.9 23.2 %collective-permute-start.1 = (bf16[2,1024,128]{2,1,0:T(8,128)(2,1)}, bf16[2,1024,128]{2,1,0:T(8,128)(2,1)}, u32[]{:S(2)}, u32[]{:S(2)}) collective-permute-start(bf16[2,1024,128]{2,1,0:T(8,128)(2,1)} %get-tuple-element.27), channel_id=1, source_target_pairs={{0,64},{64,128},{128,192},{192,0},{1,65},{65,129},{129,193},{193,1... | collective-permute-start | bytes 1572872 | tf_op jit(solution)/shard_map/ppermute | solution.py:380
  24.6 23.0 %collective-permute-start.2 = (bf16[2,1024,128]{2,1,0:T(8,128)(2,1)}, bf16[2,1024,128]{2,1,0:T(8,128)(2,1)}, u32[]{:S(2)}, u32[]{:S(2)}) collective-permute-start(bf16[2,1024,128]{2,1,0:T(8,128)(2,1)} %get-tuple-element.28), channel_id=1, source_target_pairs={{0,192},{64,0},{128,64},{192,128},{1,193},{65,1},{129,65},{193,129... | collective-permute-start | bytes 1572872 | tf_op jit(solution)/shard_map/ppermute | solution.py:380
  38.2 10.0 %copy-start.5 = (bf16[8,128,256]{2,1,0:T(8,128)(2,1)}, bf16[8,128,256]{2,1,0:T(8,128)(2,1)S(1)}, u32[]{:S(2)}) copy-start(bf16[8,128,256]{2,1,0:T(8,128)(2,1)S(1)} %all-to-all-done.q_ref) | copy-start | bytes 1572868
  39.1 34.5 %all-to-all-start.1 = ((bf16[8,36,512]{2,1,0:T(8,128)(2,1)}), bf16[8,36,512]{2,1,0:T(8,128)(2,1)S(1)}, u32[]{:S(2)}, u32[]{:S(2)}) async-start(bf16[8,36,512]{2,1,0:T(8,128)(2,1)} %copy.49), calls=%async_computation.1 | async-start | bytes 655360 | tf_op jit(solution)/shard_map/all_to_all | solution.py:401
  42.6 78.2 %all-gather.6.cloned.1.call-start = ((), (), s32[]{:S(2)}) async-start(), calls=%async_computation.13 | async-start | bytes 2359296 | tf_op jit(solution)/shard_map/all_gather | solution.py:421
  73.6 31.7 %copy-start.8 = (s32[1,128,8]{1,2,0:T(8,128)S(1)}, s32[1,128,8]{1,2,0:T(8,128)}, u32[]{:S(2)}) copy-start(s32[1,128,8]{1,2,0:T(8,128)} %param.19) | copy-start | bytes 12292
  73.6 31.7 %copy-start.9 = (f32[1,128,8]{1,2,0:T(8,128)S(1)}, f32[1,128,8]{1,2,0:T(8,128)}, u32[]{:S(2)}) copy-start(f32[1,128,8]{1,2,0:T(8,128)} %param.20) | copy-start | bytes 12292
  101.8 19.0 %all-to-all-start.3 = ((bf16[8,128,256]{2,1,0:T(8,128)(2,1)}), bf16[8,128,256]{2,1,0:T(8,128)(2,1)S(1)}, u32[]{:S(2)}, u32[]{:S(2)}) async-start(bf16[8,128,256]{2,1,0:T(8,128)(2,1)} %combine.1), calls=%async_computation.3 | async-start | bytes 1048576 | tf_op jit(solution)/shard_map/all_to_all | solution.py:423
  106.2 14.5 %copy-start.4 = (bf16[128,512]{1,0:T(8,128)(2,1)}, bf16[128,512]{1,0:T(8,128)(2,1)S(1)}, u32[]{:S(2)}) copy-start(bf16[128,512]{1,0:T(8,128)(2,1)S(1)} %constant_dynamic-update-slice_fusion.resid_ref) | copy-start | bytes 393220
  120.7 0.8 copy-start.1
  124.4 13.2 %all-to-all-start.4 = ((bf16[4,128,512]{2,1,0:T(8,128)(2,1)}), bf16[4,128,512]{2,1,0:T(8,128)(2,1)S(1)}, u32[]{:S(2)}, u32[]{:S(2)}) async-start(bf16[4,128,512]{2,1,0:T(8,128)(2,1)} %project.1), calls=%async_computation.4 | async-start | bytes 1048576 | tf_op jit(solution)/shard_map/all_to_all | solution.py:424
  129.6 73.7 %all-gather.4.cloned.1.call-start = ((), (), s32[]{:S(2)}) async-start(), calls=%async_computation.11 | async-start | bytes 4718592 | tf_op jit(solution)/shard_map/all_gather | solution.py:430
  137.7 0.8 copy-start.2
  154.6 100.4 %reduce-scatter.2.cloned.1.call-start = ((), (), s32[]{:S(2)}) async-start(), calls=%async_computation.12 | async-start | bytes 2359296 | tf_op jit(solution)/shard_map/reduce_scatter | solution.py:432
  255.0 10.9 %all-to-all-start.7 = ((bf16[8,64,256]{2,1,0:T(8,128)(2,1)}), bf16[8,64,256]{2,1,0:T(8,128)(2,1)S(1)}, u32[]{:S(2)}, u32[]{:S(2)}) async-start(bf16[8,64,256]{2,1,0:T(8,128)(2,1)} %bitcast.56), calls=%async_computation.8 | async-start | bytes 524288 | tf_op jit(solution)/shard_map/all_to_all | solution.py:440
  265.9 0.7 copy-start.3
  268.8 14.1 %all-to-all-start.8 = ((bf16[4,32,2304]{2,1,0:T(8,128)(2,1)}), bf16[4,32,2304]{2,1,0:T(8,128)(2,1)S(1)}, u32[]{:S(2)}, u32[]{:S(2)}) async-start(bf16[4,32,2304]{2,1,0:T(8,128)(2,1)} %bitcast.41), calls=%async_computation.9 | async-start | bytes 1179648 | tf_op jit(solution)/shard_map/all_to_all | solution.py:446
Sparse Core Ops, SparseCore 0:
  74.5 27.2 all-gather.5
  154.7 48.4 all-gather.3
  214.5 40.4 reduce-scatter.1

commit v4 on v3

--- a/solution.py
+++ b/solution.py
@@ -23,6 +23,7 @@
 CTX_LOCAL = 1024
 HIDDEN = 192
 STAT_ROWS = 16
+PAIRS = 2
 MASKED = -1e30
 SCALE2 = math.log2(math.e) / math.sqrt(HEAD_DIM)
 VMEM = 56 * 1024 * 1024
@@ -65,8 +66,8 @@
     )(y_pos, scale, cache)
 
 
-def attend_chunks(q_ref, kv_refs, bias_ref, last_ref, s_ref, order):
-    q_pair = jnp.concatenate([q_ref[0, :, :HEAD_DIM], q_ref[0, :, HEAD_DIM:]], axis=0)
+def attend_chunks(q_ref, kv_refs, bias_ref, last_ref, s_ref, pair, order):
+    q_pair = jnp.concatenate([q_ref[pair, :, :HEAD_DIM], q_ref[pair, :, HEAD_DIM:]], axis=0)
     peak = jnp.full((2 * WIN, BLOCK), -jnp.inf, f32)
     row = lax.broadcasted_iota(jnp.int32, (2 * WIN, BLOCK), 0)
     row = jnp.where(row >= WIN, row - WIN, row)
@@ -78,20 +79,20 @@
         s = s + bias_ref[d]
         cut = jnp.where(later & (last_ref[d] == 1), MASKED, 0.0)
         end = CTX_LOCAL - BLOCK
-        s_ref[:, i * CTX_LOCAL : i * CTX_LOCAL + end] = s[:, :end]
+        s_ref[pair, :, i * CTX_LOCAL : i * CTX_LOCAL + end] = s[:, :end]
         tail = s[:, end:] + cut
-        s_ref[:, i * CTX_LOCAL + end : (i + 1) * CTX_LOCAL] = tail
+        s_ref[pair, :, i * CTX_LOCAL + end : (i + 1) * CTX_LOCAL] = tail
         for b in range(CTX_LOCAL // BLOCK - 1):
             peak = jnp.maximum(peak, s[:, b * BLOCK : (b + 1) * BLOCK])
         peak = jnp.maximum(peak, tail)
     return jnp.max(peak, axis=1, keepdims=True)
 
 
-def weigh_chunks(kv_refs, s_ref, m):
+def weigh_chunks(kv_refs, s_ref, pair, m):
     total = jnp.zeros((2 * WIN, BLOCK), f32)
     acc = jnp.zeros((2 * WIN, HEAD_DIM), f32)
     for i, kv_ref in enumerate(kv_refs):
-        s = s_ref[:, i * CTX_LOCAL : (i + 1) * CTX_LOCAL]
+        s = s_ref[pair, :, i * CTX_LOCAL : (i + 1) * CTX_LOCAL]
         p = jnp.exp2((s - m) * SCALE2)
         for b in range(CTX_LOCAL // BLOCK):
             total = total + p[:, b * BLOCK : (b + 1) * BLOCK]
@@ -99,80 +100,86 @@
     return jnp.sum(total, axis=1, keepdims=True), acc
 
 
-def near_kernel(last_ref, q_ref, bias_ref, kv0, kv1, kv3, acc_ref, stat_ref, s_ref):
-    kv_refs = (kv0, kv1, kv3)
-    m = attend_chunks(q_ref, kv_refs, bias_ref, last_ref, s_ref, (0, 1, 3))
-    l, acc = weigh_chunks(kv_refs, s_ref, m)
-    acc_ref[0] = acc
+def own_kernel(last_ref, q_ref, bias_ref, kv0, acc_ref, stat_ref, s_ref):
     lane = lax.broadcasted_iota(jnp.int32, (2 * WIN, 128), 1)
-    stat_ref[0] = jnp.where(lane == 0, m, l)
-
-
-def far_kernel(last_ref, q_ref, bias_ref, kv2, acc_ref, stat_ref, out_ref, s_ref):
-    m = attend_chunks(q_ref, (kv2,), bias_ref, last_ref, s_ref, (2,))
-    before = stat_ref[0, :, :1]
-    m = jnp.maximum(m, before)
-    l, acc = weigh_chunks((kv2,), s_ref, m)
-    keep = jnp.exp2((before - m) * SCALE2)
-    l = l + stat_ref[0, :, 1:2] * keep
-    out_ref[0, : 2 * WIN, :] = (acc + acc_ref[0] * keep).astype(bf16)
+    maxima = [
+        attend_chunks(q_ref, (kv0,), bias_ref, last_ref, s_ref, pair, (0,))
+        for pair in range(PAIRS)
+    ]
+    for pair, m in enumerate(maxima):
+        l, acc = weigh_chunks((kv0,), s_ref, pair, m)
+        acc_ref[pair] = acc
+        stat_ref[pair] = jnp.where(lane == 0, m, l)
+
+
+def rest_kernel(last_ref, q_ref, bias_ref, kv1, kv3, kv2, acc_ref, stat_ref, out_ref, s_ref):
+    kv_refs = (kv1, kv3, kv2)
     lane = lax.broadcasted_iota(jnp.int32, (2 * WIN, 128), 1)
-    stats = jnp.zeros((2 * WIN, 128), f32)
-    for i, value in enumerate((m, l)):
-        rest = value
-        for j in range(3):
-            term = rest.astype(bf16).astype(f32)
-            rest = rest - term
-            stats = jnp.where(lane == i + 2 * j, term, stats)
-    rows = jnp.transpose(stats)
-    out_ref[0, 2 * WIN :, :] = jnp.concatenate([rows[:8, :WIN], rows[:8, WIN:]], axis=0).astype(
-        bf16
-    )
+    row = lax.broadcasted_iota(jnp.int32, (8, 2 * WIN), 0)
+    maxima = [
+        attend_chunks(q_ref, kv_refs, bias_ref, last_ref, s_ref, pair, (1, 3, 2))
+        for pair in range(PAIRS)
+    ]
+    for pair, highest in enumerate(maxima):
+        before = stat_ref[pair, :, :1]
+        m = jnp.maximum(highest, before)
+        l, acc = weigh_chunks(kv_refs, s_ref, pair, m)
+        keep = jnp.exp2((before - m) * SCALE2)
+        l = l + stat_ref[pair, :, 1:2] * keep
+        out_ref[pair, : 2 * WIN, :] = (acc + acc_ref[pair] * keep).astype(bf16)
+        turned = jnp.transpose(jnp.where(lane % 2 == 0, m, l))[:8]
+        high = turned.astype(bf16).astype(f32)
+        middle = (turned - high).astype(bf16).astype(f32)
+        low = turned - high - middle
+        rows = jnp.where(row < 2, high, jnp.where(row < 4, middle, low))
+        out_ref[pair, 2 * WIN :, :] = jnp.concatenate(
+            [rows[:, :WIN], rows[:, WIN:]], axis=0
+        ).astype(bf16)
 
 
 def attention_specs(extra, outs, chunks):
     whole = pl.BlockSpec((2, CTX_LOCAL, HEAD_DIM), lambda i, *_: (0, 0, 0))
     return pltpu.PrefetchScalarGridSpec(
         num_scalar_prefetch=1,
-        grid=(N_Z,),
+        grid=(N_Z // PAIRS,),
         in_specs=[
-            pl.BlockSpec((1, WIN, 2 * HEAD_DIM), lambda i, *_: (i, 0, 0)),
+            pl.BlockSpec((PAIRS, WIN, 2 * HEAD_DIM), lambda i, *_: (i, 0, 0)),
             pl.BlockSpec((N_Y, 1, CTX_LOCAL), lambda i, *_: (0, 0, 0)),
         ]
         + [whole] * chunks
-        + [pl.BlockSpec((1,) + e, lambda i, *_: (i, 0, 0)) for e in extra],
-        out_specs=[pl.BlockSpec((1,) + o, lambda i, *_: (i, 0, 0)) for o in outs],
-        scratch_shapes=[pltpu.VMEM((2 * WIN, chunks * CTX_LOCAL), f32)],
-    )
-
-
-def near_attention(last, queries, bias, kv0, kv1, kv3):
+        + [pl.BlockSpec((PAIRS,) + e, lambda i, *_: (i, 0, 0)) for e in extra],
+        out_specs=[pl.BlockSpec((PAIRS,) + o, lambda i, *_: (i, 0, 0)) for o in outs],
+        scratch_shapes=[pltpu.VMEM((PAIRS, 2 * WIN, chunks * CTX_LOCAL), f32)],
+    )
+
+
+def own_attention(last, queries, bias, kv0):
     square = (2 * WIN, HEAD_DIM)
     return pl.pallas_call(
-        near_kernel,
-        grid_spec=attention_specs([], [square, square], 3),
+        own_kernel,
+        grid_spec=attention_specs([], [square, square], 1),
         out_shape=[jax.ShapeDtypeStruct((N_Z,) + square, f32)] * 2,
+        compiler_params=params(),
+        cost_estimate=pl.CostEstimate(
+            flops=3 << 30, bytes_accessed=8 << 20, transcendentals=2 << 20
+        ),
+        name="own_attention",
+    )(last, queries, bias, kv0)
+
+
+def rest_attention(last, queries, bias, kv1, kv3, kv2, acc, stat):
+    square = (2 * WIN, HEAD_DIM)
+    message = (2 * WIN + STAT_ROWS, HEAD_DIM)
+    return pl.pallas_call(
+        rest_kernel,
+        grid_spec=attention_specs([square, square], [message], 3),
+        out_shape=[jax.ShapeDtypeStruct((N_Z,) + message, bf16)],
         compiler_params=params(),
         cost_estimate=pl.CostEstimate(
             flops=8 << 30, bytes_accessed=8 << 20, transcendentals=6 << 20
         ),
-        name="near_attention",
-    )(last, queries, bias, kv0, kv1, kv3)
-
-
-def far_attention(last, queries, bias, kv2, acc, stat):
-    square = (2 * WIN, HEAD_DIM)
-    message = (2 * WIN + STAT_ROWS, HEAD_DIM)
-    return pl.pallas_call(
-        far_kernel,
-        grid_spec=attention_specs([square, square], [message], 1),
-        out_shape=[jax.ShapeDtypeStruct((N_Z,) + message, bf16)],
-        compiler_params=params(),
-        cost_estimate=pl.CostEstimate(
-            flops=3 << 30, bytes_accessed=8 << 20, transcendentals=2 << 20
-        ),
-        name="far_attention",
-    )(last, queries, bias, kv2, acc, stat)[0]
+        name="rest_attention",
+    )(last, queries, bias, kv1, kv3, kv2, acc, stat)[0]
 
 
 def combine_kernel(in_ref, out_ref):
@@ -245,21 +252,24 @@
 
 def experts_kernel(x_ref, gain_ref, wg_ref, wu_ref, wd_ref, by_z_ref, by_x_ref):
     tokens = x_ref.shape[1]
-    squares = jnp.zeros((tokens, COLS), f32)
-    for z in range(N_Z):
-        wide = x_ref[z].astype(f32)
-        squares = squares + wide * wide
-    factor = lax.rsqrt(jnp.sum(squares, axis=1, keepdims=True) * (1.0 / D) + 1e-06)
+    squares = jnp.zeros((tokens, 128), f32)
     gate = jnp.zeros((tokens, HIDDEN), f32)
     up = jnp.zeros((tokens, HIDDEN), f32)
     contract = (((1,), (1,)), ((), ()))
     for z in range(N_Z):
         cols = slice(z * COLS, (z + 1) * COLS)
-        normed = (x_ref[z].astype(f32) * factor * gain_ref[:, cols]).astype(bf16)
+        wide = x_ref[z].astype(f32)
+        for b in range(COLS // 128):
+            part = wide[:, b * 128 : (b + 1) * 128]
+            squares = squares + part * part
+        gained = (wide * gain_ref[:, cols]).astype(bf16)
         gate = gate + lax.dot_general(
-            normed, wg_ref[:, cols], contract, preferred_element_type=f32
+            gained, wg_ref[:, cols], contract, preferred_element_type=f32
         )
-        up = up + lax.dot_general(normed, wu_ref[:, cols], contract, preferred_element_type=f32)
+        up = up + lax.dot_general(gained, wu_ref[:, cols], contract, preferred_element_type=f32)
+    factor = lax.rsqrt(jnp.sum(squares, axis=1, keepdims=True) * (1.0 / D) + 1e-06)
+    gate = gate * factor
+    up = up * factor
     hidden = (gate / (1.0 + jnp.exp(-gate)) * up).astype(bf16)
     for z in range(N_Z):
         cols = slice(z * COLS, (z + 1) * COLS)
@@ -268,7 +278,7 @@
         by_x_ref[:, z * HALF : (z + 1) * HALF] = done[:, HALF:]
 
 
-def experts(x, gain, w_gate, w_up, w_down, tile=128):
+def experts(x, gain, w_gate, w_up, w_down, tile=256):
     tokens = x.shape[1]
     whole = pl.BlockSpec((HIDDEN, D), lambda i: (0, 0))
     return pl.pallas_call(
@@ -412,8 +422,10 @@
     back_table = jnp.where(in_slot, weight[:, None, :], 0.0).astype(bf16)
     back_table = back_table.reshape(N_GRP * CAP, WIN).T
 
-    acc, stat = near_attention(last, queries_mine, bias, kv_own, kv_from[1], kv_from[3])
-    parts = far_attention(last, queries_mine, bias, kv_from[2], acc, stat)
+    acc, stat = own_attention(last, queries_mine, bias, kv_own)
+    parts = rest_attention(
+        last, queries_mine, bias, kv_from[1], kv_from[3], kv_from[2], acc, stat
+    )
     parts, early = lax.optimization_barrier((parts, early))
     resid_rows = lax.dynamic_update_slice_in_dim(
         jnp.zeros((WIN, COLS), bf16), early[:, part:].reshape(rows, COLS), y_pos * rows, 0

time: 307 us -> 293 us (0.954)
  Pallas kernels: 56.5 us -> 48.1 us
  waiting for transfers between devices: 104 us -> 99.8 us
    pallas_call x2, Pallas kernels: 25.4 us -> 19.7 us  [the longest x1 13.2 us: rest_attention(): pl.pallas_call(rest_kernel, grid_spec=attention_specs([square, square], [...]
    ppermute x3, waiting for transfers between devices: 4.93 us -> 0.01 us  [per_device(): lax.ppermute(chunks[d], 'y', [(i, (i + d) % N_Y) for i in range(N_Y)])]
  transfers between devices with their start and end apart: 12 -> 12, of which waited for: 9 -> 7; matrix products, arithmetic and copies ran while one was open for 2% -> 3% of each run, Pallas kernels for 10% -> 9%
where the time goes in v4:
time: 293 us; the launch traced here: 291 us
  waiting for transfers between devices  99.8 us (34%)
  blocking collectives  84.2 us (29%)
  Pallas kernels  48.1 us (16%)
  starting transfers between devices  34.3 us (12%)
  between operations  13.4 us (5%)
  local copies, waits for them, and re-layouts  8.94 us (3%)
    all_gather x1, waiting for transfers between devices, per_device(): arrivals = lax.all_gather(arrivals, 'z', axis=0, tiled=False)  48.3 us
    all_to_all x1, blocking collectives, per_device(): lax.all_to_all(by_x.reshape(N_GRP, CAP, D // 2), ('x', 'c'), 0, 0, tiled=...  31 us
    all_to_all x1, blocking collectives, per_device(): parts = lax.all_to_all(parts, 'z', 0, 0, tiled=True)  25.3 us
    all_to_all x1, waiting for transfers between devices, per_device(): attended = lax.all_to_all(combine(parts), 'z', 0, 0, tiled=True)  14.5 us
    all_to_all x1, blocking collectives, per_device(): return finish(lax.all_to_all(tail, 'z', 0, 0, tiled=True))[None]  14.1 us
    all_to_all x1, blocking collectives, per_device(): lax.all_to_all(outgoing.reshape(N_GRP, CAP, COLS), ('x', 'c'), 0, 0, tile...  13.9 us
    pallas_call x1, Pallas kernels, rest_attention(): pl.pallas_call(rest_kernel, grid_spec=attention_specs([square, square], [...  13.2 us
    reduce_scatter x1, waiting for transfers between devices, per_device(): lax.psum_scatter(by_z.reshape(N_Z * N_GRP * CAP, HALF), 'z', scatter_dime...  9.77 us
  transfers between devices with their start and end apart: 12, of which 7 were waited for; matrix products, arithmetic and copies ran while one was open for 3% of the time, Pallas kernels for 9%

profile of v4, /device:TPU:2, one launch (start us, length us, event | category | flops | bytes accessed | tf_op | source)
XLA Modules:
  0.0 291.4 jit_solution(11586667824748852312)
XLA Ops:
  6.5 4.9 %dequantize.1 = (bf16[2,1024,128]{2,1,0:T(8,128)(2,1)}, bf16[2,1024,128]{2,1,0:T(8,128)(2,1)}, bf16[2,1024,128]{2,1,0:T(8,128)(2,1)}, bf16[2,1024,128]{2,1,0:T(8,128)(2,1)}) custom-call(s32[1]{0:T(128)} %bitcast.7.y_ref, f32[8,8]{1,0:T(8,128)} %bitcast.67, bf16[1024,1024]{1,0:T(8,128)(2,1)} %bitcast.42), custom_call_target="tpu_custom_call" | custom-call | flops 1048576 | bytes 4194304 | tf_op jit(solution)/shard_map/dequantize/pallas_call | solution.py:54
  11.5 0.8 broadcast_in_dim.81
  12.3 8.5 %all-to-all-start = ((bf16[8,128,256]{2,1,0:T(8,128)(2,1)}), bf16[8,128,256]{2,1,0:T(8,128)(2,1)S(1)}, u32[]{:S(2)}, u32[]{:S(2)}) async-start(bf16[8,128,256]{2,1,0:T(8,128)(2,1)} %broadcast_in_dim.81), calls=%async_computation | async-start | bytes 1048576 | tf_op jit(solution)/shard_map/all_to_all | solution.py:386
  20.8 1.6 collective-permute-start
  22.3 1.7 collective-permute-start.1
  24.0 2.0 collective-permute-start.2
  26.0 0.1 copy.52
  26.1 0.5 broadcast.144
  26.7 0.7 reduce.4
  27.3 0.1 reshape_squeeze.3
  27.5 0.6 gather_fusion
  28.0 0.5 and_convert_fusion.last_ref
  28.6 0.1 fusion.2
  28.6 9.6 %all-to-all-done.q_ref = bf16[8,128,256]{2,1,0:T(8,128)(2,1)S(1)} async-done(((bf16[8,128,256]{2,1,0:T(8,128)(2,1)}), bf16[8,128,256]{2,1,0:T(8,128)(2,1)S(1)}, u32[]{:S(2)}, u32[]{:S(2)}) %all-to-all-start) | async-done | bytes 524320 | tf_op jit(solution)/shard_map/all_to_all | solution.py:386
  38.3 0.9 copy.49
  39.2 3.4 %all-to-all-start.1 = ((bf16[8,36,512]{2,1,0:T(8,128)(2,1)}), bf16[8,36,512]{2,1,0:T(8,128)(2,1)S(1)}, u32[]{:S(2)}, u32[]{:S(2)}) async-start(bf16[8,36,512]{2,1,0:T(8,128)(2,1)} %copy.49), calls=%async_computation.1 | async-start | bytes 655360 | tf_op jit(solution)/shard_map/all_to_all | solution.py:411
  42.6 0.0 all-gather.6.cloned.1.call-start
  42.7 0.7 broadcast_in_dim.86
  43.4 6.5 %own_attention.1 = (f32[8,256,128]{2,1,0:T(8,128)}, f32[8,256,128]{2,1,0:T(8,128)}) custom-call(s32[4]{0:T(128)} %and_convert_fusion.last_ref, bf16[8,128,256]{2,1,0:T(8,128)(2,1)} %copy-done.5, f32[4,1,1024]{2,1,0:T(1,128)} %bitcast.63, bf16[2,1024,128]{2,1,0:T(8,128)(2,1)} %get-tuple-element.28.kv0), custom_call_target="tpu_custom_call" | custom-call | flops 3221225472 | bytes 8388608 | tf_op jit(solution)/shard_map/own_attention/pallas_call | solution.py:158
  49.8 0.0 collective-permute-done.kv1
  49.8 0.0 collective-permute-done.1.kv3
  49.8 0.0 collective-permute-done.2.kv2
  49.8 13.2 %rest_attention.1 = bf16[8,272,128]{2,1,0:T(8,128)(2,1)} custom-call(s32[4]{0:T(128)} %and_convert_fusion.last_ref, bf16[8,128,256]{2,1,0:T(8,128)(2,1)} %copy-done.5, f32[4,1,1024]{2,1,0:T(1,128)} %bitcast.64, bf16[2,1024,128]{2,1,0:T(8,128)(2,1)} %collective-permute-done.kv1, bf16[2,1024,128]{2,1,0:T(8,128)(2,1)} %collective-permute-done.1.kv3, ...), custom_call_target="tpu_custom_call" | custom-call | flops 8589934592 | bytes 8388608 | tf_op jit(solution)/shard_map/rest_attention/pallas_call | solution.py:173
  63.1 0.0 all-to-all-done.1
  63.1 0.7 slice.6
  63.8 0.0 all-gather.6.cloned.1.call-update
  63.9 25.3 %all_to_all.50.in_ref = bf16[8,272,128]{2,1,0:T(8,128)(2,1)} all-to-all(bf16[8,272,128]{2,1,0:T(8,128)(2,1)} %rest_attention.1), channel_id=1, replica_groups=mesh['y'=4,'z'=8,'x'=4,'c'=2] {'z'}, dimensions={0} | all-to-all | bytes 1114112 | tf_op jit(solution)/shard_map/all_to_all | solution.py:434
  89.1 2.4 combine.1
  91.5 3.5 %all-to-all-start.3 = ((bf16[8,128,256]{2,1,0:T(8,128)(2,1)}), bf16[8,128,256]{2,1,0:T(8,128)(2,1)S(1)}, u32[]{:S(2)}, u32[]{:S(2)}) async-start(bf16[8,128,256]{2,1,0:T(8,128)(2,1)} %combine.1), calls=%async_computation.3 | async-start | bytes 1048576 | tf_op jit(solution)/shard_map/all_to_all | solution.py:435
  95.0 0.1 fusion.1
  95.2 0.1 copy.47
  95.3 0.1 compare_reduce_fusion
  95.4 0.2 copy.46
  95.6 0.3 reduce_window_sum.11
  95.9 14.5 %all-to-all-done.3.a_ref = bf16[8,128,256]{2,1,0:T(8,128)(2,1)S(1)} async-done(((bf16[8,128,256]{2,1,0:T(8,128)(2,1)}), bf16[8,128,256]{2,1,0:T(8,128)(2,1)S(1)}, u32[]{:S(2)}, u32[]{:S(2)}) %all-to-all-start.3) | async-done | bytes 524320 | tf_op jit(solution)/shard_map/all_to_all | solution.py:435
  110.5 0.8 copy-done.1
  111.3 2.9 %project.1 = bf16[4,128,512]{2,1,0:T(8,128)(2,1)} custom-call(bf16[8,128,256]{2,1,0:T(8,128)(2,1)} %copy-done.1, bf16[8,8,32,512]{3,2,1,0:T(8,128)(2,1)} %bitcast.43, bf16[128,512]{1,0:T(8,128)(2,1)} %copy-done.4), custom_call_target="tpu_custom_call" | custom-call | tf_op jit(solution)/shard_map/project/pallas_call | solution.py:224
  114.2 4.5 %all-to-all-start.4 = ((bf16[4,128,512]{2,1,0:T(8,128)(2,1)}), bf16[4,128,512]{2,1,0:T(8,128)(2,1)S(1)}, u32[]{:S(2)}, u32[]{:S(2)}) async-start(bf16[4,128,512]{2,1,0:T(8,128)(2,1)} %project.1), calls=%async_computation.4 | async-start | bytes 1048576 | tf_op jit(solution)/shard_map/all_to_all | solution.py:436
  118.7 0.1 copy.45
  118.9 0.1 eq.57
  118.9 0.7 fusion
  119.7 0.8 copy.50.table_ref
  120.5 6.3 %all-to-all-done.4.parts_ref = bf16[4,128,512]{2,1,0:T(8,128)(2,1)S(1)} async-done(((bf16[4,128,512]{2,1,0:T(8,128)(2,1)}), bf16[4,128,512]{2,1,0:T(8,128)(2,1)S(1)}, u32[]{:S(2)}, u32[]{:S(2)}) %all-to-all-start.4) | async-done | bytes 524320 | tf_op jit(solution)/shard_map/all_to_all | solution.py:436
  126.8 0.8 copy-done.2
  127.6 2.2 dispatch.1
  129.8 13.9 %all_to_all.51 = bf16[8,64,512]{2,1,0:T(8,128)(2,1)} all-to-all(bf16[8,64,512]{2,1,0:T(8,128)(2,1)} %bitcast.54), channel_id=1, replica_groups=mesh['y'=4,'z'=8,'x'=4,'c'=2] {'x','c'}, dimensions={0} | all-to-all | bytes 1048576 | tf_op jit(solution)/shard_map/all_to_all | solution.py:439
  143.6 0.0 all-gather.4.cloned.1.call-update
  143.7 0.0 reduce-scatter.2.cloned.1.call-start
  143.7 48.3 %all-gather.4.cloned.1.call-done.x_ref = bf16[8,512,512]{2,1,0:T(8,128)(2,1)} async-done(((bf16[1,512,512]{2,1,0:T(8,128)(2,1)}), bf16[8,512,512]{2,1,0:T(8,128)(2,1)}) %all-gather.4.cloned.1.call-update) | async-done | bytes 4194320 | tf_op jit(solution)/shard_map/all_gather | solution.py:442
  192.0 8.3 %experts.1 = (bf16[8,512,256]{2,1,0:T(8,128)(2,1)}, bf16[512,2048]{1,0:T(8,128)(2,1)}) custom-call(bf16[8,512,512]{2,1,0:T(8,128)(2,1)} %all-gather.4.cloned.1.call-done.x_ref, f32[1,4096]{1,0:T(1,128)} %bitcast.62, bf16[192,4096]{1,0:T(8,128)(2,1)} %bitcast.47, bf16[192,4096]{1,0:T(8,128)(2,1)} %bitcast.48, bf16[192,4096]{1,0:T(8,128)(2,1)} %bitcast.49), custom_call_target="tpu_custom_call" | custom-call | tf_op jit(solution)/shard_map/experts/pallas_call | solution.py:284
  200.3 0.0 reduce-scatter.2.cloned.1.call-update
  200.3 31.0 %all_to_all.52 = bf16[8,64,2048]{2,1,0:T(8,128)(2,1)} all-to-all(bf16[8,64,2048]{2,1,0:T(8,128)(2,1)} %bitcast.44), channel_id=1, replica_groups=mesh['y'=4,'z'=8,'x'=4,'c'=2] {'x','c'}, dimensions={0} | all-to-all | bytes 4194304 | tf_op jit(solution)/shard_map/all_to_all | solution.py:447
  231.3 9.8 %reduce-scatter.2.cloned.1.call-done = bf16[512,256]{1,0:T(8,128)(2,1)} async-done(((bf16[4096,256]{1,0:T(8,128)(2,1)}), bf16[512,256]{1,0:T(8,128)(2,1)}) %reduce-scatter.2.cloned.1.call-update) | async-done | bytes 262160 | tf_op jit(solution)/shard_map/reduce_scatter | solution.py:444
  241.1 4.8 %all-to-all-start.7 = ((bf16[8,64,256]{2,1,0:T(8,128)(2,1)}), bf16[8,64,256]{2,1,0:T(8,128)(2,1)S(1)}, u32[]{:S(2)}, u32[]{:S(2)}) async-start(bf16[8,64,256]{2,1,0:T(8,128)(2,1)} %bitcast.56), calls=%async_computation.8 | async-start | bytes 524288 | tf_op jit(solution)/shard_map/all_to_all | solution.py:452
  245.8 3.9 %mix.1.mixed_ref = bf16[128,2048]{1,0:T(8,128)(2,1)} custom-call(bf16[128,512]{1,0:T(8,128)(2,1)} %get-tuple-element.39.table_ref, bf16[512,2048]{1,0:T(8,128)(2,1)} %bitcast.40), custom_call_target="tpu_custom_call" | custom-call | flops 268435456 | bytes 4194304 | tf_op jit(solution)/shard_map/mix/pallas_call | solution.py:315
  249.8 2.1 all-to-all-done.7
  251.9 0.7 copy-done.3
  252.6 2.2 mix_rest.1
  254.8 4.4 %all-to-all-start.8 = ((bf16[4,32,2304]{2,1,0:T(8,128)(2,1)}), bf16[4,32,2304]{2,1,0:T(8,128)(2,1)S(1)}, u32[]{:S(2)}, u32[]{:S(2)}) async-start(bf16[4,32,2304]{2,1,0:T(8,128)(2,1)} %bitcast.41), calls=%async_computation.9 | async-start | bytes 1179648 | tf_op jit(solution)/shard_map/all_to_all | solution.py:458
  259.2 0.8 constant_dynamic-slice_fusion
  259.9 9.1 %all-to-all-done.8 = bf16[4,32,2304]{2,1,0:T(8,128)(2,1)S(1)} async-done(((bf16[4,32,2304]{2,1,0:T(8,128)(2,1)}), bf16[4,32,2304]{2,1,0:T(8,128)(2,1)S(1)}, u32[]{:S(2)}, u32[]{:S(2)}) %all-to-all-start.8) | async-done | bytes 589856 | tf_op jit(solution)/shard_map/all_to_all | solution.py:458
  269.0 0.1 reduce_sum.22
  269.2 14.1 %all_to_all.53.in_ref = bf16[8,4,2816]{2,1,0:T(4,128)(2,1)} all-to-all(bf16[8,4,2816]{2,1,0:T(4,128)(2,1)S(1)} %reshape.118), channel_id=1, replica_groups=mesh['y'=4,'z'=8,'x'=4,'c'=2] {'z'}, dimensions={0} | all-to-all | bytes 360448 | tf_op jit(solution)/shard_map/all_to_all | solution.py:461
  283.3 1.6 finish.1
  (42 shorter events, 0.3 us)
Async XLA Ops:
  6.5 19.5 %copy-start = (bf16[256,4096]{1,0:T(8,128)(2,1)S(1)}, bf16[256,4096]{1,0:T(8,128)(2,1)}, u32[]{:S(2)}) copy-start(bf16[256,4096]{1,0:T(8,128)(2,1)} %param.17) | copy-start | bytes 6291460
  6.5 4.9 %copy-start.6 = (bf16[1,128,256]{2,1,0:T(8,128)(2,1)S(1)}, bf16[1,128,256]{2,1,0:T(8,128)(2,1)}, u32[]{:S(2)}) copy-start(bf16[1,128,256]{2,1,0:T(8,128)(2,1)} %param.12) | copy-start | bytes 196612
  6.5 19.5 %copy-start.7 = (bf16[1,4,4096]{2,1,0:T(4,128)(2,1)S(1)}, bf16[1,4,4096]{2,1,0:T(4,128)(2,1)}, u32[]{:S(2)}) copy-start(bf16[1,4,4096]{2,1,0:T(4,128)(2,1)} %param.16) | copy-start | bytes 98308
  6.5 20.1 %copy-start.10 = (s32[1,1,256]{2,1,0:T(1,128)S(1)}, s32[1,1,256]{2,1,0:T(1,128)}, u32[]{:S(2)}) copy-start(s32[1,1,256]{2,1,0:T(1,128)} %param.15) | copy-start | bytes 3076
  12.3 26.0 %all-to-all-start = ((bf16[8,128,256]{2,1,0:T(8,128)(2,1)}), bf16[8,128,256]{2,1,0:T(8,128)(2,1)S(1)}, u32[]{:S(2)}, u32[]{:S(2)}) async-start(bf16[8,128,256]{2,1,0:T(8,128)(2,1)} %broadcast_in_dim.81), calls=%async_computation | async-start | bytes 1048576 | tf_op jit(solution)/shard_map/all_to_all | solution.py:386
  20.8 29.1 %collective-permute-start = (bf16[2,1024,128]{2,1,0:T(8,128)(2,1)}, bf16[2,1024,128]{2,1,0:T(8,128)(2,1)}, u32[]{:S(2)}, u32[]{:S(2)}) collective-permute-start(bf16[2,1024,128]{2,1,0:T(8,128)(2,1)} %get-tuple-element.25), channel_id=1, source_target_pairs={{0,64},{64,128},{128,192},{192,0},{1,65},{65,129},{129,193},{193,1... | collective-permute-start | bytes 1572872 | tf_op jit(solution)/shard_map/ppermute | solution.py:390
  22.3 27.5 %collective-permute-start.1 = (bf16[2,1024,128]{2,1,0:T(8,128)(2,1)}, bf16[2,1024,128]{2,1,0:T(8,128)(2,1)}, u32[]{:S(2)}, u32[]{:S(2)}) collective-permute-start(bf16[2,1024,128]{2,1,0:T(8,128)(2,1)} %get-tuple-element.26), channel_id=1, source_target_pairs={{0,192},{64,0},{128,64},{192,128},{1,193},{65,1},{129,65},{193,129... | collective-permute-start | bytes 1572872 | tf_op jit(solution)/shard_map/ppermute | solution.py:390
  24.0 25.8 %collective-permute-start.2 = (bf16[2,1024,128]{2,1,0:T(8,128)(2,1)}, bf16[2,1024,128]{2,1,0:T(8,128)(2,1)}, u32[]{:S(2)}, u32[]{:S(2)}) collective-permute-start(bf16[2,1024,128]{2,1,0:T(8,128)(2,1)} %get-tuple-element.27), channel_id=1, source_target_pairs={{0,128},{64,192},{128,0},{192,64},{1,129},{65,193},{129,1},{193,65... | collective-permute-start | bytes 1572872 | tf_op jit(solution)/shard_map/ppermute | solution.py:390
  38.3 5.1 %copy-start.5 = (bf16[8,128,256]{2,1,0:T(8,128)(2,1)}, bf16[8,128,256]{2,1,0:T(8,128)(2,1)S(1)}, u32[]{:S(2)}) copy-start(bf16[8,128,256]{2,1,0:T(8,128)(2,1)S(1)} %all-to-all-done.q_ref) | copy-start | bytes 1572868
  39.2 23.9 %all-to-all-start.1 = ((bf16[8,36,512]{2,1,0:T(8,128)(2,1)}), bf16[8,36,512]{2,1,0:T(8,128)(2,1)S(1)}, u32[]{:S(2)}, u32[]{:S(2)}) async-start(bf16[8,36,512]{2,1,0:T(8,128)(2,1)} %copy.49), calls=%async_computation.1 | async-start | bytes 655360 | tf_op jit(solution)/shard_map/all_to_all | solution.py:411
  42.6 67.8 %all-gather.6.cloned.1.call-start = ((), (), s32[]{:S(2)}) async-start(), calls=%async_computation.13 | async-start | bytes 2359296 | tf_op jit(solution)/shard_map/all_gather | solution.py:433
  63.1 31.9 %copy-start.8 = (s32[1,128,8]{1,2,0:T(8,128)S(1)}, s32[1,128,8]{1,2,0:T(8,128)}, u32[]{:S(2)}) copy-start(s32[1,128,8]{1,2,0:T(8,128)} %param.19) | copy-start | bytes 12292
  63.1 31.9 %copy-start.9 = (f32[1,128,8]{1,2,0:T(8,128)S(1)}, f32[1,128,8]{1,2,0:T(8,128)}, u32[]{:S(2)}) copy-start(f32[1,128,8]{1,2,0:T(8,128)} %param.20) | copy-start | bytes 12292
  91.5 19.0 %all-to-all-start.3 = ((bf16[8,128,256]{2,1,0:T(8,128)(2,1)}), bf16[8,128,256]{2,1,0:T(8,128)(2,1)S(1)}, u32[]{:S(2)}, u32[]{:S(2)}) async-start(bf16[8,128,256]{2,1,0:T(8,128)(2,1)} %combine.1), calls=%async_computation.3 | async-start | bytes 1048576 | tf_op jit(solution)/shard_map/all_to_all | solution.py:435
  95.9 14.5 %copy-start.4 = (bf16[128,512]{1,0:T(8,128)(2,1)}, bf16[128,512]{1,0:T(8,128)(2,1)S(1)}, u32[]{:S(2)}) copy-start(bf16[128,512]{1,0:T(8,128)(2,1)S(1)} %constant_dynamic-update-slice_fusion.resid_ref) | copy-start | bytes 393220
  110.5 0.8 copy-start.1
  114.2 12.6 %all-to-all-start.4 = ((bf16[4,128,512]{2,1,0:T(8,128)(2,1)}), bf16[4,128,512]{2,1,0:T(8,128)(2,1)S(1)}, u32[]{:S(2)}, u32[]{:S(2)}) async-start(bf16[4,128,512]{2,1,0:T(8,128)(2,1)} %project.1), calls=%async_computation.4 | async-start | bytes 1048576 | tf_op jit(solution)/shard_map/all_to_all | solution.py:436
  118.7 73.3 %all-gather.4.cloned.1.call-start = ((), (), s32[]{:S(2)}) async-start(), calls=%async_computation.11 | async-start | bytes 4718592 | tf_op jit(solution)/shard_map/all_gather | solution.py:442
  126.8 0.8 copy-start.2
  143.7 97.4 %reduce-scatter.2.cloned.1.call-start = ((), (), s32[]{:S(2)}) async-start(), calls=%async_computation.12 | async-start | bytes 2359296 | tf_op jit(solution)/shard_map/reduce_scatter | solution.py:444
  241.1 10.8 %all-to-all-start.7 = ((bf16[8,64,256]{2,1,0:T(8,128)(2,1)}), bf16[8,64,256]{2,1,0:T(8,128)(2,1)S(1)}, u32[]{:S(2)}, u32[]{:S(2)}) async-start(bf16[8,64,256]{2,1,0:T(8,128)(2,1)} %bitcast.56), calls=%async_computation.8 | async-start | bytes 524288 | tf_op jit(solution)/shard_map/all_to_all | solution.py:452
  251.9 0.7 copy-start.3
  254.8 14.2 %all-to-all-start.8 = ((bf16[4,32,2304]{2,1,0:T(8,128)(2,1)}), bf16[4,32,2304]{2,1,0:T(8,128)(2,1)S(1)}, u32[]{:S(2)}, u32[]{:S(2)}) async-start(bf16[4,32,2304]{2,1,0:T(8,128)(2,1)} %bitcast.41), calls=%async_computation.9 | async-start | bytes 1179648 | tf_op jit(solution)/shard_map/all_to_all | solution.py:458
Sparse Core Ops, SparseCore 0:
  64.0 27.9 all-gather.5
  143.8 48.1 all-gather.3
  200.5 40.5 reduce-scatter.1

commit v5 on v4

--- a/solution.py
+++ b/solution.py
@@ -20,6 +20,8 @@
 D = 4096
 COLS = D // N_Z
 HALF = COLS // 2
+NEAR = 384
+FAR = COLS - NEAR
 CTX_LOCAL = 1024
 HIDDEN = 192
 STAT_ROWS = 16
@@ -43,10 +45,10 @@
         for part in range(2):
             column = part * KV_HEADS + head
             lanes = pl.ds(pl.multiple_of(column * HEAD_DIM, HEAD_DIM), HEAD_DIM)
-            for b in range(2):
+            for b in range(4):
                 rows = slice(b * BLOCK, (b + 1) * BLOCK)
                 raw = cache_ref[rows, lanes].astype(f32)
-                out_ref[part, rows, :] = (raw * scale_ref[2 * step + b, column]).astype(bf16)
+                out_ref[part, rows, :] = (raw * scale_ref[4 * step + b, column]).astype(bf16)
 
 
 def dequantize(y_pos, scale, cache):
@@ -55,9 +57,9 @@
         dequantize_kernel,
         grid_spec=pltpu.PrefetchScalarGridSpec(
             num_scalar_prefetch=2,
-            grid=(CTX_LOCAL // (2 * BLOCK),),
-            in_specs=[pl.BlockSpec((2 * BLOCK, 2 * KV_HEADS * HEAD_DIM), lambda i, *_: (i, 0))],
-            out_specs=[pl.BlockSpec((2, 2 * BLOCK, HEAD_DIM), lambda i, *_: (0, i, 0))] * N_Y,
+            grid=(CTX_LOCAL // (4 * BLOCK),),
+            in_specs=[pl.BlockSpec((4 * BLOCK, 2 * KV_HEADS * HEAD_DIM), lambda i, *_: (i, 0))],
+            out_specs=[pl.BlockSpec((2, 4 * BLOCK, HEAD_DIM), lambda i, *_: (0, i, 0))] * N_Y,
         ),
         out_shape=[shape] * N_Y,
         compiler_params=params(),
@@ -229,13 +231,17 @@
     )(attended, w_cols, resid_rows)
 
 
-def dispatch_kernel(parts_ref, table_ref, stream_ref, out_ref):
+def dispatch_kernel(parts_ref, table_ref, stream_ref, out_ref, spread_ref):
     total = parts_ref[0].astype(f32)
     for y in range(1, N_Y):
         total = total + parts_ref[y].astype(f32)
     stream = total.astype(bf16)
     stream_ref[...] = stream
-    out_ref[...] = jnp.dot(table_ref[...], stream, preferred_element_type=f32).astype(bf16)
+    out_ref[...] = jnp.dot(
+        table_ref[...], stream[:, :NEAR], preferred_element_type=f32
+    ).astype(bf16)
+    for z in range(N_Z):
+        spread_ref[z] = stream[:, NEAR:]
 
 
 def dispatch(parts, table):
@@ -243,14 +249,29 @@
         dispatch_kernel,
         out_shape=(
             jax.ShapeDtypeStruct((WIN, COLS), bf16),
-            jax.ShapeDtypeStruct((N_GRP * CAP, COLS), bf16),
+            jax.ShapeDtypeStruct((N_GRP * CAP, NEAR), bf16),
+            jax.ShapeDtypeStruct((N_Z, WIN, FAR), bf16),
         ),
         compiler_params=params(),
         name="dispatch",
     )(parts, table)
 
 
-def experts_kernel(x_ref, gain_ref, wg_ref, wu_ref, wd_ref, by_z_ref, by_x_ref):
+def select_kernel(parts_ref, table_ref, out_ref):
+    wide = jnp.concatenate([parts_ref[z] for z in range(N_Z)], axis=1)
+    out_ref[...] = jnp.dot(table_ref[...], wide, preferred_element_type=f32).astype(bf16)
+
+
+def select(parts, table):
+    return pl.pallas_call(
+        select_kernel,
+        out_shape=jax.ShapeDtypeStruct((N_GRP * CAP, N_Z * FAR), bf16),
+        compiler_params=params(),
+        name="select",
+    )(parts, table)
+
+
+def experts_kernel(x_ref, rest_ref, gain_ref, wg_ref, wu_ref, wd_ref, by_z_ref, by_x_ref):
     tokens = x_ref.shape[1]
     squares = jnp.zeros((tokens, 128), f32)
     gate = jnp.zeros((tokens, HIDDEN), f32)
@@ -258,7 +279,8 @@
     contract = (((1,), (1,)), ((), ()))
     for z in range(N_Z):
         cols = slice(z * COLS, (z + 1) * COLS)
-        wide = x_ref[z].astype(f32)
+        far = rest_ref[:, z * FAR : (z + 1) * FAR]
+        wide = jnp.concatenate([x_ref[z], far], axis=1).astype(f32)
         for b in range(COLS // 128):
             part = wide[:, b * 128 : (b + 1) * 128]
             squares = squares + part * part
@@ -278,14 +300,15 @@
         by_x_ref[:, z * HALF : (z + 1) * HALF] = done[:, HALF:]
 
 
-def experts(x, gain, w_gate, w_up, w_down, tile=256):
+def experts(x, rest, gain, w_gate, w_up, w_down, tile=256):
     tokens = x.shape[1]
     whole = pl.BlockSpec((HIDDEN, D), lambda i: (0, 0))
     return pl.pallas_call(
         experts_kernel,
         grid=(tokens // tile,),
         in_specs=[
-            pl.BlockSpec((N_Z, tile, COLS), lambda i: (0, i, 0)),
+            pl.BlockSpec((N_Z, tile, NEAR), lambda i: (0, i, 0)),
+            pl.BlockSpec((tile, N_Z * FAR), lambda i: (i, 0)),
             pl.BlockSpec((1, D), lambda i: (0, 0)),
             whole,
             whole,
@@ -301,7 +324,7 @@
         ],
         compiler_params=params(),
         name="experts",
-    )(x, gain, w_gate, w_up, w_down)
+    )(x, rest, gain, w_gate, w_up, w_down)
 
 
 def mix_kernel(table_ref, parts_ref, out_ref):
@@ -311,7 +334,7 @@
 
 
 def mix(table, parts):
-    tile = 512
+    tile = 1024
     return pl.pallas_call(
         mix_kernel,
         grid=(parts.shape[1] // tile,),
@@ -382,7 +405,7 @@
     z_pos = lax.axis_index("z")
 
     chunks = dequantize(y_pos[None], kv_scale[0], kv_cache[0])
-    kv_own, queries = lax.optimization_barrier((chunks[0], queries))
+    kv_own = chunks[0]
     queries_mine = lax.all_to_all(
         jnp.broadcast_to(queries, (N_Z,) + queries.shape[1:]), "z", 0, 0, tiled=True
     )
@@ -434,13 +457,20 @@
     parts = lax.all_to_all(parts, "z", 0, 0, tiled=True)
     attended = lax.all_to_all(combine(parts), "z", 0, 0, tiled=True)
     projected = lax.all_to_all(project(attended, w_cols, resid_rows), "y", 0, 0, tiled=True)
-    stream, outgoing = dispatch(projected, out_table)
+    stream, outgoing, spread = dispatch(projected, out_table)
 
     arrivals = lax.all_to_all(
-        outgoing.reshape(N_GRP, CAP, COLS), ("x", "c"), 0, 0, tiled=True
-    ).reshape(N_GRP * CAP, COLS)
+        outgoing.reshape(N_GRP, CAP, NEAR), ("x", "c"), 0, 0, tiled=True
+    ).reshape(N_GRP * CAP, NEAR)
+    arrivals, spread = lax.optimization_barrier((arrivals, spread))
     arrivals = lax.all_gather(arrivals, "z", axis=0, tiled=False)
-    by_z, by_x = experts(arrivals, norm_gain[None], w_gate[0], w_up[0], w_down[0])
+    others = select(lax.all_to_all(spread, "z", 0, 0, tiled=True), out_table)
+    others = lax.all_to_all(
+        others.reshape(N_GRP, CAP, N_Z * FAR), ("x", "c"), 0, 0, tiled=True
+    ).reshape(N_GRP * CAP, N_Z * FAR)
+    by_z, by_x = experts(
+        arrivals, others, norm_gain[None], w_gate[0], w_up[0], w_down[0]
+    )
     by_z = lax.psum_scatter(
         by_z.reshape(N_Z * N_GRP * CAP, HALF), "z", scatter_dimension=0, tiled=True
     )

time: 293 us -> 280 us (0.956)
  waiting for transfers between devices: 99.8 us -> 48.3 us
  blocking collectives: 84.2 us -> 121 us
    all_gather x1, waiting for transfers between devices: 48.3 us -> 1.5 us  [per_device(): arrivals = lax.all_gather(arrivals, 'z', axis=0, tiled=False)]
    all_to_all x1 -> x3, blocking collectives: 13.9 us -> 51.9 us  [the longest x1 20.6 us: per_device(): lax.all_to_all(others.reshape(N_GRP, CAP, N_Z * FAR), ('x', 'c'), 0, 0, t...]
    all_to_all x1, waiting for transfers between devices: 9.63 us -> 6.02 us  [per_device(): lax.all_to_all(jnp.broadcast_to(queries, (N_Z,) + queries.shape[1:]), 'z'...]
    reduce_scatter x1, waiting for transfers between devices: 9.77 us -> 6.47 us  [per_device(): lax.psum_scatter(by_z.reshape(N_Z * N_GRP * CAP, HALF), 'z', scatter_dime...]
  transfers between devices with their start and end apart: 12 -> 12, of which waited for: 7 -> 9; matrix products, arithmetic and copies ran while one was open for 3% -> 3% of each run, Pallas kernels for 9% -> 11%
where the time goes in v5:
time: 280 us; the launch traced here: 278 us
  blocking collectives  121 us (43%)
  waiting for transfers between devices  48.3 us (17%)
  Pallas kernels  47.7 us (17%)
  starting transfers between devices  35 us (12%)
  between operations  13.3 us (5%)
  local copies, waits for them, and re-layouts  9.9 us (4%)
    all_to_all x1, blocking collectives, per_device(): lax.all_to_all(by_x.reshape(N_GRP, CAP, D // 2), ('x', 'c'), 0, 0, tiled=...  31.7 us
    all_to_all x1, blocking collectives, per_device(): parts = lax.all_to_all(parts, 'z', 0, 0, tiled=True)  23.8 us
    all_to_all x1, blocking collectives, per_device(): lax.all_to_all(others.reshape(N_GRP, CAP, N_Z * FAR), ('x', 'c'), 0, 0, t...  20.6 us
    all_to_all x1, blocking collectives, per_device(): others = select(lax.all_to_all(spread, 'z', 0, 0, tiled=True), out_table)  18.8 us
    all_to_all x1, blocking collectives, per_device(): return finish(lax.all_to_all(tail, 'z', 0, 0, tiled=True))[None]  14.2 us
    all_to_all x1, waiting for transfers between devices, per_device(): attended = lax.all_to_all(combine(parts), 'z', 0, 0, tiled=True)  13.4 us
    pallas_call x1, Pallas kernels, rest_attention(): pl.pallas_call(rest_kernel, grid_spec=attention_specs([square, square], [...  13.2 us
    all_to_all x1, blocking collectives, per_device(): lax.all_to_all(outgoing.reshape(N_GRP, CAP, NEAR), ('x', 'c'), 0, 0, tile...  12.4 us
  transfers between devices with their start and end apart: 12, of which 9 were waited for; matrix products, arithmetic and copies ran while one was open for 3% of the time, Pallas kernels for 11%

profile of v5, /device:TPU:2, one launch (start us, length us, event | category | flops | bytes accessed | tf_op | source)
XLA Modules:
  0.0 278.3 jit_solution(4857580219308463608)
XLA Ops:
  6.5 1.8 broadcast_in_dim.80
  8.4 8.5 %all-to-all-start = ((bf16[8,128,256]{2,1,0:T(8,128)(2,1)}), bf16[8,128,256]{2,1,0:T(8,128)(2,1)S(1)}, u32[]{:S(2)}, u32[]{:S(2)}) async-start(bf16[8,128,256]{2,1,0:T(8,128)(2,1)} %broadcast_in_dim.80), calls=%async_computation | async-start | bytes 1048576 | tf_op jit(solution)/shard_map/all_to_all | solution.py:409
  16.8 3.6 %dequantize.1 = (bf16[2,1024,128]{2,1,0:T(8,128)(2,1)}, bf16[2,1024,128]{2,1,0:T(8,128)(2,1)}, bf16[2,1024,128]{2,1,0:T(8,128)(2,1)}, bf16[2,1024,128]{2,1,0:T(8,128)(2,1)}) custom-call(s32[1]{0:T(128)} %bitcast.11.y_ref, f32[8,8]{1,0:T(8,128)} %bitcast.73, bf16[1024,1024]{1,0:T(8,128)(2,1)} %bitcast.48), custom_call_target="tpu_custom_call" | custom-call | flops 1048576 | bytes 4194304 | tf_op jit(solution)/shard_map/dequantize/pallas_call | solution.py:56
  20.4 1.6 collective-permute-start
  22.0 1.7 collective-permute-start.1
  23.6 2.0 collective-permute-start.2
  25.6 0.5 broadcast.144
  26.2 0.7 reduce.4
  26.8 0.1 reshape_squeeze.3
  26.9 0.1 copy.57
  27.1 0.6 gather_fusion
  27.7 0.5 and_convert_fusion.last_ref
  28.2 0.1 fusion.2
  28.3 6.0 %all-to-all-done.q_ref = bf16[8,128,256]{2,1,0:T(8,128)(2,1)S(1)} async-done(((bf16[8,128,256]{2,1,0:T(8,128)(2,1)}), bf16[8,128,256]{2,1,0:T(8,128)(2,1)S(1)}, u32[]{:S(2)}, u32[]{:S(2)}) %all-to-all-start) | async-done | bytes 524320 | tf_op jit(solution)/shard_map/all_to_all | solution.py:409
  34.3 0.9 copy.53
  35.2 3.4 %all-to-all-start.1 = ((bf16[8,36,512]{2,1,0:T(8,128)(2,1)}), bf16[8,36,512]{2,1,0:T(8,128)(2,1)S(1)}, u32[]{:S(2)}, u32[]{:S(2)}) async-start(bf16[8,36,512]{2,1,0:T(8,128)(2,1)} %copy.53), calls=%async_computation.1 | async-start | bytes 655360 | tf_op jit(solution)/shard_map/all_to_all | solution.py:434
  38.7 0.0 all-gather.5.cloned.1.call-start
  38.7 0.7 broadcast_in_dim.85
  39.4 6.5 %own_attention.1 = (f32[8,256,128]{2,1,0:T(8,128)}, f32[8,256,128]{2,1,0:T(8,128)}) custom-call(s32[4]{0:T(128)} %and_convert_fusion.last_ref, bf16[8,128,256]{2,1,0:T(8,128)(2,1)} %copy-done.5, f32[4,1,1024]{2,1,0:T(1,128)} %bitcast.69, bf16[2,1024,128]{2,1,0:T(8,128)(2,1)} %get-tuple-element.27.kv0), custom_call_target="tpu_custom_call" | custom-call | flops 3221225472 | bytes 8388608 | tf_op jit(solution)/shard_map/own_attention/pallas_call | solution.py:160
  45.9 0.1 collective-permute-done.1.kv3
  45.9 1.9 collective-permute-done.2.kv2
  47.8 13.2 %rest_attention.1 = bf16[8,272,128]{2,1,0:T(8,128)(2,1)} custom-call(s32[4]{0:T(128)} %and_convert_fusion.last_ref, bf16[8,128,256]{2,1,0:T(8,128)(2,1)} %copy-done.5, f32[4,1,1024]{2,1,0:T(1,128)} %bitcast.70, bf16[2,1024,128]{2,1,0:T(8,128)(2,1)} %collective-permute-done.kv1, bf16[2,1024,128]{2,1,0:T(8,128)(2,1)} %collective-permute-done.1.kv3, ...), custom_call_target="tpu_custom_call" | custom-call | flops 8589934592 | bytes 8388608 | tf_op jit(solution)/shard_map/rest_attention/pallas_call | solution.py:175
  61.0 0.7 slice.6
  61.7 0.0 all-gather.5.cloned.1.call-update
  61.8 23.8 %all_to_all.60.in_ref = bf16[8,272,128]{2,1,0:T(8,128)(2,1)} all-to-all(bf16[8,272,128]{2,1,0:T(8,128)(2,1)} %rest_attention.1), channel_id=1, replica_groups=mesh['y'=4,'z'=8,'x'=4,'c'=2] {'z'}, dimensions={0} | all-to-all | bytes 1114112 | tf_op jit(solution)/shard_map/all_to_all | solution.py:457
  85.5 2.4 combine.1
  87.9 3.5 %all-to-all-start.3 = ((bf16[8,128,256]{2,1,0:T(8,128)(2,1)}), bf16[8,128,256]{2,1,0:T(8,128)(2,1)S(1)}, u32[]{:S(2)}, u32[]{:S(2)}) async-start(bf16[8,128,256]{2,1,0:T(8,128)(2,1)} %combine.1), calls=%async_computation.3 | async-start | bytes 1048576 | tf_op jit(solution)/shard_map/all_to_all | solution.py:458
  91.4 0.1 compare_reduce_fusion
  91.5 0.3 reduce_window_sum.11
  91.8 0.1 eq.57
  91.9 0.2 copy.50
  92.1 0.1 fusion.1
  92.2 0.1 copy.51
  92.4 13.4 %all-to-all-done.3.a_ref = bf16[8,128,256]{2,1,0:T(8,128)(2,1)S(1)} async-done(((bf16[8,128,256]{2,1,0:T(8,128)(2,1)}), bf16[8,128,256]{2,1,0:T(8,128)(2,1)S(1)}, u32[]{:S(2)}, u32[]{:S(2)}) %all-to-all-start.3) | async-done | bytes 524320 | tf_op jit(solution)/shard_map/all_to_all | solution.py:458
  105.8 0.8 copy-done.1
  106.6 2.9 %project.1 = bf16[4,128,512]{2,1,0:T(8,128)(2,1)} custom-call(bf16[8,128,256]{2,1,0:T(8,128)(2,1)} %copy-done.1, bf16[8,8,32,512]{3,2,1,0:T(8,128)(2,1)} %bitcast.49, bf16[128,512]{1,0:T(8,128)(2,1)} %copy-done.4), custom_call_target="tpu_custom_call" | custom-call | tf_op jit(solution)/shard_map/project/pallas_call | solution.py:226
  109.6 5.1 %all-to-all-start.4 = ((bf16[4,128,512]{2,1,0:T(8,128)(2,1)}), bf16[4,128,512]{2,1,0:T(8,128)(2,1)S(1)}, u32[]{:S(2)}, u32[]{:S(2)}) async-start(bf16[4,128,512]{2,1,0:T(8,128)(2,1)} %project.1), calls=%async_computation.4 | async-start | bytes 1048576 | tf_op jit(solution)/shard_map/all_to_all | solution.py:459
  114.7 0.1 copy.49
  114.8 0.7 fusion
  115.6 0.8 copy.54.table_ref
  116.4 6.4 %all-to-all-done.4.parts_ref = bf16[4,128,512]{2,1,0:T(8,128)(2,1)S(1)} async-done(((bf16[4,128,512]{2,1,0:T(8,128)(2,1)}), bf16[4,128,512]{2,1,0:T(8,128)(2,1)S(1)}, u32[]{:S(2)}, u32[]{:S(2)}) %all-to-all-start.4) | async-done | bytes 524320 | tf_op jit(solution)/shard_map/all_to_all | solution.py:459
  122.8 0.8 copy-done.2
  123.6 2.2 dispatch.1
  125.8 12.4 %all_to_all.61 = bf16[8,64,384]{2,1,0:T(8,128)(2,1)} all-to-all(bf16[8,64,384]{2,1,0:T(8,128)(2,1)} %bitcast.61), channel_id=1, replica_groups=mesh['y'=4,'z'=8,'x'=4,'c'=2] {'x','c'}, dimensions={0} | all-to-all | bytes 786432 | tf_op jit(solution)/shard_map/all_to_all | solution.py:462
  138.2 0.0 all-gather.7.cloned.1.call-update
  138.2 0.0 reduce-scatter.2.cloned.1.call-start
  138.2 18.8 %all_to_all.62.parts_ref = bf16[8,128,128]{2,1,0:T(8,128)(2,1)} all-to-all(bf16[8,128,128]{2,1,0:T(8,128)(2,1)} %get-tuple-element.36), channel_id=1, replica_groups=mesh['y'=4,'z'=8,'x'=4,'c'=2] {'z'}, dimensions={0} | all-to-all | bytes 524288 | tf_op jit(solution)/shard_map/all_to_all | solution.py:467
  157.1 2.4 select.17
  159.4 20.6 %all_to_all.63 = bf16[8,64,1024]{2,1,0:T(8,128)(2,1)} all-to-all(bf16[8,64,1024]{2,1,0:T(8,128)(2,1)} %bitcast.45), channel_id=1, replica_groups=mesh['y'=4,'z'=8,'x'=4,'c'=2] {'x','c'}, dimensions={0} | all-to-all | bytes 2097152 | tf_op jit(solution)/shard_map/all_to_all | solution.py:468
  180.1 1.5 all-gather.7.cloned.1.call-done
  181.6 8.2 %experts.1 = (bf16[8,512,256]{2,1,0:T(8,128)(2,1)}, bf16[512,2048]{1,0:T(8,128)(2,1)}) custom-call(bf16[8,512,384]{2,1,0:T(8,128)(2,1)} %bitcast.46, bf16[512,1024]{1,0:T(8,128)(2,1)} %bitcast.44, f32[1,4096]{1,0:T(1,128)} %bitcast.68, bf16[192,4096]{1,0:T(8,128)(2,1)} %bitcast.53, bf16[192,4096]{1,0:T(8,128)(2,1)} %bitcast.54, bf16[192,4096]{1,0:T(8,128)(2,1)} %bitcast.55), custom_call_target="tpu_custom_call" | custom-call | tf_op jit(solution)/shard_map/experts/pallas_call | solution.py:306
  189.8 31.7 %all_to_all.64 = bf16[8,64,2048]{2,1,0:T(8,128)(2,1)} all-to-all(bf16[8,64,2048]{2,1,0:T(8,128)(2,1)} %bitcast.50), channel_id=1, replica_groups=mesh['y'=4,'z'=8,'x'=4,'c'=2] {'x','c'}, dimensions={0} | all-to-all | bytes 4194304 | tf_op jit(solution)/shard_map/all_to_all | solution.py:477
  221.5 6.5 %reduce-scatter.2.cloned.1.call-done = bf16[512,256]{1,0:T(8,128)(2,1)} async-done(((bf16[4096,256]{1,0:T(8,128)(2,1)}), bf16[512,256]{1,0:T(8,128)(2,1)}) %reduce-scatter.2.cloned.1.call-update) | async-done | bytes 262160 | tf_op jit(solution)/shard_map/reduce_scatter | solution.py:474
  228.0 4.8 %all-to-all-start.9 = ((bf16[8,64,256]{2,1,0:T(8,128)(2,1)}), bf16[8,64,256]{2,1,0:T(8,128)(2,1)S(1)}, u32[]{:S(2)}, u32[]{:S(2)}) async-start(bf16[8,64,256]{2,1,0:T(8,128)(2,1)} %bitcast.62), calls=%async_computation.10 | async-start | bytes 524288 | tf_op jit(solution)/shard_map/all_to_all | solution.py:482
  232.8 2.6 mix.1.mixed_ref
  235.4 3.5 %all-to-all-done.9 = bf16[8,64,256]{2,1,0:T(8,128)(2,1)S(1)} async-done(((bf16[8,64,256]{2,1,0:T(8,128)(2,1)}), bf16[8,64,256]{2,1,0:T(8,128)(2,1)S(1)}, u32[]{:S(2)}, u32[]{:S(2)}) %all-to-all-start.9) | async-done | bytes 262176 | tf_op jit(solution)/shard_map/all_to_all | solution.py:482
  238.9 0.7 copy-done.3
  239.6 2.2 mix_rest.1
  241.8 4.3 %all-to-all-start.10 = ((bf16[4,32,2304]{2,1,0:T(8,128)(2,1)}), bf16[4,32,2304]{2,1,0:T(8,128)(2,1)S(1)}, u32[]{:S(2)}, u32[]{:S(2)}) async-start(bf16[4,32,2304]{2,1,0:T(8,128)(2,1)} %bitcast.47), calls=%async_computation.11 | async-start | bytes 1179648 | tf_op jit(solution)/shard_map/all_to_all | solution.py:488
  246.1 0.8 constant_dynamic-slice_fusion
  246.9 9.1 %all-to-all-done.10 = bf16[4,32,2304]{2,1,0:T(8,128)(2,1)S(1)} async-done(((bf16[4,32,2304]{2,1,0:T(8,128)(2,1)}), bf16[4,32,2304]{2,1,0:T(8,128)(2,1)S(1)}, u32[]{:S(2)}, u32[]{:S(2)}) %all-to-all-start.10) | async-done | bytes 589856 | tf_op jit(solution)/shard_map/all_to_all | solution.py:488
  255.9 0.1 reduce_sum.22
  256.1 14.2 %all_to_all.65.in_ref = bf16[8,4,2816]{2,1,0:T(4,128)(2,1)} all-to-all(bf16[8,4,2816]{2,1,0:T(4,128)(2,1)S(1)} %reshape.130), channel_id=1, replica_groups=mesh['y'=4,'z'=8,'x'=4,'c'=2] {'z'}, dimensions={0} | all-to-all | bytes 360448 | tf_op jit(solution)/shard_map/all_to_all | solution.py:491
  270.2 1.6 finish.1
  (43 shorter events, 0.4 us)
Async XLA Ops:
  6.5 19.1 %copy-start = (bf16[256,4096]{1,0:T(8,128)(2,1)S(1)}, bf16[256,4096]{1,0:T(8,128)(2,1)}, u32[]{:S(2)}) copy-start(bf16[256,4096]{1,0:T(8,128)(2,1)} %param.17) | copy-start | bytes 6291460
  6.5 19.6 %copy-start.9 = (s32[1,1,256]{2,1,0:T(1,128)S(1)}, s32[1,1,256]{2,1,0:T(1,128)}, u32[]{:S(2)}) copy-start(s32[1,1,256]{2,1,0:T(1,128)} %param.15) | copy-start | bytes 3076
  6.5 20.4 %copy-start.6 = (bf16[1,4,4096]{2,1,0:T(4,128)(2,1)S(1)}, bf16[1,4,4096]{2,1,0:T(4,128)(2,1)}, u32[]{:S(2)}) copy-start(bf16[1,4,4096]{2,1,0:T(4,128)(2,1)} %param.16) | copy-start | bytes 98308
  8.4 26.0 %all-to-all-start = ((bf16[8,128,256]{2,1,0:T(8,128)(2,1)}), bf16[8,128,256]{2,1,0:T(8,128)(2,1)S(1)}, u32[]{:S(2)}, u32[]{:S(2)}) async-start(bf16[8,128,256]{2,1,0:T(8,128)(2,1)} %broadcast_in_dim.80), calls=%async_computation | async-start | bytes 1048576 | tf_op jit(solution)/shard_map/all_to_all | solution.py:409
  20.4 25.5 %collective-permute-start = (bf16[2,1024,128]{2,1,0:T(8,128)(2,1)}, bf16[2,1024,128]{2,1,0:T(8,128)(2,1)}, u32[]{:S(2)}, u32[]{:S(2)}) collective-permute-start(bf16[2,1024,128]{2,1,0:T(8,128)(2,1)} %get-tuple-element.24), channel_id=1, source_target_pairs={{0,64},{64,128},{128,192},{192,0},{1,65},{65,129},{129,193},{193,1... | collective-permute-start | bytes 1572872 | tf_op jit(solution)/shard_map/ppermute | solution.py:413
  22.0 24.0 %collective-permute-start.1 = (bf16[2,1024,128]{2,1,0:T(8,128)(2,1)}, bf16[2,1024,128]{2,1,0:T(8,128)(2,1)}, u32[]{:S(2)}, u32[]{:S(2)}) collective-permute-start(bf16[2,1024,128]{2,1,0:T(8,128)(2,1)} %get-tuple-element.25), channel_id=1, source_target_pairs={{0,192},{64,0},{128,64},{192,128},{1,193},{65,1},{129,65},{193,129... | collective-permute-start | bytes 1572872 | tf_op jit(solution)/shard_map/ppermute | solution.py:413
  23.6 24.1 %collective-permute-start.2 = (bf16[2,1024,128]{2,1,0:T(8,128)(2,1)}, bf16[2,1024,128]{2,1,0:T(8,128)(2,1)}, u32[]{:S(2)}, u32[]{:S(2)}) collective-permute-start(bf16[2,1024,128]{2,1,0:T(8,128)(2,1)} %get-tuple-element.26), channel_id=1, source_target_pairs={{0,128},{64,192},{128,0},{192,64},{1,129},{65,193},{129,1},{193,65... | collective-permute-start | bytes 1572872 | tf_op jit(solution)/shard_map/ppermute | solution.py:413
  34.3 5.1 %copy-start.5 = (bf16[8,128,256]{2,1,0:T(8,128)(2,1)}, bf16[8,128,256]{2,1,0:T(8,128)(2,1)S(1)}, u32[]{:S(2)}) copy-start(bf16[8,128,256]{2,1,0:T(8,128)(2,1)S(1)} %all-to-all-done.q_ref) | copy-start | bytes 1572868
  35.2 25.8 %all-to-all-start.1 = ((bf16[8,36,512]{2,1,0:T(8,128)(2,1)}), bf16[8,36,512]{2,1,0:T(8,128)(2,1)S(1)}, u32[]{:S(2)}, u32[]{:S(2)}) async-start(bf16[8,36,512]{2,1,0:T(8,128)(2,1)} %copy.53), calls=%async_computation.1 | async-start | bytes 655360 | tf_op jit(solution)/shard_map/all_to_all | solution.py:434
  38.7 67.2 %all-gather.5.cloned.1.call-start = ((), (), s32[]{:S(2)}) async-start(), calls=%async_computation.14 | async-start | bytes 2359296 | tf_op jit(solution)/shard_map/all_gather | solution.py:456
  61.0 30.4 %copy-start.7 = (s32[1,128,8]{1,2,0:T(8,128)S(1)}, s32[1,128,8]{1,2,0:T(8,128)}, u32[]{:S(2)}) copy-start(s32[1,128,8]{1,2,0:T(8,128)} %param.19) | copy-start | bytes 12292
  61.0 31.0 %copy-start.8 = (f32[1,128,8]{1,2,0:T(8,128)S(1)}, f32[1,128,8]{1,2,0:T(8,128)}, u32[]{:S(2)}) copy-start(f32[1,128,8]{1,2,0:T(8,128)} %param.20) | copy-start | bytes 12292
  87.9 18.0 %all-to-all-start.3 = ((bf16[8,128,256]{2,1,0:T(8,128)(2,1)}), bf16[8,128,256]{2,1,0:T(8,128)(2,1)S(1)}, u32[]{:S(2)}, u32[]{:S(2)}) async-start(bf16[8,128,256]{2,1,0:T(8,128)(2,1)} %combine.1), calls=%async_computation.3 | async-start | bytes 1048576 | tf_op jit(solution)/shard_map/all_to_all | solution.py:458
  92.4 13.5 %copy-start.4 = (bf16[128,512]{1,0:T(8,128)(2,1)}, bf16[128,512]{1,0:T(8,128)(2,1)S(1)}, u32[]{:S(2)}) copy-start(bf16[128,512]{1,0:T(8,128)(2,1)S(1)} %constant_dynamic-update-slice_fusion.resid_ref) | copy-start | bytes 393220
  105.8 0.8 copy-start.1
  109.6 13.2 %all-to-all-start.4 = ((bf16[4,128,512]{2,1,0:T(8,128)(2,1)}), bf16[4,128,512]{2,1,0:T(8,128)(2,1)S(1)}, u32[]{:S(2)}, u32[]{:S(2)}) async-start(bf16[4,128,512]{2,1,0:T(8,128)(2,1)} %project.1), calls=%async_computation.4 | async-start | bytes 1048576 | tf_op jit(solution)/shard_map/all_to_all | solution.py:459
  114.7 66.9 %all-gather.7.cloned.1.call-start = ((), (), s32[]{:S(2)}) async-start(), calls=%async_computation.15 | async-start | bytes 3538944 | tf_op jit(solution)/shard_map/all_gather | solution.py:466
  122.8 0.8 copy-start.2
  138.2 89.8 %reduce-scatter.2.cloned.1.call-start = ((), (), s32[]{:S(2)}) async-start(), calls=%async_computation.13 | async-start | bytes 2359296 | tf_op jit(solution)/shard_map/reduce_scatter | solution.py:474
  228.0 10.9 %all-to-all-start.9 = ((bf16[8,64,256]{2,1,0:T(8,128)(2,1)}), bf16[8,64,256]{2,1,0:T(8,128)(2,1)S(1)}, u32[]{:S(2)}, u32[]{:S(2)}) async-start(bf16[8,64,256]{2,1,0:T(8,128)(2,1)} %bitcast.62), calls=%async_computation.10 | async-start | bytes 524288 | tf_op jit(solution)/shard_map/all_to_all | solution.py:482
  238.9 0.7 copy-start.3
  241.8 14.1 %all-to-all-start.10 = ((bf16[4,32,2304]{2,1,0:T(8,128)(2,1)}), bf16[4,32,2304]{2,1,0:T(8,128)(2,1)S(1)}, u32[]{:S(2)}, u32[]{:S(2)}) async-start(bf16[4,32,2304]{2,1,0:T(8,128)(2,1)} %bitcast.47), calls=%async_computation.11 | async-start | bytes 1179648 | tf_op jit(solution)/shard_map/all_to_all | solution.py:488
Sparse Core Ops, SparseCore 0:
  61.9 26.4 all-gather.4
  138.3 43.2 all-gather.6
  189.9 38.0 reduce-scatter.1

commit v6 on v5

--- a/solution.py
+++ b/solution.py
@@ -217,24 +217,22 @@
     for z in range(N_Z):
         w_rows = jnp.concatenate([w_ref[g, z] for g in range(N_GRP)], axis=0)
         acc = acc + jnp.dot(a_ref[z], w_rows, preferred_element_type=f32)
-    done = acc.astype(bf16)
-    for y in range(N_Y):
-        out_ref[y] = done
+    out_ref[...] = acc.astype(bf16)
 
 
 def project(attended, w_cols, resid_rows):
     return pl.pallas_call(
         project_kernel,
-        out_shape=jax.ShapeDtypeStruct((N_Y, WIN, COLS), bf16),
+        out_shape=jax.ShapeDtypeStruct((WIN, COLS), bf16),
         compiler_params=params(),
         name="project",
     )(attended, w_cols, resid_rows)
 
 
-def dispatch_kernel(parts_ref, table_ref, stream_ref, out_ref, spread_ref):
-    total = parts_ref[0].astype(f32)
-    for y in range(1, N_Y):
-        total = total + parts_ref[y].astype(f32)
+def dispatch_kernel(table_ref, own_ref, one_ref, two_ref, three_ref, stream_ref, out_ref, spread_ref):
+    total = (own_ref[...].astype(f32) + two_ref[...].astype(f32)) + (
+        one_ref[...].astype(f32) + three_ref[...].astype(f32)
+    )
     stream = total.astype(bf16)
     stream_ref[...] = stream
     out_ref[...] = jnp.dot(
@@ -244,7 +242,7 @@
         spread_ref[z] = stream[:, NEAR:]
 
 
-def dispatch(parts, table):
+def dispatch(table, *parts):
     return pl.pallas_call(
         dispatch_kernel,
         out_shape=(
@@ -254,7 +252,7 @@
         ),
         compiler_params=params(),
         name="dispatch",
-    )(parts, table)
+    )(table, *parts)
 
 
 def select_kernel(parts_ref, table_ref, out_ref):
@@ -350,17 +348,18 @@
     )(table, parts)
 
 
-def mix_rest_kernel(table_ref, parts_ref, mixed_ref, out_ref):
-    out_ref[:, : D // 2] = mixed_ref[...]
-    out_ref[:, D // 2 :] = jnp.dot(
-        table_ref[...], parts_ref[...], preferred_element_type=f32
-    ).astype(bf16)
+def mix_rest_kernel(table_ref, parts_ref, mixed_ref, *out_refs):
+    rest = jnp.dot(table_ref[...], parts_ref[...], preferred_element_type=f32).astype(bf16)
+    rows = WIN // N_Y
+    for d, out_ref in enumerate(out_refs):
+        out_ref[:, : D // 2] = mixed_ref[d * rows : (d + 1) * rows, :]
+        out_ref[:, D // 2 :] = rest[d * rows : (d + 1) * rows]
 
 
 def mix_rest(table, parts, mixed):
     return pl.pallas_call(
         mix_rest_kernel,
-        out_shape=jax.ShapeDtypeStruct((WIN, D // 2 + HALF), bf16),
+        out_shape=[jax.ShapeDtypeStruct((WIN // N_Y, D // 2 + HALF), bf16)] * N_Y,
         compiler_params=params(),
         name="mix_rest",
     )(table, parts, mixed)
@@ -385,6 +384,10 @@
         compiler_params=params(),
         name="finish",
     )(parts)
+
+
+def over_y(value, d):
+    return lax.ppermute(value, "y", [(i, (i + d) % N_Y) for i in range(N_Y)])
 
 
 def per_device(
@@ -410,8 +413,7 @@
         jnp.broadcast_to(queries, (N_Z,) + queries.shape[1:]), "z", 0, 0, tiled=True
     )
     kv_from = {
-        d: lax.ppermute(chunks[d], "y", [(i, (i + d) % N_Y) for i in range(N_Y)])
-        for d in (1, 3, 2)
+        d: over_y(chunks[d], d) for d in (1, 3, 2)
     }
 
     blocks = CTX_LOCAL // BLOCK
@@ -444,6 +446,9 @@
     out_table = in_slot.astype(bf16).reshape(N_GRP * CAP, WIN)
     back_table = jnp.where(in_slot, weight[:, None, :], 0.0).astype(bf16)
     back_table = back_table.reshape(N_GRP * CAP, WIN).T
+    back_table = lax.dynamic_slice_in_dim(
+        jnp.concatenate([back_table, back_table], axis=0), y_pos * rows, WIN, 0
+    )
 
     acc, stat = own_attention(last, queries_mine, bias, kv_own)
     parts = rest_attention(
@@ -456,8 +461,9 @@
     w_cols = lax.all_gather(early[:, :part], ("x", "c"), axis=0, tiled=False)
     parts = lax.all_to_all(parts, "z", 0, 0, tiled=True)
     attended = lax.all_to_all(combine(parts), "z", 0, 0, tiled=True)
-    projected = lax.all_to_all(project(attended, w_cols, resid_rows), "y", 0, 0, tiled=True)
-    stream, outgoing, spread = dispatch(projected, out_table)
+    projected = project(attended, w_cols, resid_rows)
+    shifted = [over_y(projected, d) for d in (1, 2, 3)]
+    stream, outgoing, spread = dispatch(out_table, projected, *shifted)
 
     arrivals = lax.all_to_all(
         outgoing.reshape(N_GRP, CAP, NEAR), ("x", "c"), 0, 0, tiled=True
@@ -482,11 +488,13 @@
     by_z = lax.all_to_all(
         by_z.reshape(N_GRP, CAP, HALF), ("x", "c"), 0, 0, tiled=True
     ).reshape(N_GRP * CAP, HALF)
-    mixture = mix_rest(back_table, by_z, mixed).reshape(N_Y, rows, -1)
+    mixture, *others = mix_rest(back_table, by_z, mixed)
 
     stream_rows = lax.dynamic_slice_in_dim(stream, y_pos * rows, rows, 0)
-    mixture = lax.all_to_all(mixture, "y", 0, 0, tiled=True)
-    mixture = jnp.sum(mixture.astype(f32), axis=0).astype(bf16)
+    mixture = mixture.astype(f32)
+    for d, other in enumerate(others, 1):
+        mixture = mixture + over_y(other, d).astype(f32)
+    mixture = mixture.astype(bf16)
     tail = jnp.concatenate([mixture, stream_rows], axis=1).reshape(N_Z, own_rows, -1)
     return finish(lax.all_to_all(tail, "z", 0, 0, tiled=True))[None]
 

time: 280 us -> 276 us (0.986)
  waiting for transfers between devices: 48.3 us -> 40.6 us
    all_to_all x2 -> x0, waiting for transfers between devices: 15.4 us -> none  [the longest x1 9.05 us: per_device(): mixture = lax.all_to_all(mixture, 'y', 0, 0, tiled=True)]
    ppermute x3 -> x9, starting transfers between devices: 5.22 us -> 16.2 us  [over_y(): return lax.ppermute(value, 'y', [(i, (i + d) % N_Y) for i in range(N_Y)])]
    ppermute x3 -> x9, waiting for transfers between devices: 1.91 us -> 11.4 us  [over_y(): return lax.ppermute(value, 'y', [(i, (i + d) % N_Y) for i in range(N_Y)])]
    all_to_all x2 -> x0, starting transfers between devices: 9.46 us -> none  [the longest x1 5.13 us: per_device(): lax.all_to_all(project(attended, w_cols, resid_rows), 'y', 0, 0, tiled=True)]
  transfers between devices with their start and end apart: 12 -> 16, of which waited for: 9 -> 10; matrix products, arithmetic and copies ran while one was open for 3% -> 3% of each run, Pallas kernels for 11% -> 11%
where the time goes in v6:
time: 276 us; the launch traced here: 273 us
  blocking collectives  121 us (44%)
  Pallas kernels  47.7 us (17%)
  waiting for transfers between devices  40.6 us (15%)
  starting transfers between devices  36.4 us (13%)
  between operations  13.4 us (5%)
  local copies, waits for them, and re-layouts  10.5 us (4%)
  other arithmetic  3.71 us (1%)
    all_to_all x1, blocking collectives, per_device(): lax.all_to_all(by_x.reshape(N_GRP, CAP, D // 2), ('x', 'c'), 0, 0, tiled=...  31.2 us
    all_to_all x1, blocking collectives, per_device(): parts = lax.all_to_all(parts, 'z', 0, 0, tiled=True)  23.8 us
    all_to_all x1, blocking collectives, per_device(): lax.all_to_all(others.reshape(N_GRP, CAP, N_Z * FAR), ('x', 'c'), 0, 0, t...  20.5 us
    all_to_all x1, blocking collectives, per_device(): others = select(lax.all_to_all(spread, 'z', 0, 0, tiled=True), out_table)  19.1 us
    ppermute x9, starting transfers between devices, over_y(): return lax.ppermute(value, 'y', [(i, (i + d) % N_Y) for i in range(N_Y)])  16.2 us
    all_to_all x1, blocking collectives, per_device(): return finish(lax.all_to_all(tail, 'z', 0, 0, tiled=True))[None]  14.2 us
    pallas_call x1, Pallas kernels, rest_attention(): pl.pallas_call(rest_kernel, grid_spec=attention_specs([square, square], [...  13.2 us
    all_to_all x1, waiting for transfers between devices, per_device(): attended = lax.all_to_all(combine(parts), 'z', 0, 0, tiled=True)  12.6 us
  transfers between devices with their start and end apart: 16, of which 10 were waited for; matrix products, arithmetic and copies ran while one was open for 3% of the time, Pallas kernels for 11%

profile of v6, /device:TPU:2, one launch (start us, length us, event | category | flops | bytes accessed | tf_op | source)
XLA Modules:
  0.0 273.4 jit_solution(15005427193900880582)
XLA Ops:
  6.5 1.8 broadcast_in_dim.80
  8.4 8.5 %all-to-all-start = ((bf16[8,128,256]{2,1,0:T(8,128)(2,1)}), bf16[8,128,256]{2,1,0:T(8,128)(2,1)S(1)}, u32[]{:S(2)}, u32[]{:S(2)}) async-start(bf16[8,128,256]{2,1,0:T(8,128)(2,1)} %broadcast_in_dim.80), calls=%async_computation | async-start | bytes 1048576 | tf_op jit(solution)/shard_map/all_to_all | solution.py:412
  16.8 3.6 %dequantize.1 = (bf16[2,1024,128]{2,1,0:T(8,128)(2,1)}, bf16[2,1024,128]{2,1,0:T(8,128)(2,1)}, bf16[2,1024,128]{2,1,0:T(8,128)(2,1)}, bf16[2,1024,128]{2,1,0:T(8,128)(2,1)}) custom-call(s32[1]{0:T(128)} %bitcast.11.y_ref, f32[8,8]{1,0:T(8,128)} %bitcast.71, bf16[1024,1024]{1,0:T(8,128)(2,1)} %bitcast.46), custom_call_target="tpu_custom_call" | custom-call | flops 1048576 | bytes 4194304 | tf_op jit(solution)/shard_map/dequantize/pallas_call | solution.py:56
  20.5 1.6 collective-permute-start
  22.0 1.7 collective-permute-start.1
  23.7 2.0 collective-permute-start.2
  25.7 0.5 broadcast.144
  26.2 0.7 reduce.3
  26.9 0.1 reshape_squeeze.3
  27.0 0.1 copy.57
  27.1 0.6 gather_fusion
  27.7 0.6 and_convert_fusion.last_ref
  28.4 6.0 %all-to-all-done.q_ref = bf16[8,128,256]{2,1,0:T(8,128)(2,1)S(1)} async-done(((bf16[8,128,256]{2,1,0:T(8,128)(2,1)}), bf16[8,128,256]{2,1,0:T(8,128)(2,1)S(1)}, u32[]{:S(2)}, u32[]{:S(2)}) %all-to-all-start) | async-done | bytes 524320 | tf_op jit(solution)/shard_map/all_to_all | solution.py:412
  34.3 0.9 copy.53
  35.3 3.4 %all-to-all-start.1 = ((bf16[8,36,512]{2,1,0:T(8,128)(2,1)}), bf16[8,36,512]{2,1,0:T(8,128)(2,1)S(1)}, u32[]{:S(2)}, u32[]{:S(2)}) async-start(bf16[8,36,512]{2,1,0:T(8,128)(2,1)} %copy.53), calls=%async_computation.1 | async-start | bytes 655360 | tf_op jit(solution)/shard_map/all_to_all | solution.py:436
  38.8 0.7 broadcast_in_dim.85
  39.5 6.5 %own_attention.1 = (f32[8,256,128]{2,1,0:T(8,128)}, f32[8,256,128]{2,1,0:T(8,128)}) custom-call(s32[4]{0:T(128)} %and_convert_fusion.last_ref, bf16[8,128,256]{2,1,0:T(8,128)(2,1)} %copy-done.5, f32[4,1,1024]{2,1,0:T(1,128)} %bitcast.67, bf16[2,1024,128]{2,1,0:T(8,128)(2,1)} %get-tuple-element.31.kv0), custom_call_target="tpu_custom_call" | custom-call | flops 3221225472 | bytes 8388608 | tf_op jit(solution)/shard_map/own_attention/pallas_call | solution.py:160
  45.9 1.9 collective-permute-done.2.kv2
  47.9 13.2 %rest_attention.1 = bf16[8,272,128]{2,1,0:T(8,128)(2,1)} custom-call(s32[4]{0:T(128)} %and_convert_fusion.last_ref, bf16[8,128,256]{2,1,0:T(8,128)(2,1)} %copy-done.5, f32[4,1,1024]{2,1,0:T(1,128)} %bitcast.68, bf16[2,1024,128]{2,1,0:T(8,128)(2,1)} %collective-permute-done.kv1, bf16[2,1024,128]{2,1,0:T(8,128)(2,1)} %collective-permute-done.1.kv3, ...), custom_call_target="tpu_custom_call" | custom-call | flops 8589934592 | bytes 8388608 | tf_op jit(solution)/shard_map/rest_attention/pallas_call | solution.py:175
  61.1 0.7 slice.6
  61.9 23.8 %all_to_all.50.in_ref = bf16[8,272,128]{2,1,0:T(8,128)(2,1)} all-to-all(bf16[8,272,128]{2,1,0:T(8,128)(2,1)} %rest_attention.1), channel_id=1, replica_groups=mesh['y'=4,'z'=8,'x'=4,'c'=2] {'z'}, dimensions={0} | all-to-all | bytes 1114112 | tf_op jit(solution)/shard_map/all_to_all | solution.py:462
  85.6 2.4 combine.1
  88.0 3.5 %all-to-all-start.3 = ((bf16[8,128,256]{2,1,0:T(8,128)(2,1)}), bf16[8,128,256]{2,1,0:T(8,128)(2,1)S(1)}, u32[]{:S(2)}, u32[]{:S(2)}) async-start(bf16[8,128,256]{2,1,0:T(8,128)(2,1)} %combine.1), calls=%async_computation.3 | async-start | bytes 1048576 | tf_op jit(solution)/shard_map/all_to_all | solution.py:463
  91.6 0.1 compare_reduce_fusion
  91.7 0.3 reduce_window_sum.11
  92.1 0.2 copy.50
  92.2 0.1 fusion.2
  92.3 0.8 copy.51
  93.1 0.1 copy.49
  93.4 12.6 %all-to-all-done.3.a_ref = bf16[8,128,256]{2,1,0:T(8,128)(2,1)S(1)} async-done(((bf16[8,128,256]{2,1,0:T(8,128)(2,1)}), bf16[8,128,256]{2,1,0:T(8,128)(2,1)S(1)}, u32[]{:S(2)}, u32[]{:S(2)}) %all-to-all-start.3) | async-done | bytes 524320 | tf_op jit(solution)/shard_map/all_to_all | solution.py:463
  105.9 0.8 copy-done.1
  106.8 2.8 %project.1.own_ref = bf16[128,512]{1,0:T(8,128)(2,1)} custom-call(bf16[8,128,256]{2,1,0:T(8,128)(2,1)} %copy-done.1, bf16[8,8,32,512]{3,2,1,0:T(8,128)(2,1)} %bitcast.47, bf16[128,512]{1,0:T(8,128)(2,1)} %copy-done.4), custom_call_target="tpu_custom_call" | custom-call | tf_op jit(solution)/shard_map/project/pallas_call | solution.py:224
  109.6 3.3 %collective-permute-start.5 = (bf16[128,512]{1,0:T(8,128)(2,1)}, bf16[128,512]{1,0:T(8,128)(2,1)S(1)}, u32[]{:S(2)}, u32[]{:S(2)}) collective-permute-start(bf16[128,512]{1,0:T(8,128)(2,1)} %project.1.own_ref), channel_id=1, source_target_pairs={{0,192},{64,0},{128,64},{192,128},{1,193},{65,1},{129,65},{193,129... | collective-permute-start | bytes 393224 | tf_op jit(solution)/shard_map/ppermute | solution.py:390
  112.8 0.6 collective-permute-start.4
  113.4 1.4 collective-permute-start.3
  114.9 0.1 fusion
  115.0 0.8 copy.54.table_ref
  115.7 3.9 %collective-permute-done.4.two_ref = bf16[128,512]{1,0:T(8,128)(2,1)S(1)} collective-permute-done((bf16[128,512]{1,0:T(8,128)(2,1)}, bf16[128,512]{1,0:T(8,128)(2,1)S(1)}, u32[]{:S(2)}, u32[]{:S(2)}) %collective-permute-start.4) | collective-permute-done | bytes 131104 | tf_op jit(solution)/shard_map/ppermute | solution.py:390
  119.6 1.3 collective-permute-done.3.one_ref
  120.9 0.6 copy-done.8
  121.6 2.3 dispatch.1
  123.8 12.4 %all_to_all.51 = bf16[8,64,384]{2,1,0:T(8,128)(2,1)} all-to-all(bf16[8,64,384]{2,1,0:T(8,128)(2,1)} %bitcast.59), channel_id=1, replica_groups=mesh['y'=4,'z'=8,'x'=4,'c'=2] {'x','c'}, dimensions={0} | all-to-all | bytes 786432 | tf_op jit(solution)/shard_map/all_to_all | solution.py:468
  136.3 19.1 %all_to_all.52.parts_ref = bf16[8,128,128]{2,1,0:T(8,128)(2,1)} all-to-all(bf16[8,128,128]{2,1,0:T(8,128)(2,1)} %get-tuple-element.40), channel_id=1, replica_groups=mesh['y'=4,'z'=8,'x'=4,'c'=2] {'z'}, dimensions={0} | all-to-all | bytes 524288 | tf_op jit(solution)/shard_map/all_to_all | solution.py:473
  155.4 2.4 select.17
  157.8 20.5 %all_to_all.53 = bf16[8,64,1024]{2,1,0:T(8,128)(2,1)} all-to-all(bf16[8,64,1024]{2,1,0:T(8,128)(2,1)} %bitcast.44), channel_id=1, replica_groups=mesh['y'=4,'z'=8,'x'=4,'c'=2] {'x','c'}, dimensions={0} | all-to-all | bytes 2097152 | tf_op jit(solution)/shard_map/all_to_all | solution.py:474
  178.3 1.3 all-gather.7.cloned.1.call-done
  179.6 8.2 %experts.1 = (bf16[8,512,256]{2,1,0:T(8,128)(2,1)}, bf16[512,2048]{1,0:T(8,128)(2,1)}) custom-call(bf16[8,512,384]{2,1,0:T(8,128)(2,1)} %bitcast.45, bf16[512,1024]{1,0:T(8,128)(2,1)} %bitcast.43, f32[1,4096]{1,0:T(1,128)} %bitcast.66, bf16[192,4096]{1,0:T(8,128)(2,1)} %bitcast.51, bf16[192,4096]{1,0:T(8,128)(2,1)} %bitcast.52, bf16[192,4096]{1,0:T(8,128)(2,1)} %bitcast.53), custom_call_target="tpu_custom_call" | custom-call | tf_op jit(solution)/shard_map/experts/pallas_call | solution.py:304
  187.9 31.2 %all_to_all.54 = bf16[8,64,2048]{2,1,0:T(8,128)(2,1)} all-to-all(bf16[8,64,2048]{2,1,0:T(8,128)(2,1)} %bitcast.48), channel_id=1, replica_groups=mesh['y'=4,'z'=8,'x'=4,'c'=2] {'x','c'}, dimensions={0} | all-to-all | bytes 4194304 | tf_op jit(solution)/shard_map/all_to_all | solution.py:483
  219.1 6.6 %reduce-scatter.2.cloned.1.call-done = bf16[512,256]{1,0:T(8,128)(2,1)} async-done(((bf16[4096,256]{1,0:T(8,128)(2,1)}), bf16[512,256]{1,0:T(8,128)(2,1)}) %reduce-scatter.2.cloned.1.call-update) | async-done | bytes 262160 | tf_op jit(solution)/shard_map/reduce_scatter | solution.py:480
  225.7 4.7 %all-to-all-start.8 = ((bf16[8,64,256]{2,1,0:T(8,128)(2,1)}), bf16[8,64,256]{2,1,0:T(8,128)(2,1)S(1)}, u32[]{:S(2)}, u32[]{:S(2)}) async-start(bf16[8,64,256]{2,1,0:T(8,128)(2,1)} %bitcast.60), calls=%async_computation.9 | async-start | bytes 524288 | tf_op jit(solution)/shard_map/all_to_all | solution.py:488
  230.4 0.8 fusion.1.table_ref
  231.2 2.6 mix.1.mixed_ref
  233.8 2.7 all-to-all-done.8
  236.5 0.7 copy-done.2
  237.2 2.2 mix_rest.1
  239.4 1.4 collective-permute-start.6
  240.8 2.8 %collective-permute-start.7 = (bf16[32,2304]{1,0:T(8,128)(2,1)}, bf16[32,2304]{1,0:T(8,128)(2,1)S(1)}, u32[]{:S(2)}, u32[]{:S(2)}) collective-permute-start(bf16[32,2304]{1,0:T(8,128)(2,1)} %get-tuple-element.46), channel_id=1, source_target_pairs={{0,128},{64,192},{128,0},{192,64},{1,129},{65,193},{129,1},{193,65... | collective-permute-start | bytes 442376 | tf_op jit(solution)/shard_map/ppermute | solution.py:390
  243.5 1.5 collective-permute-start.8
  245.0 0.8 constant_dynamic-slice_fusion
  245.8 0.9 collective-permute-done.6
  246.7 3.4 %collective-permute-done.7 = bf16[32,2304]{1,0:T(8,128)(2,1)S(1)} collective-permute-done((bf16[32,2304]{1,0:T(8,128)(2,1)}, bf16[32,2304]{1,0:T(8,128)(2,1)S(1)}, u32[]{:S(2)}, u32[]{:S(2)}) %collective-permute-start.7) | collective-permute-done | bytes 147488 | tf_op jit(solution)/shard_map/ppermute | solution.py:390
  250.1 1.0 add_convert_fusion
  251.2 14.2 %all_to_all.55.in_ref = bf16[8,4,2816]{2,1,0:T(4,128)(2,1)} all-to-all(bf16[8,4,2816]{2,1,0:T(4,128)(2,1)S(1)} %reshape.126), channel_id=1, replica_groups=mesh['y'=4,'z'=8,'x'=4,'c'=2] {'z'}, dimensions={0} | all-to-all | bytes 360448 | tf_op jit(solution)/shard_map/all_to_all | solution.py:499
  265.3 1.6 finish.1
  (58 shorter events, 0.7 us)
Async XLA Ops:
  6.5 19.2 %copy-start = (bf16[256,4096]{1,0:T(8,128)(2,1)S(1)}, bf16[256,4096]{1,0:T(8,128)(2,1)}, u32[]{:S(2)}) copy-start(bf16[256,4096]{1,0:T(8,128)(2,1)} %param.17) | copy-start | bytes 6291460
  6.5 19.7 %copy-start.12 = (s32[1,1,256]{2,1,0:T(1,128)S(1)}, s32[1,1,256]{2,1,0:T(1,128)}, u32[]{:S(2)}) copy-start(s32[1,1,256]{2,1,0:T(1,128)} %param.15) | copy-start | bytes 3076
  6.5 20.4 %copy-start.9 = (bf16[1,4,4096]{2,1,0:T(4,128)(2,1)S(1)}, bf16[1,4,4096]{2,1,0:T(4,128)(2,1)}, u32[]{:S(2)}) copy-start(bf16[1,4,4096]{2,1,0:T(4,128)(2,1)} %param.16) | copy-start | bytes 98308
  8.4 26.0 %all-to-all-start = ((bf16[8,128,256]{2,1,0:T(8,128)(2,1)}), bf16[8,128,256]{2,1,0:T(8,128)(2,1)S(1)}, u32[]{:S(2)}, u32[]{:S(2)}) async-start(bf16[8,128,256]{2,1,0:T(8,128)(2,1)} %broadcast_in_dim.80), calls=%async_computation | async-start | bytes 1048576 | tf_op jit(solution)/shard_map/all_to_all | solution.py:412
  20.5 25.5 %collective-permute-start = (bf16[2,1024,128]{2,1,0:T(8,128)(2,1)}, bf16[2,1024,128]{2,1,0:T(8,128)(2,1)}, u32[]{:S(2)}, u32[]{:S(2)}) collective-permute-start(bf16[2,1024,128]{2,1,0:T(8,128)(2,1)} %get-tuple-element.28), channel_id=1, source_target_pairs={{0,64},{64,128},{128,192},{192,0},{1,65},{65,129},{129,193},{193,1... | collective-permute-start | bytes 1572872 | tf_op jit(solution)/shard_map/ppermute | solution.py:390
  22.0 23.9 %collective-permute-start.1 = (bf16[2,1024,128]{2,1,0:T(8,128)(2,1)}, bf16[2,1024,128]{2,1,0:T(8,128)(2,1)}, u32[]{:S(2)}, u32[]{:S(2)}) collective-permute-start(bf16[2,1024,128]{2,1,0:T(8,128)(2,1)} %get-tuple-element.29), channel_id=1, source_target_pairs={{0,192},{64,0},{128,64},{192,128},{1,193},{65,1},{129,65},{193,129... | collective-permute-start | bytes 1572872 | tf_op jit(solution)/shard_map/ppermute | solution.py:390
  23.7 24.1 %collective-permute-start.2 = (bf16[2,1024,128]{2,1,0:T(8,128)(2,1)}, bf16[2,1024,128]{2,1,0:T(8,128)(2,1)}, u32[]{:S(2)}, u32[]{:S(2)}) collective-permute-start(bf16[2,1024,128]{2,1,0:T(8,128)(2,1)} %get-tuple-element.30), channel_id=1, source_target_pairs={{0,128},{64,192},{128,0},{192,64},{1,129},{65,193},{129,1},{193,65... | collective-permute-start | bytes 1572872 | tf_op jit(solution)/shard_map/ppermute | solution.py:390
  34.3 5.1 %copy-start.5 = (bf16[8,128,256]{2,1,0:T(8,128)(2,1)}, bf16[8,128,256]{2,1,0:T(8,128)(2,1)S(1)}, u32[]{:S(2)}) copy-start(bf16[8,128,256]{2,1,0:T(8,128)(2,1)S(1)} %all-to-all-done.q_ref) | copy-start | bytes 1572868
  35.3 25.8 %all-to-all-start.1 = ((bf16[8,36,512]{2,1,0:T(8,128)(2,1)}), bf16[8,36,512]{2,1,0:T(8,128)(2,1)S(1)}, u32[]{:S(2)}, u32[]{:S(2)}) async-start(bf16[8,36,512]{2,1,0:T(8,128)(2,1)} %copy.53), calls=%async_computation.1 | async-start | bytes 655360 | tf_op jit(solution)/shard_map/all_to_all | solution.py:436
  38.7 67.2 %all-gather.5.cloned.1.call-start = ((), (), s32[]{:S(2)}) async-start(), calls=%async_computation.12 | async-start | bytes 2359296 | tf_op jit(solution)/shard_map/all_gather | solution.py:461
  61.1 30.5 %copy-start.10 = (s32[1,128,8]{1,2,0:T(8,128)S(1)}, s32[1,128,8]{1,2,0:T(8,128)}, u32[]{:S(2)}) copy-start(s32[1,128,8]{1,2,0:T(8,128)} %param.19) | copy-start | bytes 12292
  61.1 31.1 %copy-start.11 = (f32[1,128,8]{1,2,0:T(8,128)S(1)}, f32[1,128,8]{1,2,0:T(8,128)}, u32[]{:S(2)}) copy-start(f32[1,128,8]{1,2,0:T(8,128)} %param.20) | copy-start | bytes 12292
  88.0 18.0 %all-to-all-start.3 = ((bf16[8,128,256]{2,1,0:T(8,128)(2,1)}), bf16[8,128,256]{2,1,0:T(8,128)(2,1)S(1)}, u32[]{:S(2)}, u32[]{:S(2)}) async-start(bf16[8,128,256]{2,1,0:T(8,128)(2,1)} %combine.1), calls=%async_computation.3 | async-start | bytes 1048576 | tf_op jit(solution)/shard_map/all_to_all | solution.py:463
  91.5 88.1 %all-gather.7.cloned.1.call-start = ((), (), s32[]{:S(2)}) async-start(), calls=%async_computation.13 | async-start | bytes 3538944 | tf_op jit(solution)/shard_map/all_gather | solution.py:472
  93.3 21.6 %copy-start.3 = (bf16[512,128]{0,1:T(8,128)(2,1)S(1)}, bf16[512,128]{0,1:T(8,128)(2,1)}, u32[]{:S(2)}) copy-start(bf16[512,128]{0,1:T(8,128)(2,1)} %copy.51) | copy-start | bytes 393220
  93.4 12.6 %copy-start.4 = (bf16[128,512]{1,0:T(8,128)(2,1)}, bf16[128,512]{1,0:T(8,128)(2,1)S(1)}, u32[]{:S(2)}) copy-start(bf16[128,512]{1,0:T(8,128)(2,1)S(1)} %constant_dynamic-update-slice_fusion.resid_ref) | copy-start | bytes 393220
  105.9 0.8 copy-start.1
  109.6 6.2 %collective-permute-start.5 = (bf16[128,512]{1,0:T(8,128)(2,1)}, bf16[128,512]{1,0:T(8,128)(2,1)S(1)}, u32[]{:S(2)}, u32[]{:S(2)}) collective-permute-start(bf16[128,512]{1,0:T(8,128)(2,1)} %project.1.own_ref), channel_id=1, source_target_pairs={{0,192},{64,0},{128,64},{192,128},{1,193},{65,1},{129,65},{193,129... | collective-permute-start | bytes 393224 | tf_op jit(solution)/shard_map/ppermute | solution.py:390
  112.8 6.8 %collective-permute-start.4 = (bf16[128,512]{1,0:T(8,128)(2,1)}, bf16[128,512]{1,0:T(8,128)(2,1)S(1)}, u32[]{:S(2)}, u32[]{:S(2)}) collective-permute-start(bf16[128,512]{1,0:T(8,128)(2,1)} %project.1.own_ref), channel_id=1, source_target_pairs={{0,128},{64,192},{128,0},{192,64},{1,129},{65,193},{129,1},{193,65... | collective-permute-start | bytes 393224 | tf_op jit(solution)/shard_map/ppermute | solution.py:390
  113.4 7.5 %collective-permute-start.3 = (bf16[128,512]{1,0:T(8,128)(2,1)}, bf16[128,512]{1,0:T(8,128)(2,1)S(1)}, u32[]{:S(2)}, u32[]{:S(2)}) collective-permute-start(bf16[128,512]{1,0:T(8,128)(2,1)} %project.1.own_ref), channel_id=1, source_target_pairs={{0,64},{64,128},{128,192},{192,0},{1,65},{65,129},{129,193},{193,1... | collective-permute-start | bytes 393224 | tf_op jit(solution)/shard_map/ppermute | solution.py:390
  115.7 5.2 %copy-start.6 = (bf16[128,512]{1,0:T(8,128)(2,1)}, bf16[128,512]{1,0:T(8,128)(2,1)S(1)}, u32[]{:S(2)}) copy-start(bf16[128,512]{1,0:T(8,128)(2,1)S(1)} %collective-permute-done.5.three_ref) | copy-start | bytes 393220
  119.6 1.3 copy-start.7
  120.9 0.6 copy-start.8
  136.2 89.4 %reduce-scatter.2.cloned.1.call-start = ((), (), s32[]{:S(2)}) async-start(), calls=%async_computation.11 | async-start | bytes 2359296 | tf_op jit(solution)/shard_map/reduce_scatter | solution.py:480
  225.7 10.8 %all-to-all-start.8 = ((bf16[8,64,256]{2,1,0:T(8,128)(2,1)}), bf16[8,64,256]{2,1,0:T(8,128)(2,1)S(1)}, u32[]{:S(2)}, u32[]{:S(2)}) async-start(bf16[8,64,256]{2,1,0:T(8,128)(2,1)} %bitcast.60), calls=%async_computation.9 | async-start | bytes 524288 | tf_op jit(solution)/shard_map/all_to_all | solution.py:488
  236.5 0.7 copy-start.2
  239.4 7.3 %collective-permute-start.6 = (bf16[32,2304]{1,0:T(8,128)(2,1)}, bf16[32,2304]{1,0:T(8,128)(2,1)S(1)}, u32[]{:S(2)}, u32[]{:S(2)}) collective-permute-start(bf16[32,2304]{1,0:T(8,128)(2,1)} %get-tuple-element.45), channel_id=1, source_target_pairs={{0,64},{64,128},{128,192},{192,0},{1,65},{65,129},{129,193},{193,1... | collective-permute-start | bytes 442376 | tf_op jit(solution)/shard_map/ppermute | solution.py:390
  240.8 9.3 %collective-permute-start.7 = (bf16[32,2304]{1,0:T(8,128)(2,1)}, bf16[32,2304]{1,0:T(8,128)(2,1)S(1)}, u32[]{:S(2)}, u32[]{:S(2)}) collective-permute-start(bf16[32,2304]{1,0:T(8,128)(2,1)} %get-tuple-element.46), channel_id=1, source_target_pairs={{0,128},{64,192},{128,0},{192,64},{1,129},{65,193},{129,1},{193,65... | collective-permute-start | bytes 442376 | tf_op jit(solution)/shard_map/ppermute | solution.py:390
  243.5 6.6 %collective-permute-start.8 = (bf16[32,2304]{1,0:T(8,128)(2,1)}, bf16[32,2304]{1,0:T(8,128)(2,1)S(1)}, u32[]{:S(2)}, u32[]{:S(2)}) collective-permute-start(bf16[32,2304]{1,0:T(8,128)(2,1)} %get-tuple-element.47), channel_id=1, source_target_pairs={{0,192},{64,0},{128,64},{192,128},{1,193},{65,1},{129,65},{193,129... | collective-permute-start | bytes 442376 | tf_op jit(solution)/shard_map/ppermute | solution.py:390
Sparse Core Ops, SparseCore 0:
  62.0 26.4 all-gather.4
  136.4 43.2 all-gather.6
  188.0 37.6 reduce-scatter.1

commit v7 on v6

--- a/solution.py
+++ b/solution.py
@@ -26,16 +26,17 @@
 HIDDEN = 192
 STAT_ROWS = 16
 PAIRS = 2
+OWN_PAIRS = 4
 MASKED = -1e30
 SCALE2 = math.log2(math.e) / math.sqrt(HEAD_DIM)
-VMEM = 56 * 1024 * 1024
+MIB = 1024 * 1024
 
 f32 = jnp.float32
 bf16 = jnp.bfloat16
 
 
-def params():
-    return pltpu.CompilerParams(vmem_limit_bytes=VMEM)
+def params(mib=16):
+    return pltpu.CompilerParams(vmem_limit_bytes=mib * MIB)
 
 
 def dequantize_kernel(y_ref, scale_ref, cache_ref, *out_refs):
@@ -106,7 +107,7 @@
     lane = lax.broadcasted_iota(jnp.int32, (2 * WIN, 128), 1)
     maxima = [
         attend_chunks(q_ref, (kv0,), bias_ref, last_ref, s_ref, pair, (0,))
-        for pair in range(PAIRS)
+        for pair in range(OWN_PAIRS)
     ]
     for pair, m in enumerate(maxima):
         l, acc = weigh_chunks((kv0,), s_ref, pair, m)
@@ -139,19 +140,19 @@
         ).astype(bf16)
 
 
-def attention_specs(extra, outs, chunks):
+def attention_specs(extra, outs, chunks, pairs):
     whole = pl.BlockSpec((2, CTX_LOCAL, HEAD_DIM), lambda i, *_: (0, 0, 0))
     return pltpu.PrefetchScalarGridSpec(
         num_scalar_prefetch=1,
-        grid=(N_Z // PAIRS,),
+        grid=(N_Z // pairs,),
         in_specs=[
-            pl.BlockSpec((PAIRS, WIN, 2 * HEAD_DIM), lambda i, *_: (i, 0, 0)),
+            pl.BlockSpec((pairs, WIN, 2 * HEAD_DIM), lambda i, *_: (i, 0, 0)),
             pl.BlockSpec((N_Y, 1, CTX_LOCAL), lambda i, *_: (0, 0, 0)),
         ]
         + [whole] * chunks
-        + [pl.BlockSpec((PAIRS,) + e, lambda i, *_: (i, 0, 0)) for e in extra],
-        out_specs=[pl.BlockSpec((PAIRS,) + o, lambda i, *_: (i, 0, 0)) for o in outs],
-        scratch_shapes=[pltpu.VMEM((PAIRS, 2 * WIN, chunks * CTX_LOCAL), f32)],
+        + [pl.BlockSpec((pairs,) + e, lambda i, *_: (i, 0, 0)) for e in extra],
+        out_specs=[pl.BlockSpec((pairs,) + o, lambda i, *_: (i, 0, 0)) for o in outs],
+        scratch_shapes=[pltpu.VMEM((pairs, 2 * WIN, chunks * CTX_LOCAL), f32)],
     )
 
 
@@ -159,9 +160,9 @@
     square = (2 * WIN, HEAD_DIM)
     return pl.pallas_call(
         own_kernel,
-        grid_spec=attention_specs([], [square, square], 1),
+        grid_spec=attention_specs([], [square, square], 1, OWN_PAIRS),
         out_shape=[jax.ShapeDtypeStruct((N_Z,) + square, f32)] * 2,
-        compiler_params=params(),
+        compiler_params=params(32),
         cost_estimate=pl.CostEstimate(
             flops=3 << 30, bytes_accessed=8 << 20, transcendentals=2 << 20
         ),
@@ -174,9 +175,9 @@
     message = (2 * WIN + STAT_ROWS, HEAD_DIM)
     return pl.pallas_call(
         rest_kernel,
-        grid_spec=attention_specs([square, square], [message], 3),
+        grid_spec=attention_specs([square, square], [message], 3, PAIRS),
         out_shape=[jax.ShapeDtypeStruct((N_Z,) + message, bf16)],
-        compiler_params=params(),
+        compiler_params=params(32),
         cost_estimate=pl.CostEstimate(
             flops=8 << 30, bytes_accessed=8 << 20, transcendentals=6 << 20
         ),
@@ -212,7 +213,10 @@
     )(parts)
 
 
-def project_kernel(a_ref, w_ref, resid_ref, out_ref):
+def project_kernel(a_any, w_ref, resid_ref, out_ref, a_ref, sem):
+    copy = pltpu.make_async_copy(a_any, a_ref, sem)
+    copy.start()
+    copy.wait()
     acc = resid_ref[...].astype(f32)
     for z in range(N_Z):
         w_rows = jnp.concatenate([w_ref[g, z] for g in range(N_GRP)], axis=0)
@@ -224,12 +228,27 @@
     return pl.pallas_call(
         project_kernel,
         out_shape=jax.ShapeDtypeStruct((WIN, COLS), bf16),
+        in_specs=[pl.BlockSpec(memory_space=pl.ANY)] + [pl.BlockSpec(memory_space=pltpu.VMEM)] * 2,
+        scratch_shapes=[pltpu.VMEM((N_Z, WIN, 2 * HEAD_DIM), bf16), pltpu.SemaphoreType.DMA],
         compiler_params=params(),
         name="project",
     )(attended, w_cols, resid_rows)
 
 
-def dispatch_kernel(table_ref, own_ref, one_ref, two_ref, three_ref, stream_ref, out_ref, spread_ref):
+def dispatch_kernel(
+    table_ref, own_ref, one_any, two_any, three_any, stream_ref, out_ref, spread_ref, *scratch
+):
+    one_ref, two_ref, three_ref, sems = scratch
+    copies = [
+        pltpu.make_async_copy(source, target, sems.at[i])
+        for i, (source, target) in enumerate(
+            ((one_any, one_ref), (two_any, two_ref), (three_any, three_ref))
+        )
+    ]
+    for copy in copies:
+        copy.start()
+    for copy in copies:
+        copy.wait()
     total = (own_ref[...].astype(f32) + two_ref[...].astype(f32)) + (
         one_ref[...].astype(f32) + three_ref[...].astype(f32)
     )
@@ -250,6 +269,9 @@
             jax.ShapeDtypeStruct((N_GRP * CAP, NEAR), bf16),
             jax.ShapeDtypeStruct((N_Z, WIN, FAR), bf16),
         ),
+        in_specs=[pl.BlockSpec(memory_space=pltpu.VMEM)] * 2
+        + [pl.BlockSpec(memory_space=pl.ANY)] * 3,
+        scratch_shapes=[pltpu.VMEM((WIN, COLS), bf16)] * 3 + [pltpu.SemaphoreType.DMA((3,))],
         compiler_params=params(),
         name="dispatch",
     )(table, *parts)
@@ -320,7 +342,7 @@
             jax.ShapeDtypeStruct((N_Z, tokens, HALF), bf16),
             jax.ShapeDtypeStruct((tokens, D // 2), bf16),
         ],
-        compiler_params=params(),
+        compiler_params=params(40),
         name="experts",
     )(x, rest, gain, w_gate, w_up, w_down)
 
@@ -348,7 +370,11 @@
     )(table, parts)
 
 
-def mix_rest_kernel(table_ref, parts_ref, mixed_ref, *out_refs):
+def mix_rest_kernel(table_ref, parts_any, mixed_ref, *refs):
+    *out_refs, parts_ref, sem = refs
+    copy = pltpu.make_async_copy(parts_any, parts_ref, sem)
+    copy.start()
+    copy.wait()
     rest = jnp.dot(table_ref[...], parts_ref[...], preferred_element_type=f32).astype(bf16)
     rows = WIN // N_Y
     for d, out_ref in enumerate(out_refs):
@@ -360,6 +386,12 @@
     return pl.pallas_call(
         mix_rest_kernel,
         out_shape=[jax.ShapeDtypeStruct((WIN // N_Y, D // 2 + HALF), bf16)] * N_Y,
+        in_specs=[
+            pl.BlockSpec(memory_space=pltpu.VMEM),
+            pl.BlockSpec(memory_space=pl.ANY),
+            pl.BlockSpec(memory_space=pltpu.VMEM),
+        ],
+        scratch_shapes=[pltpu.VMEM((N_GRP * CAP, HALF), bf16), pltpu.SemaphoreType.DMA],
         compiler_params=params(),
         name="mix_rest",
     )(table, parts, mixed)
@@ -451,10 +483,10 @@
     )
 
     acc, stat = own_attention(last, queries_mine, bias, kv_own)
+    stat, early = lax.optimization_barrier((stat, early))
     parts = rest_attention(
         last, queries_mine, bias, kv_from[1], kv_from[3], kv_from[2], acc, stat
     )
-    parts, early = lax.optimization_barrier((parts, early))
     resid_rows = lax.dynamic_update_slice_in_dim(
         jnp.zeros((WIN, COLS), bf16), early[:, part:].reshape(rows, COLS), y_pos * rows, 0
     )

time: 276 us -> 297 us (1.076)
  waiting for transfers between devices: 40.6 us -> 75.9 us
  Pallas kernels: 47.7 us -> 25.1 us
  local copies, waits for them, and re-layouts: 10.5 us -> 29.8 us
  blocking collectives: 121 us -> 114 us
    ppermute x9, waiting for transfers between devices: 11.4 us -> 32.5 us  [over_y(): return lax.ppermute(value, 'y', [(i, (i + d) % N_Y) for i in range(N_Y)])]
    unnamed x29 -> x53, local copies, waits for them, and re-layouts: 2.81 us -> 23 us
    all_to_all x1, waiting for transfers between devices: 0.01 us -> 6.48 us  [per_device(): early = lax.all_to_all(early, 'z', 0, 0, tiled=True)]
    all_gather x1, waiting for transfers between devices: 1.33 us -> 5.79 us  [per_device(): arrivals = lax.all_gather(arrivals, 'z', axis=0, tiled=False)]
    pallas_call x1, Pallas kernels: 8.21 us -> 4.36 us  [experts(): pl.pallas_call(experts_kernel, grid=(tokens // tile,), in_specs=[pl.Block...]
    all_to_all x1, blocking collectives: 23.8 us -> 20.3 us  [per_device(): parts = lax.all_to_all(parts, 'z', 0, 0, tiled=True)]
  transfers between devices with their start and end apart: 16 -> 16, of which waited for: 10 -> 14; matrix products, arithmetic and copies ran while one was open for 3% -> 3% of each run, Pallas kernels for 11% -> 6%
where the time goes in v7:
time: 297 us; the launch traced here: 295 us
  blocking collectives  114 us (38%)
  waiting for transfers between devices  75.9 us (26%)
  starting transfers between devices  33.8 us (11%)
  local copies, waits for them, and re-layouts  29.8 us (10%)
  Pallas kernels  25.1 us (8%)
  between operations  13.5 us (5%)
  other arithmetic  3.11 us (1%)
    ppermute x9, waiting for transfers between devices, over_y(): return lax.ppermute(value, 'y', [(i, (i + d) % N_Y) for i in range(N_Y)])  32.5 us
    all_to_all x1, blocking collectives, per_device(): lax.all_to_all(by_x.reshape(N_GRP, CAP, D // 2), ('x', 'c'), 0, 0, tiled=...  31.9 us
    unnamed x53, local copies, waits for them, and re-layouts  23 us
    all_to_all x1, blocking collectives, per_device(): parts = lax.all_to_all(parts, 'z', 0, 0, tiled=True)  20.3 us
    all_to_all x1, blocking collectives, per_device(): lax.all_to_all(others.reshape(N_GRP, CAP, N_Z * FAR), ('x', 'c'), 0, 0, t...  19 us
    all_to_all x1, blocking collectives, per_device(): others = select(lax.all_to_all(spread, 'z', 0, 0, tiled=True), out_table)  16.6 us
    all_to_all x1, blocking collectives, per_device(): return finish(lax.all_to_all(tail, 'z', 0, 0, tiled=True))[None]  14.1 us
    ppermute x9, starting transfers between devices, over_y(): return lax.ppermute(value, 'y', [(i, (i + d) % N_Y) for i in range(N_Y)])  13.5 us
  transfers between devices with their start and end apart: 16, of which 14 were waited for; matrix products, arithmetic and copies ran while one was open for 3% of the time, Pallas kernels for 6%

profile of v7, /device:TPU:2, one launch (start us, length us, event | category | flops | bytes accessed | tf_op | source)
XLA Modules:
  0.0 295.2 jit_solution(18258132315014468104)
XLA Ops:
  6.5 1.8 broadcast_in_dim.80
  8.3 8.5 %all-to-all-start = ((bf16[8,128,256]{2,1,0:T(8,128)(2,1)}), bf16[8,128,256]{2,1,0:T(8,128)(2,1)S(1)}, u32[]{:S(2)}, u32[]{:S(2)}) async-start(bf16[8,128,256]{2,1,0:T(8,128)(2,1)} %broadcast_in_dim.80), calls=%async_computation | async-start | bytes 1048576 | tf_op jit(solution)/shard_map/all_to_all | solution.py:444
  17.3 1.3 reduce.3
  18.8 0.8 copy.60
  19.6 0.8 copy.57
  21.0 1.6 copy-done.3
  22.6 1.3 dequantize.1
  23.9 0.8 copy-done.14
  24.8 0.8 copy-done.12
  25.8 8.5 %all-to-all-done.q_ref = bf16[8,128,256]{2,1,0:T(8,128)(2,1)S(1)} async-done(((bf16[8,128,256]{2,1,0:T(8,128)(2,1)}), bf16[8,128,256]{2,1,0:T(8,128)(2,1)S(1)}, u32[]{:S(2)}, u32[]{:S(2)}) %all-to-all-start) | async-done | bytes 524320 | tf_op jit(solution)/shard_map/all_to_all | solution.py:444
  34.3 0.8 copy.53
  35.1 3.4 %all-to-all-start.1 = ((bf16[8,36,512]{2,1,0:T(8,128)(2,1)}), bf16[8,36,512]{2,1,0:T(8,128)(2,1)S(1)}, u32[]{:S(2)}, u32[]{:S(2)}) async-start(bf16[8,36,512]{2,1,0:T(8,128)(2,1)} %copy.53), calls=%async_computation.1 | async-start | bytes 655360 | tf_op jit(solution)/shard_map/all_to_all | solution.py:468
  38.8 1.0 copy-done.15
  39.8 3.9 %own_attention.1 = (f32[8,256,128]{2,1,0:T(8,128)S(1)}, f32[8,256,128]{2,1,0:T(8,128)S(1)}) custom-call(s32[4]{0:T(128)S(1)} %and_convert_fusion.last_ref, bf16[8,128,256]{2,1,0:T(8,128)(2,1)S(1)} %all-to-all-done.q_ref, f32[4,1,1024]{2,1,0:T(1,128)S(1)} %bitcast.56, bf16[2,1024,128]{2,1,0:T(8,128)(2,1)S(1)} %copy-done.15), custom_call_target="tpu_custom_call" | custom-call | flops 3221225472 | bytes 8388608 | tf_op jit(solution)/shard_map/own_attention/pallas_call | solution.py:161
  43.8 1.0 copy-done.16
  44.8 1.0 copy-done.18
  45.8 6.5 %all-to-all-done.1 = bf16[8,36,512]{2,1,0:T(8,128)(2,1)S(1)} async-done(((bf16[8,36,512]{2,1,0:T(8,128)(2,1)}), bf16[8,36,512]{2,1,0:T(8,128)(2,1)S(1)}, u32[]{:S(2)}, u32[]{:S(2)}) %all-to-all-start.1) | async-done | bytes 294944 | tf_op jit(solution)/shard_map/all_to_all | solution.py:468
  52.2 0.7 slice.6
  53.0 1.7 collective-permute-start
  54.6 1.7 collective-permute-start.1
  56.3 2.0 collective-permute-start.2
  58.3 10.1 %collective-permute-done.kv1 = bf16[2,1024,128]{2,1,0:T(8,128)(2,1)S(1)} collective-permute-done((bf16[2,1024,128]{2,1,0:T(8,128)(2,1)}, bf16[2,1024,128]{2,1,0:T(8,128)(2,1)S(1)}, u32[]{:S(2)}, u32[]{:S(2)}) %collective-permute-start) | collective-permute-done | bytes 524320 | tf_op jit(solution)/shard_map/ppermute | solution.py:422
  68.4 10.7 %collective-permute-done.1.kv3 = bf16[2,1024,128]{2,1,0:T(8,128)(2,1)S(1)} collective-permute-done((bf16[2,1024,128]{2,1,0:T(8,128)(2,1)}, bf16[2,1024,128]{2,1,0:T(8,128)(2,1)S(1)}, u32[]{:S(2)}, u32[]{:S(2)}) %collective-permute-start.1) | collective-permute-done | bytes 524320 | tf_op jit(solution)/shard_map/ppermute | solution.py:422
  79.1 1.7 collective-permute-done.2.kv2
  80.8 1.2 copy-done.17
  82.0 1.2 copy-done.19
  83.3 10.7 %rest_attention.1 = bf16[8,272,128]{2,1,0:T(8,128)(2,1)S(1)} custom-call(s32[4]{0:T(128)S(1)} %and_convert_fusion.last_ref, bf16[8,128,256]{2,1,0:T(8,128)(2,1)S(1)} %all-to-all-done.q_ref, f32[4,1,1024]{2,1,0:T(1,128)S(1)} %bitcast.57, bf16[2,1024,128]{2,1,0:T(8,128)(2,1)S(1)} %collective-permute-done.kv1, ...), custom_call_target="tpu_custom_call" | custom-call | flops 8589934592 | bytes 8388608 | tf_op jit(solution)/shard_map/rest_attention/pallas_call | solution.py:176
  94.0 20.3 %all_to_all.50.in_ref = bf16[8,272,128]{2,1,0:T(8,128)(2,1)S(1)} all-to-all(bf16[8,272,128]{2,1,0:T(8,128)(2,1)S(1)} %rest_attention.1), channel_id=1, replica_groups=mesh['y'=4,'z'=8,'x'=4,'c'=2] {'z'}, dimensions={0} | all-to-all | bytes 1114112 | tf_op jit(solution)/shard_map/all_to_all | solution.py:494
  114.3 1.3 combine.1
  115.6 3.5 %all-to-all-start.3 = ((bf16[8,128,256]{2,1,0:T(8,128)(2,1)}), bf16[8,128,256]{2,1,0:T(8,128)(2,1)S(1)}, u32[]{:S(2)}, u32[]{:S(2)}) async-start(bf16[8,128,256]{2,1,0:T(8,128)(2,1)} %combine.1), calls=%async_computation.3 | async-start | bytes 1048576 | tf_op jit(solution)/shard_map/all_to_all | solution.py:495
  119.7 0.8 copy.50
  120.6 0.8 copy.51
  121.4 0.8 copy.49
  122.3 12.2 %all-to-all-done.3.a_any = bf16[8,128,256]{2,1,0:T(8,128)(2,1)S(1)} async-done(((bf16[8,128,256]{2,1,0:T(8,128)(2,1)}), bf16[8,128,256]{2,1,0:T(8,128)(2,1)S(1)}, u32[]{:S(2)}, u32[]{:S(2)}) %all-to-all-start.3) | async-done | bytes 524320 | tf_op jit(solution)/shard_map/all_to_all | solution.py:495
  134.5 1.6 copy-done.4
  137.2 1.8 collective-permute-start.4
  139.0 0.9 fusion
  140.1 1.5 collective-permute-done.5.three_any
  141.6 2.1 collective-permute-done.4.two_any
  143.7 1.5 collective-permute-done.3.one_any
  145.2 0.8 dispatch.1
  146.0 12.2 %all_to_all.51 = bf16[8,64,384]{2,1,0:T(8,128)(2,1)} all-to-all(bf16[8,64,384]{2,1,0:T(8,128)(2,1)S(1)} %bitcast.54), channel_id=1, replica_groups=mesh['y'=4,'z'=8,'x'=4,'c'=2] {'x','c'}, dimensions={0} | all-to-all | bytes 786432 | tf_op jit(solution)/shard_map/all_to_all | solution.py:500
  158.3 16.6 %all_to_all.52.parts_ref = bf16[8,128,128]{2,1,0:T(8,128)(2,1)S(1)} all-to-all(bf16[8,128,128]{2,1,0:T(8,128)(2,1)S(1)} %get-tuple-element.40), channel_id=1, replica_groups=mesh['y'=4,'z'=8,'x'=4,'c'=2] {'z'}, dimensions={0} | all-to-all | bytes 524288 | tf_op jit(solution)/shard_map/all_to_all | solution.py:505
  175.3 19.0 %all_to_all.53 = bf16[8,64,1024]{2,1,0:T(8,128)(2,1)S(1)} all-to-all(bf16[8,64,1024]{2,1,0:T(8,128)(2,1)S(1)} %bitcast.44), channel_id=1, replica_groups=mesh['y'=4,'z'=8,'x'=4,'c'=2] {'x','c'}, dimensions={0} | all-to-all | bytes 2097152 | tf_op jit(solution)/shard_map/all_to_all | solution.py:506
  194.3 5.8 %all-gather.7.cloned.1.call-done = bf16[4096,384]{1,0:T(8,128)(2,1)} async-done(((bf16[512,384]{1,0:T(8,128)(2,1)}), bf16[4096,384]{1,0:T(8,128)(2,1)}) %all-gather.7.cloned.1.call-update) | async-done | bytes 3145744 | tf_op jit(solution)/shard_map/all_gather | solution.py:504
  200.1 1.9 copy-done.2
  202.0 1.4 copy-done.7
  203.4 1.4 copy-done.8
  204.8 1.4 copy-done.9
  206.2 4.4 %experts.1 = (bf16[8,512,256]{2,1,0:T(8,128)(2,1)S(1)}, bf16[512,2048]{1,0:T(8,128)(2,1)S(1)}) custom-call(bf16[8,512,384]{2,1,0:T(8,128)(2,1)S(1)} %bitcast.45, bf16[512,1024]{1,0:T(8,128)(2,1)S(1)} %bitcast.43, f32[1,4096]{1,0:T(1,128)S(1)} %bitcast.55, bf16[192,4096]{1,0:T(8,128)(2,1)S(1)} %bitcast.50, bf16[192,4096]{1,0:T(8,128)(2,1)S(1)} %bitcast.51, ...), custom_call_target="tpu_custom_call" | custom-call | tf_op jit(solution)/shard_map/experts/pallas_call | solution.py:326
  210.6 1.3 copy-done.5
  211.9 1.4 copy-done.6
  213.3 31.9 %all_to_all.54 = bf16[8,64,2048]{2,1,0:T(8,128)(2,1)} all-to-all(bf16[8,64,2048]{2,1,0:T(8,128)(2,1)} %bitcast.48), channel_id=1, replica_groups=mesh['y'=4,'z'=8,'x'=4,'c'=2] {'x','c'}, dimensions={0} | all-to-all | bytes 4194304 | tf_op jit(solution)/shard_map/all_to_all | solution.py:515
  245.2 6.8 %reduce-scatter.2.cloned.1.call-done = bf16[512,256]{1,0:T(8,128)(2,1)} async-done(((bf16[4096,256]{1,0:T(8,128)(2,1)}), bf16[512,256]{1,0:T(8,128)(2,1)}) %reduce-scatter.2.cloned.1.call-update) | async-done | bytes 262160 | tf_op jit(solution)/shard_map/reduce_scatter | solution.py:512
  252.0 4.8 %all-to-all-start.8 = ((bf16[8,64,256]{2,1,0:T(8,128)(2,1)}), bf16[8,64,256]{2,1,0:T(8,128)(2,1)S(1)}, u32[]{:S(2)}, u32[]{:S(2)}) async-start(bf16[8,64,256]{2,1,0:T(8,128)(2,1)} %bitcast.64), calls=%async_computation.9 | async-start | bytes 524288 | tf_op jit(solution)/shard_map/all_to_all | solution.py:520
  256.9 1.6 copy-done.1
  258.4 0.8 mix.1.mixed_ref
  259.3 3.5 %all-to-all-done.8 = bf16[8,64,256]{2,1,0:T(8,128)(2,1)S(1)} async-done(((bf16[8,64,256]{2,1,0:T(8,128)(2,1)}), bf16[8,64,256]{2,1,0:T(8,128)(2,1)S(1)}, u32[]{:S(2)}, u32[]{:S(2)}) %all-to-all-start.8) | async-done | bytes 262176 | tf_op jit(solution)/shard_map/all_to_all | solution.py:520
  263.1 1.6 collective-permute-start.6
  264.6 2.8 collective-permute-start.7
  267.4 1.4 collective-permute-start.8
  268.9 1.3 collective-permute-done.6
  270.1 3.6 %collective-permute-done.7 = bf16[32,2304]{1,0:T(8,128)(2,1)S(1)} collective-permute-done((bf16[32,2304]{1,0:T(8,128)(2,1)S(1)}, bf16[32,2304]{1,0:T(8,128)(2,1)S(1)}, u32[]{:S(2)}, u32[]{:S(2)}) %collective-permute-start.7) | collective-permute-done | bytes 147488 | tf_op jit(solution)/shard_map/ppermute | solution.py:422
  273.9 14.1 %all_to_all.55.in_ref = bf16[8,4,2816]{2,1,0:T(4,128)(2,1)S(1)} all-to-all(bf16[8,4,2816]{2,1,0:T(4,128)(2,1)S(1)} %reshape.126), channel_id=1, replica_groups=mesh['y'=4,'z'=8,'x'=4,'c'=2] {'z'}, dimensions={0} | all-to-all | bytes 360448 | tf_op jit(solution)/shard_map/all_to_all | solution.py:531
  (82 shorter events, 5.4 us)
Async XLA Ops:
  6.5 13.0 %copy-start = (bf16[256,4096]{1,0:T(8,128)(2,1)S(1)}, bf16[256,4096]{1,0:T(8,128)(2,1)}, u32[]{:S(2)}) copy-start(bf16[256,4096]{1,0:T(8,128)(2,1)} %param.17) | copy-start | bytes 6291460
  6.5 14.4 %copy-start.11 = (f32[1,8,8]{2,1,0:T(8,128)S(1)}, f32[1,8,8]{2,1,0:T(8,128)}, u32[]{:S(2)}) copy-start(f32[1,8,8]{2,1,0:T(8,128)} %param.14) | copy-start | bytes 772
  8.3 26.0 %all-to-all-start = ((bf16[8,128,256]{2,1,0:T(8,128)(2,1)}), bf16[8,128,256]{2,1,0:T(8,128)(2,1)S(1)}, u32[]{:S(2)}, u32[]{:S(2)}) async-start(bf16[8,128,256]{2,1,0:T(8,128)(2,1)} %broadcast_in_dim.80), calls=%async_computation | async-start | bytes 1048576 | tf_op jit(solution)/shard_map/all_to_all | solution.py:444
  21.0 1.6 copy-start.3
  22.6 3.2 %copy-start.21 = (bf16[4,8,8,512]{3,2,1,0:T(8,128)(2,1)S(1)}, bf16[4,8,8,512]{3,2,1,0:T(8,128)(2,1)}, u32[]{:S(2)}) copy-start(bf16[4,8,8,512]{3,2,1,0:T(8,128)(2,1)} %copy.57) | copy-start | bytes 786436
  23.9 0.8 copy-start.14
  24.8 0.8 copy-start.12
  24.8 1.0 copy-start.13
  35.1 17.1 %all-to-all-start.1 = ((bf16[8,36,512]{2,1,0:T(8,128)(2,1)}), bf16[8,36,512]{2,1,0:T(8,128)(2,1)S(1)}, u32[]{:S(2)}, u32[]{:S(2)}) async-start(bf16[8,36,512]{2,1,0:T(8,128)(2,1)} %copy.53), calls=%async_computation.1 | async-start | bytes 655360 | tf_op jit(solution)/shard_map/all_to_all | solution.py:468
  38.6 95.9 %all-gather.5.cloned.1.call-start = ((), (), s32[]{:S(2)}) async-start(), calls=%async_computation.12 | async-start | bytes 2359296 | tf_op jit(solution)/shard_map/all_gather | solution.py:493
  38.8 1.0 copy-start.15
  43.8 1.0 copy-start.16
  44.8 1.0 copy-start.18
  53.0 15.4 %collective-permute-start = (bf16[2,1024,128]{2,1,0:T(8,128)(2,1)}, bf16[2,1024,128]{2,1,0:T(8,128)(2,1)S(1)}, u32[]{:S(2)}, u32[]{:S(2)}) collective-permute-start(bf16[2,1024,128]{2,1,0:T(8,128)(2,1)} %copy-done.13), channel_id=1, source_target_pairs={{0,64},{64,128},{128,192},{192,0},{1,65},{65,129},{129,193},{193,1... | collective-permute-start | bytes 1572872 | tf_op jit(solution)/shard_map/ppermute | solution.py:422
  54.6 24.5 %collective-permute-start.1 = (bf16[2,1024,128]{2,1,0:T(8,128)(2,1)}, bf16[2,1024,128]{2,1,0:T(8,128)(2,1)S(1)}, u32[]{:S(2)}, u32[]{:S(2)}) collective-permute-start(bf16[2,1024,128]{2,1,0:T(8,128)(2,1)} %copy-done.12), channel_id=1, source_target_pairs={{0,192},{64,0},{128,64},{192,128},{1,193},{65,1},{129,65},{193,129... | collective-permute-start | bytes 1572872 | tf_op jit(solution)/shard_map/ppermute | solution.py:422
  56.3 24.5 %collective-permute-start.2 = (bf16[2,1024,128]{2,1,0:T(8,128)(2,1)S(1)}, bf16[2,1024,128]{2,1,0:T(8,128)(2,1)S(1)}, u32[]{:S(2)}, u32[]{:S(2)}) collective-permute-start(bf16[2,1024,128]{2,1,0:T(8,128)(2,1)S(1)} %get-tuple-element.30), channel_id=1, source_target_pairs={{0,128},{64,192},{128,0},{192,64},{1,129},{65,193},{129,1},{193,65... | collective-permute-start | bytes 1572872 | tf_op jit(solution)/shard_map/ppermute | solution.py:422
  80.8 1.2 copy-start.17
  82.0 1.2 copy-start.19
  94.0 25.2 %copy-start.23 = (s32[1,128,8]{1,2,0:T(8,128)S(1)}, s32[1,128,8]{1,2,0:T(8,128)}, u32[]{:S(2)}) copy-start(s32[1,128,8]{1,2,0:T(8,128)} %param.19) | copy-start | bytes 12292
  94.0 26.5 %copy-start.24 = (f32[1,128,8]{1,2,0:T(8,128)S(1)}, f32[1,128,8]{1,2,0:T(8,128)}, u32[]{:S(2)}) copy-start(f32[1,128,8]{1,2,0:T(8,128)} %param.20) | copy-start | bytes 12292
  115.6 18.8 %all-to-all-start.3 = ((bf16[8,128,256]{2,1,0:T(8,128)(2,1)}), bf16[8,128,256]{2,1,0:T(8,128)(2,1)S(1)}, u32[]{:S(2)}, u32[]{:S(2)}) async-start(bf16[8,128,256]{2,1,0:T(8,128)(2,1)} %combine.1), calls=%async_computation.3 | async-start | bytes 1048576 | tf_op jit(solution)/shard_map/all_to_all | solution.py:495
  119.1 81.0 %all-gather.7.cloned.1.call-start = ((), (), s32[]{:S(2)}) async-start(), calls=%async_computation.13 | async-start | bytes 3538944 | tf_op jit(solution)/shard_map/all_gather | solution.py:504
  122.2 16.8 %copy-start.20 = (s32[512,128]{0,1:T(8,128)S(1)}, s32[512,128]{0,1:T(8,128)}, u32[]{:S(2)}) copy-start(s32[512,128]{0,1:T(8,128)} %copy.49) | copy-start | bytes 786436
  134.5 1.6 copy-start.4
  136.1 2.9 copy-start.22
  136.6 5.0 %collective-permute-start.5 = (bf16[128,512]{1,0:T(8,128)(2,1)S(1)}, bf16[128,512]{1,0:T(8,128)(2,1)S(1)}, u32[]{:S(2)}, u32[]{:S(2)}) collective-permute-start(bf16[128,512]{1,0:T(8,128)(2,1)S(1)} %project.1.own_ref), channel_id=1, source_target_pairs={{0,192},{64,0},{128,64},{192,128},{1,193},{65,1},{129,65},{193,129... | collective-permute-start | bytes 393224 | tf_op jit(solution)/shard_map/ppermute | solution.py:422
  137.2 6.5 %collective-permute-start.4 = (bf16[128,512]{1,0:T(8,128)(2,1)S(1)}, bf16[128,512]{1,0:T(8,128)(2,1)S(1)}, u32[]{:S(2)}, u32[]{:S(2)}) collective-permute-start(bf16[128,512]{1,0:T(8,128)(2,1)S(1)} %project.1.own_ref), channel_id=1, source_target_pairs={{0,128},{64,192},{128,0},{192,64},{1,129},{65,193},{129,1},{193,65... | collective-permute-start | bytes 393224 | tf_op jit(solution)/shard_map/ppermute | solution.py:422
  139.0 6.2 %collective-permute-start.3 = (bf16[128,512]{1,0:T(8,128)(2,1)S(1)}, bf16[128,512]{1,0:T(8,128)(2,1)S(1)}, u32[]{:S(2)}, u32[]{:S(2)}) collective-permute-start(bf16[128,512]{1,0:T(8,128)(2,1)S(1)} %project.1.own_ref), channel_id=1, source_target_pairs={{0,64},{64,128},{128,192},{192,0},{1,65},{65,129},{129,193},{193,1... | collective-permute-start | bytes 393224 | tf_op jit(solution)/shard_map/ppermute | solution.py:422
  158.2 41.9 %copy-start.10 = (f32[4096]{0:T(1024)S(1)}, f32[4096]{0:T(1024)}, u32[]{:S(2)}) copy-start(f32[4096]{0:T(1024)} %param.18) | copy-start | bytes 49156
  158.2 93.7 %reduce-scatter.2.cloned.1.call-start = ((), (), s32[]{:S(2)}) async-start(), calls=%async_computation.11 | async-start | bytes 2359296 | tf_op jit(solution)/shard_map/reduce_scatter | solution.py:512
  200.1 1.9 copy-start.2
  202.0 1.4 copy-start.7
  203.4 1.4 copy-start.8
  204.8 1.4 copy-start.9
  210.6 1.3 copy-start.5
  211.9 1.4 copy-start.6
  252.0 10.9 %all-to-all-start.8 = ((bf16[8,64,256]{2,1,0:T(8,128)(2,1)}), bf16[8,64,256]{2,1,0:T(8,128)(2,1)S(1)}, u32[]{:S(2)}, u32[]{:S(2)}) async-start(bf16[8,64,256]{2,1,0:T(8,128)(2,1)} %bitcast.64), calls=%async_computation.9 | async-start | bytes 524288 | tf_op jit(solution)/shard_map/all_to_all | solution.py:520
  256.9 1.6 copy-start.1
  263.1 7.1 %collective-permute-start.6 = (bf16[32,2304]{1,0:T(8,128)(2,1)S(1)}, bf16[32,2304]{1,0:T(8,128)(2,1)S(1)}, u32[]{:S(2)}, u32[]{:S(2)}) collective-permute-start(bf16[32,2304]{1,0:T(8,128)(2,1)S(1)} %get-tuple-element.45), channel_id=1, source_target_pairs={{0,64},{64,128},{128,192},{192,0},{1,65},{65,129},{129,193},{193,1... | collective-permute-start | bytes 442376 | tf_op jit(solution)/shard_map/ppermute | solution.py:422
  264.6 9.1 %collective-permute-start.7 = (bf16[32,2304]{1,0:T(8,128)(2,1)S(1)}, bf16[32,2304]{1,0:T(8,128)(2,1)S(1)}, u32[]{:S(2)}, u32[]{:S(2)}) collective-permute-start(bf16[32,2304]{1,0:T(8,128)(2,1)S(1)} %get-tuple-element.46), channel_id=1, source_target_pairs={{0,128},{64,192},{128,0},{192,64},{1,129},{65,193},{129,1},{193,65... | collective-permute-start | bytes 442376 | tf_op jit(solution)/shard_map/ppermute | solution.py:422
  267.4 6.4 %collective-permute-start.8 = (bf16[32,2304]{1,0:T(8,128)(2,1)S(1)}, bf16[32,2304]{1,0:T(8,128)(2,1)S(1)}, u32[]{:S(2)}, u32[]{:S(2)}) collective-permute-start(bf16[32,2304]{1,0:T(8,128)(2,1)S(1)} %get-tuple-element.47), channel_id=1, source_target_pairs={{0,192},{64,0},{128,64},{192,128},{1,193},{65,1},{129,65},{193,129... | collective-permute-start | bytes 442376 | tf_op jit(solution)/shard_map/ppermute | solution.py:422
Sparse Core Ops, SparseCore 0:
  53.1 22.7 all-gather.4
  158.3 41.7 all-gather.6
  213.4 38.5 reduce-scatter.1

commit v8 on v7

--- a/solution.py
+++ b/solution.py
@@ -63,7 +63,7 @@
             out_specs=[pl.BlockSpec((2, 4 * BLOCK, HEAD_DIM), lambda i, *_: (0, i, 0))] * N_Y,
         ),
         out_shape=[shape] * N_Y,
-        compiler_params=params(),
+        compiler_params=params(56),
         cost_estimate=pl.CostEstimate(flops=1 << 20, bytes_accessed=4 << 20, transcendentals=0),
         name="dequantize",
     )(y_pos, scale, cache)
@@ -342,7 +342,7 @@
             jax.ShapeDtypeStruct((N_Z, tokens, HALF), bf16),
             jax.ShapeDtypeStruct((tokens, D // 2), bf16),
         ],
-        compiler_params=params(40),
+        compiler_params=params(56),
         name="experts",
     )(x, rest, gain, w_gate, w_up, w_down)
 
@@ -483,10 +483,10 @@
     )
 
     acc, stat = own_attention(last, queries_mine, bias, kv_own)
-    stat, early = lax.optimization_barrier((stat, early))
     parts = rest_attention(
         last, queries_mine, bias, kv_from[1], kv_from[3], kv_from[2], acc, stat
     )
+    parts, early = lax.optimization_barrier((parts, early))
     resid_rows = lax.dynamic_update_slice_in_dim(
         jnp.zeros((WIN, COLS), bf16), early[:, part:].reshape(rows, COLS), y_pos * rows, 0
     )

time: 297 us -> 263 us (0.89)
  waiting for transfers between devices: 75.9 us -> 44.4 us
  local copies, waits for them, and re-layouts: 29.8 us -> 14.2 us
  Pallas kernels: 25.1 us -> 32.6 us
  blocking collectives: 114 us -> 118 us
    ppermute x9, waiting for transfers between devices: 32.5 us -> 13 us  [over_y(): return lax.ppermute(value, 'y', [(i, (i + d) % N_Y) for i in range(N_Y)])]
    unnamed x53 -> x27, local copies, waits for them, and re-layouts: 23 us -> 7.41 us
    all_to_all x1, waiting for transfers between devices: 6.48 us -> 0.01 us  [per_device(): early = lax.all_to_all(early, 'z', 0, 0, tiled=True)]
    pallas_call x1, Pallas kernels: 4.36 us -> 8.24 us  [experts(): pl.pallas_call(experts_kernel, grid=(tokens // tile,), in_specs=[pl.Block...]
    all_to_all x1, waiting for transfers between devices: 8.5 us -> 4.95 us  [per_device(): lax.all_to_all(jnp.broadcast_to(queries, (N_Z,) + queries.shape[1:]), 'z'...]
    all_to_all x1, blocking collectives: 20.3 us -> 23.4 us  [per_device(): parts = lax.all_to_all(parts, 'z', 0, 0, tiled=True)]
  transfers between devices with their start and end apart: 16 -> 16, of which waited for: 14 -> 12; matrix products, arithmetic and copies ran while one was open for 3% -> 3% of each run, Pallas kernels for 6% -> 9%
where the time goes in v8:
time: 263 us; the launch traced here: 261 us
  blocking collectives  118 us (45%)
  waiting for transfers between devices  44.4 us (17%)
  starting transfers between devices  34.2 us (13%)
  Pallas kernels  32.6 us (12%)
  local copies, waits for them, and re-layouts  14.2 us (5%)
  between operations  13.4 us (5%)
  other arithmetic  3.37 us (1%)
    all_to_all x1, blocking collectives, per_device(): lax.all_to_all(by_x.reshape(N_GRP, CAP, D // 2), ('x', 'c'), 0, 0, tiled=...  31.9 us
    all_to_all x1, blocking collectives, per_device(): parts = lax.all_to_all(parts, 'z', 0, 0, tiled=True)  23.4 us
    all_to_all x1, blocking collectives, per_device(): lax.all_to_all(others.reshape(N_GRP, CAP, N_Z * FAR), ('x', 'c'), 0, 0, t...  19.6 us
    all_to_all x1, blocking collectives, per_device(): others = select(lax.all_to_all(spread, 'z', 0, 0, tiled=True), out_table)  16.7 us
    all_to_all x1, blocking collectives, per_device(): return finish(lax.all_to_all(tail, 'z', 0, 0, tiled=True))[None]  14.2 us
    ppermute x9, starting transfers between devices, over_y(): return lax.ppermute(value, 'y', [(i, (i + d) % N_Y) for i in range(N_Y)])  13.9 us
    ppermute x9, waiting for transfers between devices, over_y(): return lax.ppermute(value, 'y', [(i, (i + d) % N_Y) for i in range(N_Y)])  13 us
    all_to_all x1, blocking collectives, per_device(): lax.all_to_all(outgoing.reshape(N_GRP, CAP, NEAR), ('x', 'c'), 0, 0, tile...  12.5 us
  transfers between devices with their start and end apart: 16, of which 12 were waited for; matrix products, arithmetic and copies ran while one was open for 3% of the time, Pallas kernels for 9%

profile of v8, /device:TPU:2, one launch (start us, length us, event | category | flops | bytes accessed | tf_op | source)
XLA Modules:
  0.0 260.6 jit_solution(5286389231196314298)
XLA Ops:
  6.5 1.8 broadcast_in_dim.80
  8.4 8.5 %all-to-all-start = ((bf16[8,128,256]{2,1,0:T(8,128)(2,1)}), bf16[8,128,256]{2,1,0:T(8,128)(2,1)S(1)}, u32[]{:S(2)}, u32[]{:S(2)}) async-start(bf16[8,128,256]{2,1,0:T(8,128)(2,1)} %broadcast_in_dim.80), calls=%async_computation | async-start | bytes 1048576 | tf_op jit(solution)/shard_map/all_to_all | solution.py:444
  16.8 3.5 %dequantize.1 = (bf16[2,1024,128]{2,1,0:T(8,128)(2,1)}, bf16[2,1024,128]{2,1,0:T(8,128)(2,1)}, bf16[2,1024,128]{2,1,0:T(8,128)(2,1)}, bf16[2,1024,128]{2,1,0:T(8,128)(2,1)}) custom-call(s32[1]{0:T(128)} %bitcast.11.y_ref, f32[8,8]{1,0:T(8,128)} %bitcast.71, bf16[1024,1024]{1,0:T(8,128)(2,1)} %bitcast.51), custom_call_target="tpu_custom_call" | custom-call | flops 1048576 | bytes 4194304 | tf_op jit(solution)/shard_map/dequantize/pallas_call | solution.py:57
  20.4 1.6 collective-permute-start
  21.9 1.7 collective-permute-start.1
  23.6 2.0 collective-permute-start.2
  25.6 0.5 broadcast.144
  26.2 0.7 reduce.3
  26.9 0.8 copy.57
  27.7 0.6 gather_fusion
  28.3 1.0 maximum_bitcast_fusion
  29.4 4.9 %all-to-all-done.q_ref = bf16[8,128,256]{2,1,0:T(8,128)(2,1)S(1)} async-done(((bf16[8,128,256]{2,1,0:T(8,128)(2,1)}), bf16[8,128,256]{2,1,0:T(8,128)(2,1)S(1)}, u32[]{:S(2)}, u32[]{:S(2)}) %all-to-all-start) | async-done | bytes 524320 | tf_op jit(solution)/shard_map/all_to_all | solution.py:444
  34.3 0.8 copy.53
  35.1 3.4 %all-to-all-start.1 = ((bf16[8,36,512]{2,1,0:T(8,128)(2,1)}), bf16[8,36,512]{2,1,0:T(8,128)(2,1)S(1)}, u32[]{:S(2)}, u32[]{:S(2)}) async-start(bf16[8,36,512]{2,1,0:T(8,128)(2,1)} %copy.53), calls=%async_computation.1 | async-start | bytes 655360 | tf_op jit(solution)/shard_map/all_to_all | solution.py:468
  38.7 1.0 copy-done.5
  39.7 3.9 %own_attention.1 = (f32[8,256,128]{2,1,0:T(8,128)S(1)}, f32[8,256,128]{2,1,0:T(8,128)S(1)}) custom-call(s32[4]{0:T(128)S(1)} %and_convert_fusion.last_ref, bf16[8,128,256]{2,1,0:T(8,128)(2,1)S(1)} %all-to-all-done.q_ref, f32[4,1,1024]{2,1,0:T(1,128)S(1)} %bitcast.47, bf16[2,1024,128]{2,1,0:T(8,128)(2,1)S(1)} %copy-done.5), custom_call_target="tpu_custom_call" | custom-call | flops 3221225472 | bytes 8388608 | tf_op jit(solution)/shard_map/own_attention/pallas_call | solution.py:161
  43.7 0.8 copy-done.3
  44.5 1.4 collective-permute-done.1.kv3
  45.9 1.9 collective-permute-done.2.kv2
  47.7 1.0 copy-done.4
  48.8 12.1 %rest_attention.1 = bf16[8,272,128]{2,1,0:T(8,128)(2,1)S(1)} custom-call(s32[4]{0:T(128)S(1)} %and_convert_fusion.last_ref, bf16[8,128,256]{2,1,0:T(8,128)(2,1)S(1)} %all-to-all-done.q_ref, f32[4,1,1024]{2,1,0:T(1,128)S(1)} %bitcast.48, bf16[2,1024,128]{2,1,0:T(8,128)(2,1)S(1)} %copy-done.4, bf16[2,1024,128]{2,1,0:T(8,128)(2,1)} %collective-permute-done.1.kv3, ...), custom_call_target="tpu_custom_call" | custom-call | flops 8589934592 | bytes 8388608 | tf_op jit(solution)/shard_map/rest_attention/pallas_call | solution.py:176
  60.9 0.7 slice.6
  61.7 23.4 %all_to_all.50.in_ref = bf16[8,272,128]{2,1,0:T(8,128)(2,1)S(1)} all-to-all(bf16[8,272,128]{2,1,0:T(8,128)(2,1)S(1)} %rest_attention.1), channel_id=1, replica_groups=mesh['y'=4,'z'=8,'x'=4,'c'=2] {'z'}, dimensions={0} | all-to-all | bytes 1114112 | tf_op jit(solution)/shard_map/all_to_all | solution.py:494
  85.1 1.3 combine.1
  86.5 3.5 %all-to-all-start.3 = ((bf16[8,128,256]{2,1,0:T(8,128)(2,1)}), bf16[8,128,256]{2,1,0:T(8,128)(2,1)S(1)}, u32[]{:S(2)}, u32[]{:S(2)}) async-start(bf16[8,128,256]{2,1,0:T(8,128)(2,1)} %combine.1), calls=%async_computation.3 | async-start | bytes 1048576 | tf_op jit(solution)/shard_map/all_to_all | solution.py:495
  90.0 0.1 compare_reduce_fusion
  90.1 0.3 reduce_window_sum.11
  90.5 0.8 copy.50
  91.3 0.1 fusion.2
  91.4 0.8 copy.51
  92.2 0.8 copy.49
  93.1 11.3 %all-to-all-done.3.a_any = bf16[8,128,256]{2,1,0:T(8,128)(2,1)S(1)} async-done(((bf16[8,128,256]{2,1,0:T(8,128)(2,1)}), bf16[8,128,256]{2,1,0:T(8,128)(2,1)S(1)}, u32[]{:S(2)}, u32[]{:S(2)}) %all-to-all-start.3) | async-done | bytes 524320 | tf_op jit(solution)/shard_map/all_to_all | solution.py:495
  104.4 1.6 copy-done.2
  106.0 0.5 project.1.own_ref
  106.5 0.9 collective-permute-start.5
  107.4 1.9 collective-permute-start.4
  109.3 0.2 collective-permute-start.3
  109.5 0.9 fusion
  110.4 0.1 copy.54.table_ref
  110.6 1.0 collective-permute-done.5.three_any
  111.5 2.3 collective-permute-done.4.two_any
  113.8 1.6 collective-permute-done.3.one_any
  115.4 0.8 dispatch.1
  116.2 12.5 %all_to_all.51 = bf16[8,64,384]{2,1,0:T(8,128)(2,1)} all-to-all(bf16[8,64,384]{2,1,0:T(8,128)(2,1)S(1)} %bitcast.46), channel_id=1, replica_groups=mesh['y'=4,'z'=8,'x'=4,'c'=2] {'x','c'}, dimensions={0} | all-to-all | bytes 786432 | tf_op jit(solution)/shard_map/all_to_all | solution.py:500
  128.8 16.7 %all_to_all.52.parts_ref = bf16[8,128,128]{2,1,0:T(8,128)(2,1)S(1)} all-to-all(bf16[8,128,128]{2,1,0:T(8,128)(2,1)S(1)} %get-tuple-element.40), channel_id=1, replica_groups=mesh['y'=4,'z'=8,'x'=4,'c'=2] {'z'}, dimensions={0} | all-to-all | bytes 524288 | tf_op jit(solution)/shard_map/all_to_all | solution.py:505
  145.6 0.4 select.17
  146.0 19.6 %all_to_all.53 = bf16[8,64,1024]{2,1,0:T(8,128)(2,1)} all-to-all(bf16[8,64,1024]{2,1,0:T(8,128)(2,1)S(1)} %bitcast.43), channel_id=1, replica_groups=mesh['y'=4,'z'=8,'x'=4,'c'=2] {'x','c'}, dimensions={0} | all-to-all | bytes 2097152 | tf_op jit(solution)/shard_map/all_to_all | solution.py:506
  165.6 5.0 %all-gather.7.cloned.1.call-done = bf16[4096,384]{1,0:T(8,128)(2,1)} async-done(((bf16[512,384]{1,0:T(8,128)(2,1)}), bf16[4096,384]{1,0:T(8,128)(2,1)}) %all-gather.7.cloned.1.call-update) | async-done | bytes 3145744 | tf_op jit(solution)/shard_map/all_gather | solution.py:504
  170.7 8.2 %experts.1 = (bf16[8,512,256]{2,1,0:T(8,128)(2,1)}, bf16[512,2048]{1,0:T(8,128)(2,1)}) custom-call(bf16[8,512,384]{2,1,0:T(8,128)(2,1)} %bitcast.50, bf16[512,1024]{1,0:T(8,128)(2,1)} %bitcast.49, f32[1,4096]{1,0:T(1,128)} %bitcast.68, bf16[192,4096]{1,0:T(8,128)(2,1)} %bitcast.55, bf16[192,4096]{1,0:T(8,128)(2,1)} %bitcast.56, bf16[192,4096]{1,0:T(8,128)(2,1)} %bitcast.57), custom_call_target="tpu_custom_call" | custom-call | tf_op jit(solution)/shard_map/experts/pallas_call | solution.py:326
  178.9 31.9 %all_to_all.54 = bf16[8,64,2048]{2,1,0:T(8,128)(2,1)} all-to-all(bf16[8,64,2048]{2,1,0:T(8,128)(2,1)} %bitcast.52), channel_id=1, replica_groups=mesh['y'=4,'z'=8,'x'=4,'c'=2] {'x','c'}, dimensions={0} | all-to-all | bytes 4194304 | tf_op jit(solution)/shard_map/all_to_all | solution.py:515
  210.8 6.6 %reduce-scatter.2.cloned.1.call-done = bf16[512,256]{1,0:T(8,128)(2,1)} async-done(((bf16[4096,256]{1,0:T(8,128)(2,1)}), bf16[512,256]{1,0:T(8,128)(2,1)}) %reduce-scatter.2.cloned.1.call-update) | async-done | bytes 262160 | tf_op jit(solution)/shard_map/reduce_scatter | solution.py:512
  217.4 4.8 %all-to-all-start.8 = ((bf16[8,64,256]{2,1,0:T(8,128)(2,1)}), bf16[8,64,256]{2,1,0:T(8,128)(2,1)S(1)}, u32[]{:S(2)}, u32[]{:S(2)}) async-start(bf16[8,64,256]{2,1,0:T(8,128)(2,1)} %bitcast.62), calls=%async_computation.9 | async-start | bytes 524288 | tf_op jit(solution)/shard_map/all_to_all | solution.py:520
  222.2 0.1 fusion.1.table_ref
  222.3 1.6 copy-done.1
  223.9 0.8 mix.1.mixed_ref
  224.8 3.5 %all-to-all-done.8 = bf16[8,64,256]{2,1,0:T(8,128)(2,1)S(1)} async-done(((bf16[8,64,256]{2,1,0:T(8,128)(2,1)}), bf16[8,64,256]{2,1,0:T(8,128)(2,1)S(1)}, u32[]{:S(2)}, u32[]{:S(2)}) %all-to-all-start.8) | async-done | bytes 262176 | tf_op jit(solution)/shard_map/all_to_all | solution.py:520
  228.3 0.3 mix_rest.1
  228.6 1.6 collective-permute-start.6
  230.1 2.7 %collective-permute-start.7 = (bf16[32,2304]{1,0:T(8,128)(2,1)S(1)}, bf16[32,2304]{1,0:T(8,128)(2,1)S(1)}, u32[]{:S(2)}, u32[]{:S(2)}) collective-permute-start(bf16[32,2304]{1,0:T(8,128)(2,1)S(1)} %get-tuple-element.46), channel_id=1, source_target_pairs={{0,128},{64,192},{128,0},{192,64},{1,129},{65,193},{129,1},{193,65... | collective-permute-start | bytes 442376 | tf_op jit(solution)/shard_map/ppermute | solution.py:422
  232.8 1.5 collective-permute-start.8
  234.3 1.5 collective-permute-done.6
  235.7 3.4 %collective-permute-done.7 = bf16[32,2304]{1,0:T(8,128)(2,1)S(1)} collective-permute-done((bf16[32,2304]{1,0:T(8,128)(2,1)S(1)}, bf16[32,2304]{1,0:T(8,128)(2,1)S(1)}, u32[]{:S(2)}, u32[]{:S(2)}) %collective-permute-start.7) | collective-permute-done | bytes 147488 | tf_op jit(solution)/shard_map/ppermute | solution.py:422
  239.3 14.2 %all_to_all.55.in_ref = bf16[8,4,2816]{2,1,0:T(4,128)(2,1)S(1)} all-to-all(bf16[8,4,2816]{2,1,0:T(4,128)(2,1)S(1)} %reshape.126), channel_id=1, replica_groups=mesh['y'=4,'z'=8,'x'=4,'c'=2] {'z'}, dimensions={0} | all-to-all | bytes 360448 | tf_op jit(solution)/shard_map/all_to_all | solution.py:531
  253.4 0.6 finish.1
  (56 shorter events, 0.9 us)
Async XLA Ops:
  6.5 19.0 %copy-start = (bf16[256,4096]{1,0:T(8,128)(2,1)S(1)}, bf16[256,4096]{1,0:T(8,128)(2,1)}, u32[]{:S(2)}) copy-start(bf16[256,4096]{1,0:T(8,128)(2,1)} %param.17) | copy-start | bytes 6291460
  6.5 19.6 %copy-start.11 = (s32[1,1,256]{2,1,0:T(1,128)S(1)}, s32[1,1,256]{2,1,0:T(1,128)}, u32[]{:S(2)}) copy-start(s32[1,1,256]{2,1,0:T(1,128)} %param.15) | copy-start | bytes 3076
  6.5 20.4 %copy-start.8 = (bf16[1,4,4096]{2,1,0:T(4,128)(2,1)S(1)}, bf16[1,4,4096]{2,1,0:T(4,128)(2,1)}, u32[]{:S(2)}) copy-start(bf16[1,4,4096]{2,1,0:T(4,128)(2,1)} %param.16) | copy-start | bytes 98308
  8.4 26.0 %all-to-all-start = ((bf16[8,128,256]{2,1,0:T(8,128)(2,1)}), bf16[8,128,256]{2,1,0:T(8,128)(2,1)S(1)}, u32[]{:S(2)}, u32[]{:S(2)}) async-start(bf16[8,128,256]{2,1,0:T(8,128)(2,1)} %broadcast_in_dim.80), calls=%async_computation | async-start | bytes 1048576 | tf_op jit(solution)/shard_map/all_to_all | solution.py:444
  20.4 23.3 %collective-permute-start = (bf16[2,1024,128]{2,1,0:T(8,128)(2,1)}, bf16[2,1024,128]{2,1,0:T(8,128)(2,1)S(1)}, u32[]{:S(2)}, u32[]{:S(2)}) collective-permute-start(bf16[2,1024,128]{2,1,0:T(8,128)(2,1)} %get-tuple-element.28), channel_id=1, source_target_pairs={{0,64},{64,128},{128,192},{192,0},{1,65},{65,129},{129,193},{193,1... | collective-permute-start | bytes 1572872 | tf_op jit(solution)/shard_map/ppermute | solution.py:422
  21.9 24.0 %collective-permute-start.1 = (bf16[2,1024,128]{2,1,0:T(8,128)(2,1)}, bf16[2,1024,128]{2,1,0:T(8,128)(2,1)}, u32[]{:S(2)}, u32[]{:S(2)}) collective-permute-start(bf16[2,1024,128]{2,1,0:T(8,128)(2,1)} %get-tuple-element.29), channel_id=1, source_target_pairs={{0,192},{64,0},{128,64},{192,128},{1,193},{65,1},{129,65},{193,129... | collective-permute-start | bytes 1572872 | tf_op jit(solution)/shard_map/ppermute | solution.py:422
  23.6 24.1 %collective-permute-start.2 = (bf16[2,1024,128]{2,1,0:T(8,128)(2,1)}, bf16[2,1024,128]{2,1,0:T(8,128)(2,1)}, u32[]{:S(2)}, u32[]{:S(2)}) collective-permute-start(bf16[2,1024,128]{2,1,0:T(8,128)(2,1)} %get-tuple-element.30), channel_id=1, source_target_pairs={{0,128},{64,192},{128,0},{192,64},{1,129},{65,193},{129,1},{193,65... | collective-permute-start | bytes 1572872 | tf_op jit(solution)/shard_map/ppermute | solution.py:422
  35.1 25.8 %all-to-all-start.1 = ((bf16[8,36,512]{2,1,0:T(8,128)(2,1)}), bf16[8,36,512]{2,1,0:T(8,128)(2,1)S(1)}, u32[]{:S(2)}, u32[]{:S(2)}) async-start(bf16[8,36,512]{2,1,0:T(8,128)(2,1)} %copy.53), calls=%async_computation.1 | async-start | bytes 655360 | tf_op jit(solution)/shard_map/all_to_all | solution.py:468
  38.6 65.8 %all-gather.5.cloned.1.call-start = ((), (), s32[]{:S(2)}) async-start(), calls=%async_computation.12 | async-start | bytes 2359296 | tf_op jit(solution)/shard_map/all_gather | solution.py:493
  38.7 1.0 copy-start.5
  43.7 0.8 copy-start.3
  47.7 1.0 copy-start.4
  60.9 29.1 %copy-start.9 = (s32[1,128,8]{1,2,0:T(8,128)S(1)}, s32[1,128,8]{1,2,0:T(8,128)}, u32[]{:S(2)}) copy-start(s32[1,128,8]{1,2,0:T(8,128)} %param.19) | copy-start | bytes 12292
  60.9 30.4 %copy-start.10 = (f32[1,128,8]{1,2,0:T(8,128)S(1)}, f32[1,128,8]{1,2,0:T(8,128)}, u32[]{:S(2)}) copy-start(f32[1,128,8]{1,2,0:T(8,128)} %param.20) | copy-start | bytes 12292
  86.5 17.9 %all-to-all-start.3 = ((bf16[8,128,256]{2,1,0:T(8,128)(2,1)}), bf16[8,128,256]{2,1,0:T(8,128)(2,1)S(1)}, u32[]{:S(2)}, u32[]{:S(2)}) async-start(bf16[8,128,256]{2,1,0:T(8,128)(2,1)} %combine.1), calls=%async_computation.3 | async-start | bytes 1048576 | tf_op jit(solution)/shard_map/all_to_all | solution.py:495
  90.0 80.7 %all-gather.7.cloned.1.call-start = ((), (), s32[]{:S(2)}) async-start(), calls=%async_computation.13 | async-start | bytes 3538944 | tf_op jit(solution)/shard_map/all_gather | solution.py:504
  93.1 16.4 %copy-start.6 = (s32[512,128]{0,1:T(8,128)S(1)}, s32[512,128]{0,1:T(8,128)}, u32[]{:S(2)}) copy-start(s32[512,128]{0,1:T(8,128)} %copy.49) | copy-start | bytes 786436
  104.4 1.6 copy-start.2
  106.0 3.5 %copy-start.7 = (bf16[512,128]{0,1:T(8,128)(2,1)S(1)}, bf16[512,128]{0,1:T(8,128)(2,1)}, u32[]{:S(2)}) copy-start(bf16[512,128]{0,1:T(8,128)(2,1)} %copy.51) | copy-start | bytes 393220
  106.5 5.0 %collective-permute-start.5 = (bf16[128,512]{1,0:T(8,128)(2,1)S(1)}, bf16[128,512]{1,0:T(8,128)(2,1)S(1)}, u32[]{:S(2)}, u32[]{:S(2)}) collective-permute-start(bf16[128,512]{1,0:T(8,128)(2,1)S(1)} %project.1.own_ref), channel_id=1, source_target_pairs={{0,192},{64,0},{128,64},{192,128},{1,193},{65,1},{129,65},{193,129... | collective-permute-start | bytes 393224 | tf_op jit(solution)/shard_map/ppermute | solution.py:422
  107.4 6.5 %collective-permute-start.4 = (bf16[128,512]{1,0:T(8,128)(2,1)S(1)}, bf16[128,512]{1,0:T(8,128)(2,1)S(1)}, u32[]{:S(2)}, u32[]{:S(2)}) collective-permute-start(bf16[128,512]{1,0:T(8,128)(2,1)S(1)} %project.1.own_ref), channel_id=1, source_target_pairs={{0,128},{64,192},{128,0},{192,64},{1,129},{65,193},{129,1},{193,65... | collective-permute-start | bytes 393224 | tf_op jit(solution)/shard_map/ppermute | solution.py:422
  109.3 6.2 %collective-permute-start.3 = (bf16[128,512]{1,0:T(8,128)(2,1)S(1)}, bf16[128,512]{1,0:T(8,128)(2,1)S(1)}, u32[]{:S(2)}, u32[]{:S(2)}) collective-permute-start(bf16[128,512]{1,0:T(8,128)(2,1)S(1)} %project.1.own_ref), channel_id=1, source_target_pairs={{0,64},{64,128},{128,192},{192,0},{1,65},{65,129},{129,193},{193,1... | collective-permute-start | bytes 393224 | tf_op jit(solution)/shard_map/ppermute | solution.py:422
  128.8 88.6 %reduce-scatter.2.cloned.1.call-start = ((), (), s32[]{:S(2)}) async-start(), calls=%async_computation.11 | async-start | bytes 2359296 | tf_op jit(solution)/shard_map/reduce_scatter | solution.py:512
  217.4 10.9 %all-to-all-start.8 = ((bf16[8,64,256]{2,1,0:T(8,128)(2,1)}), bf16[8,64,256]{2,1,0:T(8,128)(2,1)S(1)}, u32[]{:S(2)}, u32[]{:S(2)}) async-start(bf16[8,64,256]{2,1,0:T(8,128)(2,1)} %bitcast.62), calls=%async_computation.9 | async-start | bytes 524288 | tf_op jit(solution)/shard_map/all_to_all | solution.py:520
  222.3 1.6 copy-start.1
  228.6 7.2 %collective-permute-start.6 = (bf16[32,2304]{1,0:T(8,128)(2,1)S(1)}, bf16[32,2304]{1,0:T(8,128)(2,1)S(1)}, u32[]{:S(2)}, u32[]{:S(2)}) collective-permute-start(bf16[32,2304]{1,0:T(8,128)(2,1)S(1)} %get-tuple-element.45), channel_id=1, source_target_pairs={{0,64},{64,128},{128,192},{192,0},{1,65},{65,129},{129,193},{193,1... | collective-permute-start | bytes 442376 | tf_op jit(solution)/shard_map/ppermute | solution.py:422
  230.1 9.0 %collective-permute-start.7 = (bf16[32,2304]{1,0:T(8,128)(2,1)S(1)}, bf16[32,2304]{1,0:T(8,128)(2,1)S(1)}, u32[]{:S(2)}, u32[]{:S(2)}) collective-permute-start(bf16[32,2304]{1,0:T(8,128)(2,1)S(1)} %get-tuple-element.46), channel_id=1, source_target_pairs={{0,128},{64,192},{128,0},{192,64},{1,129},{65,193},{129,1},{193,65... | collective-permute-start | bytes 442376 | tf_op jit(solution)/shard_map/ppermute | solution.py:422
  232.8 6.4 %collective-permute-start.8 = (bf16[32,2304]{1,0:T(8,128)(2,1)S(1)}, bf16[32,2304]{1,0:T(8,128)(2,1)S(1)}, u32[]{:S(2)}, u32[]{:S(2)}) collective-permute-start(bf16[32,2304]{1,0:T(8,128)(2,1)S(1)} %get-tuple-element.47), channel_id=1, source_target_pairs={{0,192},{64,0},{128,64},{192,128},{1,193},{65,1},{129,65},{193,129... | collective-permute-start | bytes 442376 | tf_op jit(solution)/shard_map/ppermute | solution.py:422
Sparse Core Ops, SparseCore 0:
  61.8 26.4 all-gather.4
  128.9 41.6 all-gather.6
  179.0 38.3 reduce-scatter.1

commit v9 on v8

--- a/solution.py
+++ b/solution.py
@@ -291,13 +291,47 @@
     )(parts, table)
 
 
-def experts_kernel(x_ref, rest_ref, gain_ref, wg_ref, wu_ref, wd_ref, by_z_ref, by_x_ref):
+def experts_kernel(
+    gain_ref, x_hbm, rest_hbm, wg_hbm, wu_hbm, wd_hbm, hidden_ref, by_z_hbm, *scratch
+):
+    x_ref, rest_ref, wg_ref, wu_ref, wd_ref, by_z_ref, in_sems, out_sems = scratch
     tokens = x_ref.shape[1]
+    rest_copy = pltpu.make_async_copy(rest_hbm, rest_ref, in_sems.at[3 * N_Z])
+    rest_copy.start()
+    block_copies = []
+    for z in range(N_Z):
+        cols = pl.ds(z * COLS, COLS)
+        group = [
+            pltpu.make_async_copy(x_hbm.at[z], x_ref.at[z], in_sems.at[3 * z]),
+            pltpu.make_async_copy(
+                wg_hbm.at[:, cols], wg_ref.at[:, cols], in_sems.at[3 * z + 1]
+            ),
+            pltpu.make_async_copy(
+                wu_hbm.at[:, cols], wu_ref.at[:, cols], in_sems.at[3 * z + 2]
+            ),
+        ]
+        for copy in group:
+            copy.start()
+        block_copies.append(group)
+    down_copies = [
+        pltpu.make_async_copy(
+            wd_hbm.at[:, pl.ds(z * COLS, HALF)],
+            wd_ref.at[:, pl.ds(z * HALF, HALF)],
+            in_sems.at[3 * N_Z + 1 + z],
+        )
+        for z in range(N_Z)
+    ]
+    for copy in down_copies:
+        copy.start()
+
     squares = jnp.zeros((tokens, 128), f32)
     gate = jnp.zeros((tokens, HIDDEN), f32)
     up = jnp.zeros((tokens, HIDDEN), f32)
     contract = (((1,), (1,)), ((), ()))
+    rest_copy.wait()
     for z in range(N_Z):
+        for copy in block_copies[z]:
+            copy.wait()
         cols = slice(z * COLS, (z + 1) * COLS)
         far = rest_ref[:, z * FAR : (z + 1) * FAR]
         wide = jnp.concatenate([x_ref[z], far], axis=1).astype(f32)
@@ -313,38 +347,89 @@
     gate = gate * factor
     up = up * factor
     hidden = (gate / (1.0 + jnp.exp(-gate)) * up).astype(bf16)
+    hidden_ref[...] = hidden
+    out_copies = []
     for z in range(N_Z):
-        cols = slice(z * COLS, (z + 1) * COLS)
-        done = jnp.dot(hidden, wd_ref[:, cols], preferred_element_type=f32).astype(bf16)
-        by_z_ref[z] = done[:, :HALF]
-        by_x_ref[:, z * HALF : (z + 1) * HALF] = done[:, HALF:]
-
-
-def experts(x, rest, gain, w_gate, w_up, w_down, tile=256):
+        down_copies[z].wait()
+        by_z_ref[z] = jnp.dot(
+            hidden, wd_ref[:, z * HALF : (z + 1) * HALF], preferred_element_type=f32
+        ).astype(bf16)
+        copy = pltpu.make_async_copy(by_z_ref.at[z], by_z_hbm.at[z], out_sems.at[z])
+        copy.start()
+        out_copies.append(copy)
+    for copy in out_copies:
+        copy.wait()
+
+
+def down_kernel(hidden_ref, wd_hbm, by_x_hbm, wd_ref, by_x_ref, in_sems, out_sems):
+    halves = [pl.ds(z * HALF, HALF) for z in range(N_Z)]
+    in_copies = [
+        pltpu.make_async_copy(
+            wd_hbm.at[:, pl.ds(z * COLS + HALF, HALF)], wd_ref.at[:, halves[z]], in_sems.at[z]
+        )
+        for z in range(N_Z)
+    ]
+    out_copies = [
+        pltpu.make_async_copy(
+            by_x_ref.at[:, halves[z]], by_x_hbm.at[:, halves[z]], out_sems.at[z]
+        )
+        for z in range(N_Z)
+    ]
+    for copy in in_copies:
+        copy.start()
+    for z in range(N_Z):
+        in_copies[z].wait()
+        cols = slice(z * HALF, (z + 1) * HALF)
+        by_x_ref[:, cols] = jnp.dot(
+            hidden_ref[...], wd_ref[:, cols], preferred_element_type=f32
+        ).astype(bf16)
+        out_copies[z].start()
+    for copy in out_copies:
+        copy.wait()
+
+
+def down(hidden, w_down):
+    hbm = pl.BlockSpec(memory_space=pltpu.HBM)
+    return pl.pallas_call(
+        down_kernel,
+        in_specs=[pl.BlockSpec(memory_space=pltpu.VMEM), hbm],
+        out_specs=hbm,
+        out_shape=jax.ShapeDtypeStruct((hidden.shape[0], D // 2), bf16),
+        scratch_shapes=[
+            pltpu.VMEM((HIDDEN, D // 2), bf16),
+            pltpu.VMEM((hidden.shape[0], D // 2), bf16),
+            pltpu.SemaphoreType.DMA((N_Z,)),
+            pltpu.SemaphoreType.DMA((N_Z,)),
+        ],
+        compiler_params=params(56),
+        name="down",
+    )(hidden, w_down)
+
+
+def experts(x, rest, gain, w_gate, w_up, w_down):
     tokens = x.shape[1]
-    whole = pl.BlockSpec((HIDDEN, D), lambda i: (0, 0))
+    hbm = pl.BlockSpec(memory_space=pltpu.HBM)
     return pl.pallas_call(
         experts_kernel,
-        grid=(tokens // tile,),
-        in_specs=[
-            pl.BlockSpec((N_Z, tile, NEAR), lambda i: (0, i, 0)),
-            pl.BlockSpec((tile, N_Z * FAR), lambda i: (i, 0)),
-            pl.BlockSpec((1, D), lambda i: (0, 0)),
-            whole,
-            whole,
-            whole,
+        in_specs=[pl.BlockSpec(memory_space=pltpu.VMEM)] + [hbm] * 5,
+        out_specs=[pl.BlockSpec(memory_space=pltpu.VMEM), hbm],
+        out_shape=[
+            jax.ShapeDtypeStruct((tokens, HIDDEN), bf16),
+            jax.ShapeDtypeStruct((N_Z, tokens, HALF), bf16),
         ],
-        out_specs=[
-            pl.BlockSpec((N_Z, tile, HALF), lambda i: (0, i, 0)),
-            pl.BlockSpec((tile, D // 2), lambda i: (i, 0)),
-        ],
-        out_shape=[
-            jax.ShapeDtypeStruct((N_Z, tokens, HALF), bf16),
-            jax.ShapeDtypeStruct((tokens, D // 2), bf16),
+        scratch_shapes=[
+            pltpu.VMEM((N_Z, tokens, NEAR), bf16),
+            pltpu.VMEM((tokens, N_Z * FAR), bf16),
+            pltpu.VMEM((HIDDEN, D), bf16),
+            pltpu.VMEM((HIDDEN, D), bf16),
+            pltpu.VMEM((HIDDEN, D // 2), bf16),
+            pltpu.VMEM((N_Z, tokens, HALF), bf16),
+            pltpu.SemaphoreType.DMA((4 * N_Z + 1,)),
+            pltpu.SemaphoreType.DMA((N_Z,)),
         ],
         compiler_params=params(56),
         name="experts",
-    )(x, rest, gain, w_gate, w_up, w_down)
+    )(gain, x, rest, w_gate, w_up, w_down)
 
 
 def mix_kernel(table_ref, parts_ref, out_ref):
@@ -506,9 +591,10 @@
     others = lax.all_to_all(
         others.reshape(N_GRP, CAP, N_Z * FAR), ("x", "c"), 0, 0, tiled=True
     ).reshape(N_GRP * CAP, N_Z * FAR)
-    by_z, by_x = experts(
+    hidden, by_z = experts(
         arrivals, others, norm_gain[None], w_gate[0], w_up[0], w_down[0]
     )
+    by_x = down(hidden, w_down[0])
     by_z = lax.psum_scatter(
         by_z.reshape(N_Z * N_GRP * CAP, HALF), "z", scatter_dimension=0, tiled=True
     )

time: 263 us -> 264 us (level)
  Pallas kernels: 32.6 us -> 38.6 us
  waiting for transfers between devices: 44.4 us -> 39.8 us
    pallas_call x1 -> x2, Pallas kernels: 8.24 us -> 14.3 us  [the longest x1 9.35 us: experts(): pl.pallas_call(experts_kernel, in_specs=[pl.BlockSpec(memory_space=pltpu....]
    reduce_scatter x1, waiting for transfers between devices: 6.62 us -> 1.86 us  [per_device(): lax.psum_scatter(by_z.reshape(N_Z * N_GRP * CAP, HALF), 'z', scatter_dime...]
  transfers between devices with their start and end apart: 16 -> 16, of which waited for: 12 -> 12; matrix products, arithmetic and copies ran while one was open for 3% -> 3% of each run, Pallas kernels for 9% -> 10%
where the time goes in v9:
time: 264 us; the launch traced here: 262 us
  blocking collectives  118 us (45%)
  waiting for transfers between devices  39.8 us (15%)
  Pallas kernels  38.6 us (15%)
  starting transfers between devices  34.1 us (13%)
  local copies, waits for them, and re-layouts  14.2 us (5%)
  between operations  13.4 us (5%)
  other arithmetic  3.37 us (1%)
    all_to_all x1, blocking collectives, per_device(): lax.all_to_all(by_x.reshape(N_GRP, CAP, D // 2), ('x', 'c'), 0, 0, tiled=...  31.9 us
    all_to_all x1, blocking collectives, per_device(): parts = lax.all_to_all(parts, 'z', 0, 0, tiled=True)  23.4 us
    all_to_all x1, blocking collectives, per_device(): lax.all_to_all(others.reshape(N_GRP, CAP, N_Z * FAR), ('x', 'c'), 0, 0, t...  19.6 us
    all_to_all x1, blocking collectives, per_device(): others = select(lax.all_to_all(spread, 'z', 0, 0, tiled=True), out_table)  16.7 us
    all_to_all x1, blocking collectives, per_device(): return finish(lax.all_to_all(tail, 'z', 0, 0, tiled=True))[None]  14 us
    ppermute x9, starting transfers between devices, over_y(): return lax.ppermute(value, 'y', [(i, (i + d) % N_Y) for i in range(N_Y)])  13.9 us
    ppermute x9, waiting for transfers between devices, over_y(): return lax.ppermute(value, 'y', [(i, (i + d) % N_Y) for i in range(N_Y)])  13.1 us
    all_to_all x1, blocking collectives, per_device(): lax.all_to_all(outgoing.reshape(N_GRP, CAP, NEAR), ('x', 'c'), 0, 0, tile...  12.5 us
  transfers between devices with their start and end apart: 16, of which 12 were waited for; matrix products, arithmetic and copies ran while one was open for 3% of the time, Pallas kernels for 10%

profile of v9, /device:TPU:2, one launch (start us, length us, event | category | flops | bytes accessed | tf_op | source)
XLA Modules:
  0.0 261.7 jit_solution(13667772303789280510)
XLA Ops:
  6.5 1.8 broadcast_in_dim.81
  8.4 8.5 %all-to-all-start = ((bf16[8,128,256]{2,1,0:T(8,128)(2,1)}), bf16[8,128,256]{2,1,0:T(8,128)(2,1)S(1)}, u32[]{:S(2)}, u32[]{:S(2)}) async-start(bf16[8,128,256]{2,1,0:T(8,128)(2,1)} %broadcast_in_dim.81), calls=%async_computation | async-start | bytes 1048576 | tf_op jit(solution)/shard_map/all_to_all | solution.py:529
  16.8 3.5 %dequantize.1 = (bf16[2,1024,128]{2,1,0:T(8,128)(2,1)}, bf16[2,1024,128]{2,1,0:T(8,128)(2,1)}, bf16[2,1024,128]{2,1,0:T(8,128)(2,1)}, bf16[2,1024,128]{2,1,0:T(8,128)(2,1)}) custom-call(s32[1]{0:T(128)} %bitcast.12.y_ref, f32[8,8]{1,0:T(8,128)} %bitcast.72, bf16[1024,1024]{1,0:T(8,128)(2,1)} %bitcast.54), custom_call_target="tpu_custom_call" | custom-call | flops 1048576 | bytes 4194304 | tf_op jit(solution)/shard_map/dequantize/pallas_call | solution.py:57
  20.4 1.6 collective-permute-start
  21.9 1.7 collective-permute-start.1
  23.6 2.0 collective-permute-start.2
  25.6 0.5 broadcast.144
  26.2 0.7 reduce.3
  26.9 0.8 copy.57
  27.7 0.6 gather_fusion
  28.3 1.0 maximum_bitcast_fusion
  29.4 4.9 %all-to-all-done.q_ref = bf16[8,128,256]{2,1,0:T(8,128)(2,1)S(1)} async-done(((bf16[8,128,256]{2,1,0:T(8,128)(2,1)}), bf16[8,128,256]{2,1,0:T(8,128)(2,1)S(1)}, u32[]{:S(2)}, u32[]{:S(2)}) %all-to-all-start) | async-done | bytes 524320 | tf_op jit(solution)/shard_map/all_to_all | solution.py:529
  34.3 0.8 copy.53
  35.1 3.4 %all-to-all-start.1 = ((bf16[8,36,512]{2,1,0:T(8,128)(2,1)}), bf16[8,36,512]{2,1,0:T(8,128)(2,1)S(1)}, u32[]{:S(2)}, u32[]{:S(2)}) async-start(bf16[8,36,512]{2,1,0:T(8,128)(2,1)} %copy.53), calls=%async_computation.1 | async-start | bytes 655360 | tf_op jit(solution)/shard_map/all_to_all | solution.py:553
  38.7 1.0 copy-done.5
  39.7 3.9 %own_attention.1 = (f32[8,256,128]{2,1,0:T(8,128)S(1)}, f32[8,256,128]{2,1,0:T(8,128)S(1)}) custom-call(s32[4]{0:T(128)S(1)} %and_convert_fusion.last_ref, bf16[8,128,256]{2,1,0:T(8,128)(2,1)S(1)} %all-to-all-done.q_ref, f32[4,1,1024]{2,1,0:T(1,128)S(1)} %bitcast.47, bf16[2,1024,128]{2,1,0:T(8,128)(2,1)S(1)} %copy-done.5), custom_call_target="tpu_custom_call" | custom-call | flops 3221225472 | bytes 8388608 | tf_op jit(solution)/shard_map/own_attention/pallas_call | solution.py:161
  43.7 0.8 copy-done.3
  44.5 1.4 collective-permute-done.1.kv3
  45.9 1.9 collective-permute-done.2.kv2
  47.7 1.0 copy-done.4
  48.8 12.1 %rest_attention.1 = bf16[8,272,128]{2,1,0:T(8,128)(2,1)S(1)} custom-call(s32[4]{0:T(128)S(1)} %and_convert_fusion.last_ref, bf16[8,128,256]{2,1,0:T(8,128)(2,1)S(1)} %all-to-all-done.q_ref, f32[4,1,1024]{2,1,0:T(1,128)S(1)} %bitcast.48, bf16[2,1024,128]{2,1,0:T(8,128)(2,1)S(1)} %copy-done.4, bf16[2,1024,128]{2,1,0:T(8,128)(2,1)} %collective-permute-done.1.kv3, ...), custom_call_target="tpu_custom_call" | custom-call | flops 8589934592 | bytes 8388608 | tf_op jit(solution)/shard_map/rest_attention/pallas_call | solution.py:176
  60.9 0.7 slice.6
  61.7 23.4 %all_to_all.50.in_ref = bf16[8,272,128]{2,1,0:T(8,128)(2,1)S(1)} all-to-all(bf16[8,272,128]{2,1,0:T(8,128)(2,1)S(1)} %rest_attention.1), channel_id=1, replica_groups=mesh['y'=4,'z'=8,'x'=4,'c'=2] {'z'}, dimensions={0} | all-to-all | bytes 1114112 | tf_op jit(solution)/shard_map/all_to_all | solution.py:579
  85.1 1.3 combine.1
  86.4 3.5 %all-to-all-start.3 = ((bf16[8,128,256]{2,1,0:T(8,128)(2,1)}), bf16[8,128,256]{2,1,0:T(8,128)(2,1)S(1)}, u32[]{:S(2)}, u32[]{:S(2)}) async-start(bf16[8,128,256]{2,1,0:T(8,128)(2,1)} %combine.1), calls=%async_computation.3 | async-start | bytes 1048576 | tf_op jit(solution)/shard_map/all_to_all | solution.py:580
  90.0 0.1 compare_reduce_fusion
  90.1 0.3 reduce_window_sum.11
  90.5 0.8 copy.50
  91.4 0.8 copy.51
  92.2 0.8 copy.49
  93.1 11.3 %all-to-all-done.3.a_any = bf16[8,128,256]{2,1,0:T(8,128)(2,1)S(1)} async-done(((bf16[8,128,256]{2,1,0:T(8,128)(2,1)}), bf16[8,128,256]{2,1,0:T(8,128)(2,1)S(1)}, u32[]{:S(2)}, u32[]{:S(2)}) %all-to-all-start.3) | async-done | bytes 524320 | tf_op jit(solution)/shard_map/all_to_all | solution.py:580
  104.4 1.6 copy-done.2
  106.0 0.5 project.1.own_ref
  106.5 0.9 collective-permute-start.5
  107.3 1.9 collective-permute-start.4
  109.2 0.2 collective-permute-start.3
  109.5 0.9 fusion
  110.4 0.1 copy.54.table_ref
  110.5 1.0 collective-permute-done.5.three_any
  111.5 2.3 collective-permute-done.4.two_any
  113.8 1.6 collective-permute-done.3.one_any
  115.4 0.8 dispatch.1
  116.2 12.5 %all_to_all.51 = bf16[8,64,384]{2,1,0:T(8,128)(2,1)} all-to-all(bf16[8,64,384]{2,1,0:T(8,128)(2,1)S(1)} %bitcast.46), channel_id=1, replica_groups=mesh['y'=4,'z'=8,'x'=4,'c'=2] {'x','c'}, dimensions={0} | all-to-all | bytes 786432 | tf_op jit(solution)/shard_map/all_to_all | solution.py:585
  128.8 16.7 %all_to_all.52.parts_ref = bf16[8,128,128]{2,1,0:T(8,128)(2,1)S(1)} all-to-all(bf16[8,128,128]{2,1,0:T(8,128)(2,1)S(1)} %get-tuple-element.40), channel_id=1, replica_groups=mesh['y'=4,'z'=8,'x'=4,'c'=2] {'z'}, dimensions={0} | all-to-all | bytes 524288 | tf_op jit(solution)/shard_map/all_to_all | solution.py:590
  145.5 0.4 select.17
  146.0 19.6 %all_to_all.53 = bf16[8,64,1024]{2,1,0:T(8,128)(2,1)} all-to-all(bf16[8,64,1024]{2,1,0:T(8,128)(2,1)S(1)} %bitcast.43), channel_id=1, replica_groups=mesh['y'=4,'z'=8,'x'=4,'c'=2] {'x','c'}, dimensions={0} | all-to-all | bytes 2097152 | tf_op jit(solution)/shard_map/all_to_all | solution.py:591
  165.6 5.0 %all-gather.7.cloned.1.call-done = bf16[4096,384]{1,0:T(8,128)(2,1)} async-done(((bf16[512,384]{1,0:T(8,128)(2,1)}), bf16[4096,384]{1,0:T(8,128)(2,1)}) %all-gather.7.cloned.1.call-update) | async-done | bytes 3145744 | tf_op jit(solution)/shard_map/all_gather | solution.py:589
  170.6 9.4 %experts.1 = (bf16[512,192]{1,0:T(8,128)(2,1)}, bf16[8,512,256]{2,1,0:T(8,128)(2,1)}) custom-call(f32[1,4096]{1,0:T(1,128)} %bitcast.69, bf16[8,512,384]{2,1,0:T(8,128)(2,1)} %bitcast.53, bf16[512,1024]{1,0:T(8,128)(2,1)} %bitcast.52, bf16[192,4096]{1,0:T(8,128)(2,1)} %bitcast.57, bf16[192,4096]{1,0:T(8,128)(2,1)} %bitcast.58, bf16[192,4096]{1,0:T(8,128)(2,1)} %bitcast.50), custom_call_target="tpu_custom_call" | custom-call | tf_op jit(solution)/shard_map/experts/pallas_call | solution.py:412
  180.0 4.9 %down.1 = bf16[512,2048]{1,0:T(8,128)(2,1)} custom-call(bf16[512,192]{1,0:T(8,128)(2,1)} %get-tuple-element.42.hidden_ref, bf16[192,4096]{1,0:T(8,128)(2,1)} %bitcast.51), custom_call_target="tpu_custom_call" | custom-call | tf_op jit(solution)/shard_map/down/pallas_call | solution.py:393
  185.0 31.9 %all_to_all.54 = bf16[8,64,2048]{2,1,0:T(8,128)(2,1)} all-to-all(bf16[8,64,2048]{2,1,0:T(8,128)(2,1)} %bitcast.49), channel_id=1, replica_groups=mesh['y'=4,'z'=8,'x'=4,'c'=2] {'x','c'}, dimensions={0} | all-to-all | bytes 4194304 | tf_op jit(solution)/shard_map/all_to_all | solution.py:601
  216.8 1.9 reduce-scatter.2.cloned.1.call-done
  218.7 4.7 %all-to-all-start.8 = ((bf16[8,64,256]{2,1,0:T(8,128)(2,1)}), bf16[8,64,256]{2,1,0:T(8,128)(2,1)S(1)}, u32[]{:S(2)}, u32[]{:S(2)}) async-start(bf16[8,64,256]{2,1,0:T(8,128)(2,1)} %bitcast.63), calls=%async_computation.9 | async-start | bytes 524288 | tf_op jit(solution)/shard_map/all_to_all | solution.py:606
  223.4 0.1 fusion.1.table_ref
  223.5 1.6 copy-done.1
  225.1 0.8 mix.1.mixed_ref
  225.9 3.5 %all-to-all-done.8 = bf16[8,64,256]{2,1,0:T(8,128)(2,1)S(1)} async-done(((bf16[8,64,256]{2,1,0:T(8,128)(2,1)}), bf16[8,64,256]{2,1,0:T(8,128)(2,1)S(1)}, u32[]{:S(2)}, u32[]{:S(2)}) %all-to-all-start.8) | async-done | bytes 262176 | tf_op jit(solution)/shard_map/all_to_all | solution.py:606
  229.5 0.3 mix_rest.1
  229.7 1.6 collective-permute-start.6
  231.3 2.7 %collective-permute-start.7 = (bf16[32,2304]{1,0:T(8,128)(2,1)S(1)}, bf16[32,2304]{1,0:T(8,128)(2,1)S(1)}, u32[]{:S(2)}, u32[]{:S(2)}) collective-permute-start(bf16[32,2304]{1,0:T(8,128)(2,1)S(1)} %get-tuple-element.46), channel_id=1, source_target_pairs={{0,128},{64,192},{128,0},{192,64},{1,129},{65,193},{129,1},{193,65... | collective-permute-start | bytes 442376 | tf_op jit(solution)/shard_map/ppermute | solution.py:507
  234.0 1.4 collective-permute-start.8
  235.4 1.5 collective-permute-done.6
  236.9 3.5 %collective-permute-done.7 = bf16[32,2304]{1,0:T(8,128)(2,1)S(1)} collective-permute-done((bf16[32,2304]{1,0:T(8,128)(2,1)S(1)}, bf16[32,2304]{1,0:T(8,128)(2,1)S(1)}, u32[]{:S(2)}, u32[]{:S(2)}) %collective-permute-start.7) | collective-permute-done | bytes 147488 | tf_op jit(solution)/shard_map/ppermute | solution.py:507
  240.5 14.0 %all_to_all.55.in_ref = bf16[8,4,2816]{2,1,0:T(4,128)(2,1)S(1)} all-to-all(bf16[8,4,2816]{2,1,0:T(4,128)(2,1)S(1)} %reshape.126), channel_id=1, replica_groups=mesh['y'=4,'z'=8,'x'=4,'c'=2] {'z'}, dimensions={0} | all-to-all | bytes 360448 | tf_op jit(solution)/shard_map/all_to_all | solution.py:617
  254.5 0.6 finish.1
  (57 shorter events, 1.0 us)
Async XLA Ops:
  6.5 19.0 %copy-start = (bf16[256,4096]{1,0:T(8,128)(2,1)S(1)}, bf16[256,4096]{1,0:T(8,128)(2,1)}, u32[]{:S(2)}) copy-start(bf16[256,4096]{1,0:T(8,128)(2,1)} %param.17) | copy-start | bytes 6291460
  6.5 19.6 %copy-start.11 = (s32[1,1,256]{2,1,0:T(1,128)S(1)}, s32[1,1,256]{2,1,0:T(1,128)}, u32[]{:S(2)}) copy-start(s32[1,1,256]{2,1,0:T(1,128)} %param.15) | copy-start | bytes 3076
  6.5 20.4 %copy-start.8 = (bf16[1,4,4096]{2,1,0:T(4,128)(2,1)S(1)}, bf16[1,4,4096]{2,1,0:T(4,128)(2,1)}, u32[]{:S(2)}) copy-start(bf16[1,4,4096]{2,1,0:T(4,128)(2,1)} %param.16) | copy-start | bytes 98308
  8.4 26.0 %all-to-all-start = ((bf16[8,128,256]{2,1,0:T(8,128)(2,1)}), bf16[8,128,256]{2,1,0:T(8,128)(2,1)S(1)}, u32[]{:S(2)}, u32[]{:S(2)}) async-start(bf16[8,128,256]{2,1,0:T(8,128)(2,1)} %broadcast_in_dim.81), calls=%async_computation | async-start | bytes 1048576 | tf_op jit(solution)/shard_map/all_to_all | solution.py:529
  20.4 23.3 %collective-permute-start = (bf16[2,1024,128]{2,1,0:T(8,128)(2,1)}, bf16[2,1024,128]{2,1,0:T(8,128)(2,1)S(1)}, u32[]{:S(2)}, u32[]{:S(2)}) collective-permute-start(bf16[2,1024,128]{2,1,0:T(8,128)(2,1)} %get-tuple-element.28), channel_id=1, source_target_pairs={{0,64},{64,128},{128,192},{192,0},{1,65},{65,129},{129,193},{193,1... | collective-permute-start | bytes 1572872 | tf_op jit(solution)/shard_map/ppermute | solution.py:507
  21.9 24.0 %collective-permute-start.1 = (bf16[2,1024,128]{2,1,0:T(8,128)(2,1)}, bf16[2,1024,128]{2,1,0:T(8,128)(2,1)}, u32[]{:S(2)}, u32[]{:S(2)}) collective-permute-start(bf16[2,1024,128]{2,1,0:T(8,128)(2,1)} %get-tuple-element.29), channel_id=1, source_target_pairs={{0,192},{64,0},{128,64},{192,128},{1,193},{65,1},{129,65},{193,129... | collective-permute-start | bytes 1572872 | tf_op jit(solution)/shard_map/ppermute | solution.py:507
  23.6 24.1 %collective-permute-start.2 = (bf16[2,1024,128]{2,1,0:T(8,128)(2,1)}, bf16[2,1024,128]{2,1,0:T(8,128)(2,1)}, u32[]{:S(2)}, u32[]{:S(2)}) collective-permute-start(bf16[2,1024,128]{2,1,0:T(8,128)(2,1)} %get-tuple-element.30), channel_id=1, source_target_pairs={{0,128},{64,192},{128,0},{192,64},{1,129},{65,193},{129,1},{193,65... | collective-permute-start | bytes 1572872 | tf_op jit(solution)/shard_map/ppermute | solution.py:507
  35.1 25.8 %all-to-all-start.1 = ((bf16[8,36,512]{2,1,0:T(8,128)(2,1)}), bf16[8,36,512]{2,1,0:T(8,128)(2,1)S(1)}, u32[]{:S(2)}, u32[]{:S(2)}) async-start(bf16[8,36,512]{2,1,0:T(8,128)(2,1)} %copy.53), calls=%async_computation.1 | async-start | bytes 655360 | tf_op jit(solution)/shard_map/all_to_all | solution.py:553
  38.6 65.8 %all-gather.5.cloned.1.call-start = ((), (), s32[]{:S(2)}) async-start(), calls=%async_computation.12 | async-start | bytes 2359296 | tf_op jit(solution)/shard_map/all_gather | solution.py:578
  38.7 1.0 copy-start.5
  43.7 0.8 copy-start.3
  47.7 1.0 copy-start.4
  60.9 29.1 %copy-start.9 = (s32[1,128,8]{1,2,0:T(8,128)S(1)}, s32[1,128,8]{1,2,0:T(8,128)}, u32[]{:S(2)}) copy-start(s32[1,128,8]{1,2,0:T(8,128)} %param.19) | copy-start | bytes 12292
  60.9 30.4 %copy-start.10 = (f32[1,128,8]{1,2,0:T(8,128)S(1)}, f32[1,128,8]{1,2,0:T(8,128)}, u32[]{:S(2)}) copy-start(f32[1,128,8]{1,2,0:T(8,128)} %param.20) | copy-start | bytes 12292
  86.4 17.9 %all-to-all-start.3 = ((bf16[8,128,256]{2,1,0:T(8,128)(2,1)}), bf16[8,128,256]{2,1,0:T(8,128)(2,1)S(1)}, u32[]{:S(2)}, u32[]{:S(2)}) async-start(bf16[8,128,256]{2,1,0:T(8,128)(2,1)} %combine.1), calls=%async_computation.3 | async-start | bytes 1048576 | tf_op jit(solution)/shard_map/all_to_all | solution.py:580
  89.9 80.7 %all-gather.7.cloned.1.call-start = ((), (), s32[]{:S(2)}) async-start(), calls=%async_computation.13 | async-start | bytes 3538944 | tf_op jit(solution)/shard_map/all_gather | solution.py:589
  93.0 16.4 %copy-start.6 = (s32[512,128]{0,1:T(8,128)S(1)}, s32[512,128]{0,1:T(8,128)}, u32[]{:S(2)}) copy-start(s32[512,128]{0,1:T(8,128)} %copy.49) | copy-start | bytes 786436
  104.4 1.6 copy-start.2
  106.0 3.5 %copy-start.7 = (bf16[512,128]{0,1:T(8,128)(2,1)S(1)}, bf16[512,128]{0,1:T(8,128)(2,1)}, u32[]{:S(2)}) copy-start(bf16[512,128]{0,1:T(8,128)(2,1)} %copy.51) | copy-start | bytes 393220
  106.5 5.0 %collective-permute-start.5 = (bf16[128,512]{1,0:T(8,128)(2,1)S(1)}, bf16[128,512]{1,0:T(8,128)(2,1)S(1)}, u32[]{:S(2)}, u32[]{:S(2)}) collective-permute-start(bf16[128,512]{1,0:T(8,128)(2,1)S(1)} %project.1.own_ref), channel_id=1, source_target_pairs={{0,192},{64,0},{128,64},{192,128},{1,193},{65,1},{129,65},{193,129... | collective-permute-start | bytes 393224 | tf_op jit(solution)/shard_map/ppermute | solution.py:507
  107.3 6.5 %collective-permute-start.4 = (bf16[128,512]{1,0:T(8,128)(2,1)S(1)}, bf16[128,512]{1,0:T(8,128)(2,1)S(1)}, u32[]{:S(2)}, u32[]{:S(2)}) collective-permute-start(bf16[128,512]{1,0:T(8,128)(2,1)S(1)} %project.1.own_ref), channel_id=1, source_target_pairs={{0,128},{64,192},{128,0},{192,64},{1,129},{65,193},{129,1},{193,65... | collective-permute-start | bytes 393224 | tf_op jit(solution)/shard_map/ppermute | solution.py:507
  109.2 6.2 %collective-permute-start.3 = (bf16[128,512]{1,0:T(8,128)(2,1)S(1)}, bf16[128,512]{1,0:T(8,128)(2,1)S(1)}, u32[]{:S(2)}, u32[]{:S(2)}) collective-permute-start(bf16[128,512]{1,0:T(8,128)(2,1)S(1)} %project.1.own_ref), channel_id=1, source_target_pairs={{0,64},{64,128},{128,192},{192,0},{1,65},{65,129},{129,193},{193,1... | collective-permute-start | bytes 393224 | tf_op jit(solution)/shard_map/ppermute | solution.py:507
  128.8 89.9 %reduce-scatter.2.cloned.1.call-start = ((), (), s32[]{:S(2)}) async-start(), calls=%async_computation.11 | async-start | bytes 2359296 | tf_op jit(solution)/shard_map/reduce_scatter | solution.py:598
  218.7 10.8 %all-to-all-start.8 = ((bf16[8,64,256]{2,1,0:T(8,128)(2,1)}), bf16[8,64,256]{2,1,0:T(8,128)(2,1)S(1)}, u32[]{:S(2)}, u32[]{:S(2)}) async-start(bf16[8,64,256]{2,1,0:T(8,128)(2,1)} %bitcast.63), calls=%async_computation.9 | async-start | bytes 524288 | tf_op jit(solution)/shard_map/all_to_all | solution.py:606
  223.5 1.6 copy-start.1
  229.7 7.1 %collective-permute-start.6 = (bf16[32,2304]{1,0:T(8,128)(2,1)S(1)}, bf16[32,2304]{1,0:T(8,128)(2,1)S(1)}, u32[]{:S(2)}, u32[]{:S(2)}) collective-permute-start(bf16[32,2304]{1,0:T(8,128)(2,1)S(1)} %get-tuple-element.45), channel_id=1, source_target_pairs={{0,64},{64,128},{128,192},{192,0},{1,65},{65,129},{129,193},{193,1... | collective-permute-start | bytes 442376 | tf_op jit(solution)/shard_map/ppermute | solution.py:507
  231.3 9.0 %collective-permute-start.7 = (bf16[32,2304]{1,0:T(8,128)(2,1)S(1)}, bf16[32,2304]{1,0:T(8,128)(2,1)S(1)}, u32[]{:S(2)}, u32[]{:S(2)}) collective-permute-start(bf16[32,2304]{1,0:T(8,128)(2,1)S(1)} %get-tuple-element.46), channel_id=1, source_target_pairs={{0,128},{64,192},{128,0},{192,64},{1,129},{65,193},{129,1},{193,65... | collective-permute-start | bytes 442376 | tf_op jit(solution)/shard_map/ppermute | solution.py:507
  234.0 6.4 %collective-permute-start.8 = (bf16[32,2304]{1,0:T(8,128)(2,1)S(1)}, bf16[32,2304]{1,0:T(8,128)(2,1)S(1)}, u32[]{:S(2)}, u32[]{:S(2)}) collective-permute-start(bf16[32,2304]{1,0:T(8,128)(2,1)S(1)} %get-tuple-element.47), channel_id=1, source_target_pairs={{0,192},{64,0},{128,64},{192,128},{1,193},{65,1},{129,65},{193,129... | collective-permute-start | bytes 442376 | tf_op jit(solution)/shard_map/ppermute | solution.py:507
Sparse Core Ops, SparseCore 0:
  61.8 26.4 all-gather.4
  128.9 41.6 all-gather.6
  180.1 38.5 reduce-scatter.1
